TPU v7x, 32 devices: a whole 2x2x4 slice. The times are simulated.
32 devices in a mesh: fsdp: 8 (over y, x, core), rep: 4 (over z).
Axes of the slice: x: 2, y: 2, z: 4, core: 2. Of those that a mesh axis runs over, the one named last changes fastest.
Arguments:
- tokens: bfloat16 [8192, 2048], P(('fsdp', 'rep')), may hold values from -6 to 6
- block_lengths: int32 [64], P(('fsdp', 'rep')), may hold values from 0 to 256, as said below
- w_query: bfloat16 [2048, 2048], P(('fsdp', 'rep')), may hold values from -0.125 to 0.125
- w_key: bfloat16 [2048, 2048], P(('fsdp', 'rep')), may hold values from -0.125 to 0.125
- w_value: bfloat16 [2048, 2048], P(('fsdp', 'rep')), may hold values from -0.125 to 0.125
- w_out: bfloat16 [2048, 2048], P(('fsdp', 'rep')), may hold values from -0.125 to 0.125
- w_gate: bfloat16 [2048, 8192], P(('fsdp', 'rep')), may hold values from -0.125 to 0.125
- w_up: bfloat16 [2048, 8192], P(('fsdp', 'rep')), may hold values from -0.125 to 0.125
- w_down: bfloat16 [8192, 2048], P(('fsdp', 'rep')), may hold values from -0.0625 to 0.0625
- query_gain: bfloat16 [2048], P(('fsdp', 'rep')), may hold values from 0.099609375 to 1.8984375
- key_gain: bfloat16 [2048], P(('fsdp', 'rep')), may hold values from 0.099609375 to 1.8984375
- attn_gain: bfloat16 [2048], P(('fsdp', 'rep')), may hold values from 0.099609375 to 1.8984375
- mlp_gain: bfloat16 [2048], P(('fsdp', 'rep')), may hold values from 0.099609375 to 1.8984375
- cotangent: bfloat16 [8192, 2048], P(('fsdp', 'rep')), may hold values from -6 to 6
Outputs:
- block_out: bfloat16 [8192, 2048], P(('fsdp', 'rep'))
- grad_tokens: bfloat16 [8192, 2048], P(('fsdp', 'rep'))
- grad_w_query: float32 [2048, 2048], P(('fsdp', 'rep'))
- grad_w_key: float32 [2048, 2048], P(('fsdp', 'rep'))
- grad_w_value: float32 [2048, 2048], P(('fsdp', 'rep'))
- grad_w_out: float32 [2048, 2048], P(('fsdp', 'rep'))
- grad_w_gate: float32 [2048, 8192], P(('fsdp', 'rep'))
- grad_w_up: float32 [2048, 8192], P(('fsdp', 'rep'))
- grad_w_down: float32 [8192, 2048], P(('fsdp', 'rep'))
- grad_query_gain: float32 [2048], P(('fsdp', 'rep'))
- grad_key_gain: float32 [2048], P(('fsdp', 'rep'))
- grad_attn_gain: float32 [2048], P(('fsdp', 'rep'))
- grad_mlp_gain: float32 [2048], P(('fsdp', 'rep'))
Inputs may be any that keep to these rules, and one draw needn't show every extreme that they name: `block_lengths`: entry b is the length of the sequence whose first token is the first row of block b, 0 where none starts there. A device's sequences lie in its own 2 blocks and never run into a block where another starts; every device holds one or more, and in every draw some device holds one of 256 tokens.
All inputs are finite; a program needn't handle non-finite values.
Results may differ from a plain program's by a relative error of at most 0.015.
Values may be sent and summed in bfloat16 or wider, within the bound.
No kernel may reach another device: no remote copies, remote signals or barrier semaphores. Data moves between devices by JAX's collectives and lax.ppermute only.
A program may use at most 768 MiB of HBM per device.

v0:
```python
import jax
import jax.numpy as jnp
from jax import lax
from jax.sharding import PartitionSpec as P

HEADS = 16
HEAD_DIM = 128
BLOCK = 128


epsilon = 1e-06
rope_base = 500000.0


def product(left, right):
    return jnp.dot(left, right, preferred_element_type=jnp.float32)


def product_tt(left, right):
    return lax.dot_general(
        left, right, (((1,), (1,)), ((), ())), preferred_element_type=jnp.float32
    )


def inner_rows(left, right):
    return lax.dot_general(
        left, right, (((0,), (0,)), ((), ())), preferred_element_type=jnp.float32
    )


def norm_forward(values, gain):
    inverse = lax.rsqrt(jnp.mean(values * values, axis=-1, keepdims=True) + epsilon)
    return (values * inverse * gain, inverse)


def norm_back(values, inverse, gain, incoming):
    normed = values * inverse
    scaled = incoming * gain
    gain_term = jnp.sum(incoming * normed, axis=0)
    back = inverse * (scaled - normed * jnp.mean(scaled * normed, axis=-1, keepdims=True))
    return (back, gain_term)


def rotate(values, position, sign):
    half = HEAD_DIM // 2
    freq = rope_base ** (-jnp.arange(half, dtype=jnp.float32) / half)
    angle = sign * position.astype(jnp.float32)[:, None] * freq[None, :]
    cosine = jnp.cos(angle)[:, None, :]
    sine = jnp.sin(angle)[:, None, :]
    shaped = values.reshape(values.shape[0], HEADS, HEAD_DIM)
    first = shaped[..., :half]
    second = shaped[..., half:]
    turned = jnp.concatenate(
        [first * cosine - second * sine, second * cosine + first * sine], axis=-1
    )
    return turned.reshape(values.shape)


def row_layout(lengths):
    nblock = lengths.shape[0]
    row_ids = jnp.arange(nblock * BLOCK, dtype=jnp.int32)
    begin = jnp.arange(nblock, dtype=jnp.int32) * BLOCK
    cover = (
        (lengths[None, :] > 0)
        & (row_ids[:, None] >= begin[None, :])
        & (row_ids[:, None] < begin[None, :] + lengths[None, :])
    )
    live = jnp.any(cover, axis=1)
    owner = jnp.sum(jnp.where(cover, begin[None, :], 0), axis=1)
    position = row_ids - owner
    same = (
        live[:, None]
        & live[None, :]
        & (owner[:, None] == owner[None, :])
        & (row_ids[None, :] <= row_ids[:, None])
    )
    allowed = same | (row_ids[:, None] == row_ids[None, :])
    return (live, position, allowed)


def local(
    tokens,
    block_lengths,
    w_query,
    w_key,
    w_value,
    w_out,
    w_gate,
    w_up,
    w_down,
    query_gain,
    key_gain,
    attn_gain,
    mlp_gain,
    cotangent,
):
    nrows = tokens.shape[0]
    width = tokens.shape[1]
    hidden_width = w_gate.shape[1]
    shard_rows = w_query.shape[0]
    ratio = w_down.shape[0] // shard_rows
    score_scale = HEAD_DIM ** (-0.5)
    live, position, allowed = row_layout(block_lengths)
    live_col = live.astype(jnp.float32)[:, None]
    tokens_wide = tokens.astype(jnp.float32)
    attn_stack = jnp.stack([w_query, w_key, w_value])
    mlp_stack = jnp.stack([w_gate, w_up])
    attn_whole, query_gain_full, key_gain_full = (
        lax.all_gather(attn_stack, ("fsdp", "rep"), axis=1, tiled=True),
        lax.all_gather(query_gain, ("fsdp", "rep"), axis=0, tiled=True),
        lax.all_gather(key_gain, ("fsdp", "rep"), axis=0, tiled=True),
    )
    query_raw = product(tokens, attn_whole[0])
    key_raw = product(tokens, attn_whole[1])
    value_raw = product(tokens, attn_whole[2])
    query_normed, query_inverse = norm_forward(query_raw, query_gain_full.astype(jnp.float32))
    key_normed, key_inverse = norm_forward(key_raw, key_gain_full.astype(jnp.float32))
    head_shape = (nrows, HEADS, HEAD_DIM)
    query_rot = rotate(query_normed, position, 1.0).astype(jnp.bfloat16).reshape(head_shape)
    key_rot = rotate(key_normed, position, 1.0).astype(jnp.bfloat16).reshape(head_shape)
    value_low = value_raw.astype(jnp.bfloat16).reshape(head_shape)

    def masked_scores():
        raw_scores = (
            jnp.einsum("qhd,khd->hqk", query_rot, key_rot, preferred_element_type=jnp.float32)
            * score_scale
        )
        return jnp.where(allowed[None], raw_scores, -1e30)

    scores = masked_scores()
    log_total = jax.nn.logsumexp(scores, axis=-1, keepdims=True)
    probs_low = jnp.exp(scores - log_total).astype(jnp.bfloat16)
    mixed = jnp.einsum("hqk,khd->qhd", probs_low, value_low, preferred_element_type=jnp.float32)
    mixed_low = mixed.reshape(nrows, width).astype(jnp.bfloat16)
    out_whole, attn_gain_full = (
        lax.all_gather(w_out, ("fsdp", "rep"), axis=0, tiled=True),
        lax.all_gather(attn_gain, ("fsdp", "rep"), axis=0, tiled=True),
    )
    attn_gain_wide = attn_gain_full.astype(jnp.float32)
    attn_proj = product(mixed_low, out_whole)
    attn_normed, attn_inverse = norm_forward(attn_proj, attn_gain_wide)
    hidden = tokens_wide + attn_normed
    hidden_low = hidden.astype(jnp.bfloat16)
    mlp_whole, mlp_gain_full = (
        lax.all_gather(mlp_stack, ("fsdp", "rep"), axis=1, tiled=True),
        lax.all_gather(mlp_gain, ("fsdp", "rep"), axis=0, tiled=True),
    )
    mlp_gain_wide = mlp_gain_full.astype(jnp.float32)
    gate = product(hidden_low, mlp_whole[0])
    upward = product(hidden_low, mlp_whole[1])
    sigmoid_gate = jax.nn.sigmoid(gate)
    activated = gate * sigmoid_gate
    inner_low = (activated * upward).astype(jnp.bfloat16)
    down_whole = lax.all_gather(w_down, ("fsdp", "rep"), axis=0, tiled=True)
    down = product(inner_low, down_whole)
    down_normed, down_inverse = norm_forward(down, mlp_gain_wide)
    block_out = (live_col * (hidden + down_normed)).astype(jnp.bfloat16)
    grad_out = live_col * cotangent.astype(jnp.float32)
    grad_down, term_mlp_gain = norm_back(down, down_inverse, mlp_gain_wide, grad_out)
    grad_down_low = grad_down.astype(jnp.bfloat16)
    grad_inner = product_tt(
        grad_down_low, lax.all_gather(w_down, ("fsdp", "rep"), axis=0, tiled=True)
    )
    grad_gate_low = (
        grad_inner * upward * sigmoid_gate * (1.0 + gate * (1.0 - sigmoid_gate))
    ).astype(jnp.bfloat16)
    grad_up_low = (grad_inner * activated).astype(jnp.bfloat16)
    piece = lax.all_gather(mlp_stack, ("fsdp", "rep"), axis=1, tiled=True)
    grad_from_mlp = product_tt(grad_gate_low, piece[0]) + product_tt(grad_up_low, piece[1])
    grad_hidden = grad_out + grad_from_mlp
    grad_proj, term_attn_gain = norm_back(attn_proj, attn_inverse, attn_gain_wide, grad_hidden)
    grad_proj_low = grad_proj.astype(jnp.bfloat16)
    grad_mixed = product_tt(
        grad_proj_low, lax.all_gather(w_out, ("fsdp", "rep"), axis=0, tiled=True)
    )
    grad_mixed_low = grad_mixed.astype(jnp.bfloat16).reshape(head_shape)
    probs = jnp.exp(masked_scores() - log_total)
    grad_probs = jnp.einsum(
        "qhd,khd->hqk", grad_mixed_low, value_low, preferred_element_type=jnp.float32
    )
    grad_scores_low = (
        probs * (grad_probs - jnp.sum(probs * grad_probs, axis=-1, keepdims=True))
    ).astype(jnp.bfloat16)
    grad_query_rot = (
        jnp.einsum("hqk,khd->qhd", grad_scores_low, key_rot, preferred_element_type=jnp.float32)
        * score_scale
    )
    grad_key_rot = (
        jnp.einsum("hqk,qhd->khd", grad_scores_low, query_rot, preferred_element_type=jnp.float32)
        * score_scale
    )
    grad_value_low = (
        jnp.einsum("hqk,qhd->khd", probs_low, grad_mixed_low, preferred_element_type=jnp.float32)
        .reshape(nrows, width)
        .astype(jnp.bfloat16)
    )
    grad_query_normed = rotate(grad_query_rot.reshape(nrows, width), position, -1.0)
    grad_key_normed = rotate(grad_key_rot.reshape(nrows, width), position, -1.0)
    grad_query, term_query_gain = norm_back(
        query_raw, query_inverse, query_gain_full.astype(jnp.float32), grad_query_normed
    )
    grad_key, term_key_gain = norm_back(
        key_raw, key_inverse, key_gain_full.astype(jnp.float32), grad_key_normed
    )
    grad_query_low = grad_query.astype(jnp.bfloat16)
    grad_key_low = grad_key.astype(jnp.bfloat16)
    piece = lax.all_gather(attn_stack, ("fsdp", "rep"), axis=1, tiled=True)
    grad_from_attn = (
        product_tt(grad_query_low, piece[0])
        + product_tt(grad_key_low, piece[1])
        + product_tt(grad_value_low, piece[2])
    )
    grad_tokens = (grad_hidden + grad_from_attn).astype(jnp.bfloat16)
    columns = hidden_low
    down_term = inner_rows(inner_low, grad_down_low).reshape(
        shard_rows * lax.axis_size(("fsdp", "rep")), ratio * width
    )
    mlp_grads = lax.psum_scatter(
        jnp.concatenate(
            [inner_rows(columns, grad_gate_low), inner_rows(columns, grad_up_low), down_term],
            axis=1,
        ),
        ("fsdp", "rep"),
        scatter_dimension=0,
        tiled=True,
    )
    columns = tokens
    attn_grads = lax.psum_scatter(
        jnp.concatenate(
            [
                inner_rows(columns, grad_query_low),
                inner_rows(columns, grad_key_low),
                inner_rows(columns, grad_value_low),
                inner_rows(mixed_low, grad_proj_low),
            ],
            axis=1,
        ),
        ("fsdp", "rep"),
        scatter_dimension=0,
        tiled=True,
    )
    gain_terms = jnp.stack([term_query_gain, term_key_gain, term_attn_gain, term_mlp_gain])
    gain_grads = lax.psum_scatter(gain_terms, ("fsdp", "rep"), scatter_dimension=1, tiled=True)
    return (
        block_out,
        grad_tokens,
        attn_grads[:, :width],
        attn_grads[:, width : 2 * width],
        attn_grads[:, 2 * width : 3 * width],
        attn_grads[:, 3 * width :],
        mlp_grads[:, :hidden_width],
        mlp_grads[:, hidden_width : 2 * hidden_width],
        mlp_grads[:, 2 * hidden_width :].reshape(w_down.shape),
        gain_grads[0],
        gain_grads[1],
        gain_grads[2],
        gain_grads[3],
    )


def solution(mesh):
    placed = (
        P(("fsdp", "rep"), None),
        P(("fsdp", "rep")),
        P(("fsdp", "rep"), None),
        P(("fsdp", "rep"), None),
        P(("fsdp", "rep"), None),
        P(("fsdp", "rep"), None),
        P(("fsdp", "rep"), None),
        P(("fsdp", "rep"), None),
        P(("fsdp", "rep"), None),
        P(("fsdp", "rep")),
        P(("fsdp", "rep")),
        P(("fsdp", "rep")),
        P(("fsdp", "rep")),
        P(("fsdp", "rep"), None),
    )
    return jax.shard_map(
        local,
        mesh=mesh,
        in_specs=placed,
        out_specs=(
            P(("fsdp", "rep"), None),
            P(("fsdp", "rep"), None),
            P(("fsdp", "rep"), None),
            P(("fsdp", "rep"), None),
            P(("fsdp", "rep"), None),
            P(("fsdp", "rep"), None),
            P(("fsdp", "rep"), None),
            P(("fsdp", "rep"), None),
            P(("fsdp", "rep"), None),
            P(("fsdp", "rep")),
            P(("fsdp", "rep")),
            P(("fsdp", "rep")),
            P(("fsdp", "rep")),
        ),
        check_vma=False,
    )
```

profile of v0, /device:TPU:0, one launch (start us, length us, event | category | flops | bytes accessed | tf_op | source)
XLA Modules:
  0.0 4079.2 jit_solution(8642194011372673629)
XLA Ops:
  13.7 43.6 %all-reduce.4 = (bf16[2048]{0:T(1024)(128)(2,1)S(1)}, bf16[2048]{0:T(1024)(128)(2,1)S(1)}, bf16[2048]{0:T(1024)(128)(2,1)S(1)}, bf16[2048]{0:T(1024)(128)(2,1)S(1)}) all-reduce(bf16[2048]{0:T(1024)(128)(2,1)S(1)} %dynamic-update-slice.1, bf16[2048]{0:T(1024)(128)(2,1)S(1)} %dynamic-update-slice, ...), channel_id=1, replica_groups=mesh['fsdp'=8,'rep'=4] {'fsdp','rep'}, use_global_device_ids=true, to_apply=%add.1 | all-reduce | flops 8192 | bytes 32768
  59.1 111.5 %all-gather.5.cloned.1.call-done = bf16[3,2048,2048]{2,1,0:T(8,128)(2,1)} async-done(((bf16[3,64,2048]{2,1,0:T(8,128)(2,1)}), bf16[3,2048,2048]{2,1,0:T(8,128)(2,1)}) %all-gather.5.cloned.1.call-update) | async-done | bytes 25165840 | tf_op jit(solution)/shard_map/all_gather | solution.py:109
  170.5 6.1 multiply_reduce_fusion.7
  184.4 6.1 multiply_reduce_fusion.8
  206.8 6.2 fusion.18
  216.1 33.0 all-gather.7.cloned.1.call-done
  249.1 6.1 multiply_reduce_fusion.6
  256.6 350.3 %all-gather.9.cloned.1.call-done = bf16[2,2048,8192]{2,1,0:T(8,128)(2,1)} async-done(((bf16[2,64,8192]{2,1,0:T(8,128)(2,1)}), bf16[2,2048,8192]{2,1,0:T(8,128)(2,1)}) %all-gather.9.cloned.1.call-update) | async-done | bytes 67108880 | tf_op jit(solution)/shard_map/all_gather | solution.py:145
  606.9 18.4 fusion.1
  625.3 22.4 multiply_convert_fusion.2
  647.7 154.9 %all-gather.11.cloned.1.call-done = bf16[8192,2048]{1,0:T(8,128)(2,1)} async-done(((bf16[256,2048]{1,0:T(8,128)(2,1)}), bf16[8192,2048]{1,0:T(8,128)(2,1)}) %all-gather.11.cloned.1.call-update) | async-done | bytes 33554448 | tf_op jit(solution)/shard_map/all_gather | solution.py:154
  802.7 16.4 multiply_reduce_fusion.5
  821.7 23.2 multiply_convert_fusion
  844.9 17.4 fusion
  862.2 16.5 multiply_reduce_fusion.2
  881.0 6.7 convolution_convert_fusion
  900.0 8.2 fusion.53
  916.6 9.4 convolution_bitcast_fusion
  926.0 8.2 convolution_bitcast_fusion.1
  934.2 8.1 convolution_bitcast_fusion.2
  942.3 40.1 pad_maximum_fusion.1
  982.4 61.2 %copy.110 = f32[2048,8192]{1,0:T(8,128)} copy(f32[2048,8192]{0,1:T(8,128)} %pad_maximum_fusion.1) | data formatting | bytes 134217728
  1045.5 26.4 fusion.46
  1071.9 79.5 %reshape.339 = f32[2048,8192]{1,0:T(8,128)} reshape(f32[8192,2048]{1,0:T(8,128)} %fusion.46) | data formatting | bytes 134217728 | tf_op jit(solution)/shard_map/reshape | solution.py:215
  1151.4 25.6 fusion.55
  1177.0 25.6 fusion.54
  1202.6 132.0 %pad_maximum_fusion = f32[2048,24576]{1,0:T(8,128)} fusion(f32[2048,8192]{1,0:T(8,128)} %reshape.339, f32[2048,8192]{1,0:T(8,128)} %fusion.55, f32[2048,8192]{1,0:T(8,128)} %fusion.54), kind=kLoop, calls=%fused_computation | loop fusion | flops 100663296 | bytes 402653184 | tf_op jit(solution)/shard_map/concatenate | solution.py:219
  1335.9 5.9 fusion.7
  1341.8 6.0 fusion.12
  1347.9 6.9 fusion.17
  1358.1 1101.2 %reduce-scatter.10.cloned.1.call-done = f32[64,8192]{1,0:T(8,128)} async-done(((f32[2048,8192]{1,0:T(8,128)}), f32[64,8192]{1,0:T(8,128)}) %reduce-scatter.10.cloned.1.call-update) | async-done | bytes 2097168
  2462.2 1603.0 %reduce-scatter.8.cloned.1.call-done = f32[64,24576]{1,0:T(8,128)} async-done(((f32[2048,24576]{1,0:T(8,128)}), f32[64,24576]{1,0:T(8,128)}) %reduce-scatter.8.cloned.1.call-update) | async-done | bytes 6291472 | tf_op jit(solution)/shard_map/reduce_scatter | solution.py:218
  (216 shorter events, 77.8 us)
Async XLA Ops:
  7.2 3.1 copy-start.34
  7.2 3.1 copy-start.35
  7.2 163.3 %all-gather.5.cloned.1.call-start = ((), (), s32[]{:S(2)}) async-start(), calls=%async_computation.3 | async-start | bytes 25952256 | tf_op jit(solution)/shard_map/all_gather | solution.py:109
  9.5 239.6 %all-gather.7.cloned.1.call-start = ((), (), s32[]{:S(2)}) async-start(), calls=%async_computation.4 | async-start | bytes 8650752 | tf_op jit(solution)/shard_map/all_gather | solution.py:136
  10.2 596.7 %all-gather.9.cloned.1.call-start = ((), (), s32[]{:S(2)}) async-start(), calls=%async_computation.5 | async-start | bytes 69206016 | tf_op jit(solution)/shard_map/all_gather | solution.py:145
  11.9 158.7 %copy-start.2 = (bf16[256,2048]{1,0:T(8,128)(2,1)S(1)}, bf16[256,2048]{1,0:T(8,128)(2,1)}, u32[]{:S(2)}) copy-start(bf16[256,2048]{1,0:T(8,128)(2,1)} %param.14) | copy-start | bytes 3145732
  11.9 790.8 %all-gather.11.cloned.1.call-start = ((), (), s32[]{:S(2)}) async-start(), calls=%async_computation.6 | async-start | bytes 34603008 | tf_op jit(solution)/shard_map/all_gather | solution.py:154
  12.5 1342.3 %reduce-scatter.12.cloned.1.call-start = ((), (), s32[]{:S(2)}) async-start(), calls=%async_computation.9 | async-start | bytes 1081344
  57.4 119.3 %copy-start.42 = (f32[2048]{0:T(1024)}, f32[2048]{0:T(1024)S(1)}, u32[]{:S(2)}) copy-start(f32[2048]{0:T(1024)S(1)} %convert_element_type.115) | copy-start | bytes 24580
  57.4 133.1 %copy-start.40 = (f32[2048]{0:T(1024)}, f32[2048]{0:T(1024)S(1)}, u32[]{:S(2)}) copy-start(f32[2048]{0:T(1024)S(1)} %convert_element_type.113) | copy-start | bytes 24580
  57.4 764.2 %copy-start.44 = (f32[2048]{0:T(1024)}, f32[2048]{0:T(1024)S(1)}, u32[]{:S(2)}) copy-start(f32[2048]{0:T(1024)S(1)} %convert_element_type.123) | copy-start | bytes 24580
  59.1 153.9 %copy-start.29 = (pred[256,256]{0,1:T(8,128)(4,1)}, pred[256,256]{0,1:T(8,128)(4,1)S(1)}, u32[]{:S(2)}) copy-start(pred[256,256]{0,1:T(8,128)(4,1)S(1)} %fusion.33) | copy-start | bytes 196612
  205.5 7.4 copy-start
  206.7 6.2 copy-start.38
  802.7 16.4 copy-start.19
  821.6 23.2 copy-start.52
  889.5 4.4 copy-start.1
  889.5 4.4 copy-start.33
  900.0 8.2 copy-start.36
  900.0 8.2 copy-start.37
  911.5 14.5 copy-start.23
  914.7 19.5 copy-start.25
  916.1 1543.2 %reduce-scatter.10.cloned.1.call-start = ((), (), s32[]{:S(2)}) async-start(), calls=%async_computation.8 | async-start | bytes 69206016
  926.0 16.3 slice-start
  926.0 16.3 slice-start.1
  934.2 8.1 slice-start.2
  934.2 8.1 slice-start.3
  1043.7 3021.5 %reduce-scatter.8.cloned.1.call-start = ((), (), s32[]{:S(2)}) async-start(), calls=%async_computation.7 | async-start | bytes 207618048 | tf_op jit(solution)/shard_map/reduce_scatter | solution.py:218
  1071.9 79.5 %copy-start.7 = (bf16[256,2048]{1,0:T(8,128)(2,1)S(1)}, bf16[256,2048]{1,0:T(8,128)(2,1)}, u32[]{:S(2)}) copy-start(bf16[256,2048]{1,0:T(8,128)(2,1)} %fusion.31) | copy-start | bytes 3145732
  1335.8 5.9 copy-start.24
  1341.8 6.0 copy-start.28
  1341.8 6.0 copy-start.31
  (38 other events, 59.2 us)
Sparse Core Ops, SparseCore 0:
  11.6 158.8 all-gather.4
  173.5 75.5 all-gather.6
  252.1 354.7 all-gather.8
  609.7 192.9 all-gather.10
  916.2 133.4 reduce-scatter.11
  1052.1 1407.1 reduce-scatter.9
  2466.9 1598.2 reduce-scatter.7
where the time goes:
time: 4090 us; the launch traced here: 4080 us
  waiting for transfers between devices  3360 us (82%)
  matrix products  288 us (7%)
  other arithmetic  192 us (5%)
  local copies, waits for them, and re-layouts  185 us (5%)
  blocking collectives  43.6 us (1%)
    reduce_scatter x1, waiting for transfers between devices, local(): lax.psum_scatter(jnp.concatenate([inner_rows(columns, grad_gate_low), inn...  1600 us
    unnamed x9, waiting for transfers between devices  1100 us
    all_gather x1, waiting for transfers between devices, local(): lax.all_gather(mlp_stack, ('fsdp', 'rep'), axis=1, tiled=True)  350 us
    all_gather x1, waiting for transfers between devices, local(): down_whole = lax.all_gather(w_down, ('fsdp', 'rep'), axis=0, tiled=True)  155 us
    concatenate x1, other arithmetic, local(): jnp.concatenate([inner_rows(columns, grad_gate_low), inner_rows(columns,...  132 us
    all_gather x1, waiting for transfers between devices, local(): lax.all_gather(attn_stack, ('fsdp', 'rep'), axis=1, tiled=True)  111 us
    dot_general x7, matrix products, inner_rows(): lax.dot_general(left, right, (((0,), (0,)), ((), ())), preferred_element_...  111 us
    unnamed x144, local copies, waits for them, and re-layouts  89.4 us
  transfers between devices with their start and end apart: 7, of which 6 were waited for; matrix products, arithmetic and copies ran while one was open for 13% of the time, Pallas kernels for 0%

commit v1 on v0

v1 whole, which is shorter than its diff:
```python
import jax
import jax.numpy as jnp
from jax import lax
from jax.sharding import Mesh, PartitionSpec as P

HEAD_DIM = 128
BLOCK = 128

epsilon = 1e-06
rope_base = 500000.0
f32 = jnp.float32
bf16 = jnp.bfloat16


def product(left, right):
    return jnp.dot(left, right, preferred_element_type=f32)


def product_tt(left, right):
    return lax.dot_general(left, right, (((1,), (1,)), ((), ())), preferred_element_type=f32)


def inner_rows(left, right):
    return lax.dot_general(left, right, (((0,), (0,)), ((), ())), preferred_element_type=f32)


def norm_forward(values, gain):
    inverse = lax.rsqrt(jnp.mean(values * values, axis=-1, keepdims=True) + epsilon)
    return (values * inverse * gain, inverse)


def norm_back(values, inverse, gain, incoming):
    normed = values * inverse
    scaled = incoming * gain
    gain_term = jnp.sum(incoming * normed, axis=0)
    back = inverse * (scaled - normed * jnp.mean(scaled * normed, axis=-1, keepdims=True))
    return (back, gain_term)


def angles(position):
    half = HEAD_DIM // 2
    freq = rope_base ** (-jnp.arange(half, dtype=f32) / half)
    angle = position.astype(f32)[..., None] * freq
    return jnp.cos(angle)[..., None, :], jnp.sin(angle)[..., None, :]


def rotate(values, cosine, sine):
    half = HEAD_DIM // 2
    first = values[..., :half]
    second = values[..., half:]
    return jnp.concatenate(
        [first * cosine - second * sine, second * cosine + first * sine], axis=-1
    )


def row_layout(lengths):
    nblock = lengths.shape[0]
    row_ids = jnp.arange(nblock * BLOCK, dtype=jnp.int32)
    begin = jnp.arange(nblock, dtype=jnp.int32) * BLOCK
    cover = (
        (lengths[None, :] > 0)
        & (row_ids[:, None] >= begin[None, :])
        & (row_ids[:, None] < begin[None, :] + lengths[None, :])
    )
    live = jnp.any(cover, axis=1)
    owner = jnp.sum(jnp.where(cover, begin[None, :], 0), axis=1)
    position = row_ids - owner
    same = (
        live[:, None]
        & live[None, :]
        & (owner[:, None] == owner[None, :])
        & (row_ids[None, :] <= row_ids[:, None])
    )
    allowed = same | (row_ids[:, None] == row_ids[None, :])
    return (live, position, allowed)


def swap(value, axis):
    return lax.ppermute(value, axis, ((0, 1), (1, 0)))


def pick(value, index, axis):
    return lax.dynamic_index_in_dim(value, index, axis, keepdims=False)


class Cube:
    every = ("y", "x", "c", "zh", "zl")
    team = ("zl", "x", "c")

    def __init__(self):
        self.y = lax.axis_index("y")
        self.zh = lax.axis_index("zh")
        self.size = 8
        self.index = lax.axis_index(self.team)

    def gather_lengths(self, lengths):
        for axis in ("x", "zl", "c"):
            lengths = jnp.stack([lengths, swap(lengths, axis)])
        return lengths.reshape(8, -1)

    def gather_rows(self, rows):
        half = rows.shape[0] // 2
        top, low = rows[:half], rows[half:]
        top_x, low_z = swap(top, "x"), swap(low, "zl")
        top_z, low_x = swap(top, "zl"), swap(low, "x")
        top_zx, low_zx = swap(top_x, "zl"), swap(low_z, "x")
        near = swap(rows, "c")
        middle = swap(jnp.concatenate([top_x, low_z]), "c")
        far = swap(jnp.concatenate([low_x, top_z, top_zx, low_zx]), "c")
        return jnp.concatenate(
            [
                rows, top_x, low_x, top_z, low_z, top_zx, low_zx,
                near, middle[:half], far[:half], far[half : 2 * half], middle[half:], far[2 * half :],
            ]
        )

    def scatter_rows(self, make):
        away = make(1).astype(bf16)
        mine = make(0)
        total = mine.astype(f32) + swap(away, "c").astype(f32)
        width = total.shape[1]
        total = total.reshape(2, 2, 2, -1, width)
        top, low = total[:, :, 0], total[:, :, 1]
        top = top[0] + swap(top[1].astype(bf16), "zl").astype(f32)
        low = low[:, 0] + swap(low[:, 1].astype(bf16), "x").astype(f32)
        top = top[0] + swap(top[1].astype(bf16), "x").astype(f32)
        low = low[0] + swap(low[1].astype(bf16), "zl").astype(f32)
        return jnp.concatenate([top, low])

    def split_rows(self, rows):
        half = rows.shape[0] // 2
        return rows[:half], rows[half:]

    def sum_rows(self, rows):
        shape = rows.shape
        rows = rows.reshape((2, 2, 2, -1) + shape[1:])
        for dim, axis in enumerate(("c", "zl", "x")):
            rows = rows + jnp.flip(swap(rows, axis), dim)
        return rows.reshape(shape)

    def order(self, mine, other, index, axis):
        first = index == 0
        return jnp.stack([jnp.where(first, mine, other), jnp.where(first, other, mine)], axis)

    def gather_group(self, block, axis_zh, axis_y):
        zh_block = swap(block, "zh")
        y_block, both_block = swap(block, "y"), swap(zh_block, "y")
        mine = self.order(block, zh_block, self.zh, axis_zh)
        other = self.order(y_block, both_block, self.zh, axis_zh)
        return self.order(mine, other, self.y, axis_y)

    def scatter_group(self, terms, axis_y, axis_zh):
        away = pick(terms, 1 - self.y, axis_y)
        mine = pick(terms, self.y, axis_y)
        total = mine.astype(f32) + swap(away, "y").astype(f32)
        away = pick(total, 1 - self.zh, axis_zh).astype(bf16)
        mine = pick(total, self.zh, axis_zh)
        return mine + swap(away, "zh").astype(f32)

    def team_columns(self, weight):
        rows = weight.shape[0]
        return weight.reshape(rows, 8, -1).transpose(1, 0, 2)

    def team_hidden(self, weight):
        rows = weight.shape[0]
        parts = weight.reshape(rows, 2, 2, 2, 2, 2, -1)
        return parts.transpose(5, 2, 3, 0, 4, 1, 6).reshape(8, rows, -1)

    def whole_columns(self, parts):
        return parts.transpose(1, 0, 2).reshape(parts.shape[1], -1)

    def whole_hidden(self, parts):
        rows = parts.shape[1]
        parts = parts.reshape(2, 2, 2, rows, 2, 2, -1)
        return parts.transpose(3, 5, 1, 2, 4, 0, 6).reshape(rows, -1)

    def gather_columns(self, parts):
        rows, width = parts.shape[1:]
        block = lax.all_to_all(parts, self.team, 0, 0)
        block = block.reshape(2, 2, 2, rows, width).transpose(1, 2, 0, 3, 4)
        return self.gather_group(block, 2, 0).reshape(-1, width)

    def scatter_columns(self, terms):
        width = terms.shape[1]
        terms = terms.reshape(2, 2, 2, 2, 2, -1, width)
        block = self.scatter_group(terms, 0, 2).astype(bf16)
        block = block.transpose(2, 0, 1, 3, 4).reshape(8, -1, width)
        return lax.all_to_all(block, self.team, 0, 0)

    def gather_down(self, weight):
        return self.gather_group(weight, 0, 1).reshape(-1, weight.shape[1])

    def scatter_down(self, terms):
        width = terms.shape[1]
        return self.scatter_group(terms.reshape(2, 2, -1, width), 1, 0)

    def turn(self, value):
        return lax.ppermute(value, ("y", "zl"), ((0, 0), (1, 2), (2, 1), (3, 3)))

    def gather_out(self, weight):
        return self.gather_down(self.turn(weight))

    def scatter_out(self, terms):
        return self.turn(self.scatter_down(terms).astype(bf16)).astype(f32)


class Plain:
    def __init__(self, team, group):
        self.team, self.group = team, group
        self.every = (team, group)
        self.size = lax.axis_size(team)
        self.groups = lax.axis_size(group)
        self.index = lax.axis_index(team)

    def gather_lengths(self, lengths):
        return lax.all_gather(lengths, self.team)

    def gather_rows(self, rows):
        return lax.all_gather(rows, self.team, axis=0, tiled=True)

    def scatter_rows(self, make):
        terms = jnp.concatenate([make(0), make(1)]).astype(bf16)
        return lax.psum_scatter(terms, self.team, scatter_dimension=0, tiled=True).astype(f32)

    def split_rows(self, rows):
        half = rows.shape[0] // 2
        return rows[:half], rows[half:]

    def sum_rows(self, rows):
        return lax.psum(rows, self.team)

    def team_columns(self, weight):
        rows = weight.shape[0]
        return weight.reshape(rows, self.size, -1).transpose(1, 0, 2)

    team_hidden = team_columns

    def whole_columns(self, parts):
        return parts.transpose(1, 0, 2).reshape(parts.shape[1], -1)

    whole_hidden = whole_columns

    def gather_columns(self, parts):
        width = parts.shape[2]
        block = lax.all_to_all(parts, self.team, 0, 0)
        return lax.all_gather(block, self.group, axis=1, tiled=True).reshape(-1, width)

    def scatter_columns(self, terms):
        width = terms.shape[1]
        terms = terms.reshape(self.size, -1, width)
        block = lax.psum_scatter(terms, self.group, scatter_dimension=1, tiled=True)
        return lax.all_to_all(block, self.team, 0, 0)

    def gather_down(self, weight):
        return lax.all_gather(weight, self.group, axis=0, tiled=True)

    def scatter_down(self, terms):
        return lax.psum_scatter(terms, self.group, scatter_dimension=0, tiled=True).astype(f32)

    gather_out = gather_down
    scatter_out = scatter_down


def local(
    make_plan,
    tokens,
    block_lengths,
    w_query,
    w_key,
    w_value,
    w_out,
    w_gate,
    w_up,
    w_down,
    query_gain,
    key_gain,
    attn_gain,
    mlp_gain,
    cotangent,
):
    plan = make_plan()
    nrows, width = tokens.shape
    size = plan.size
    columns = width // size
    heads = columns // HEAD_DIM
    score_scale = HEAD_DIM ** (-0.5)

    live = row_layout(block_lengths)[0]
    live_col = live.astype(f32)[:, None]
    lengths = plan.gather_lengths(block_lengths)
    _, position, allowed = jax.vmap(row_layout)(lengths)
    cosine, sine = angles(position)
    gains = lax.all_gather(
        jnp.stack([query_gain, key_gain, attn_gain, mlp_gain]), plan.every, axis=1, tiled=True
    ).astype(f32)
    query_gain_part = lax.dynamic_slice_in_dim(gains[0], plan.index * columns, columns)
    key_gain_part = lax.dynamic_slice_in_dim(gains[1], plan.index * columns, columns)
    attn_gain_wide, mlp_gain_wide = gains[2], gains[3]

    attn_parts = jnp.concatenate([plan.team_columns(w) for w in (w_query, w_key, w_value)], axis=2)
    attn_whole = plan.gather_columns(attn_parts)
    out_whole = plan.gather_out(w_out)
    mlp_parts = jnp.concatenate([plan.team_hidden(w) for w in (w_gate, w_up)], axis=2)
    mlp_whole = plan.gather_columns(mlp_parts)
    down_whole = plan.gather_down(w_down)
    hidden_columns = mlp_whole.shape[1] // 2

    team_tokens = plan.gather_rows(tokens)
    raw = product(team_tokens, attn_whole)
    query_raw, key_raw = raw[:, :columns], raw[:, columns : 2 * columns]
    value_low = raw[:, 2 * columns :].astype(bf16)
    squares = jnp.stack(
        [jnp.sum(query_raw * query_raw, axis=-1), jnp.sum(key_raw * key_raw, axis=-1)], axis=-1
    )
    inverse = lax.rsqrt(plan.sum_rows(squares) / width + epsilon)
    query_inverse, key_inverse = inverse[:, :1], inverse[:, 1:]
    head_shape = (size, nrows, heads, HEAD_DIM)
    query_normed = query_raw * query_inverse
    key_normed = key_raw * key_inverse
    query_rot = rotate((query_normed * query_gain_part).reshape(head_shape), cosine, sine)
    key_rot = rotate((key_normed * key_gain_part).reshape(head_shape), cosine, sine)
    query_rot, key_rot = query_rot.astype(bf16), key_rot.astype(bf16)
    value_low = value_low.reshape(head_shape)

    def dots(spec, left, right):
        return jnp.einsum(spec, left, right, preferred_element_type=f32)

    scores = dots("bqhd,bkhd->bhqk", query_rot, key_rot) * score_scale
    scores = jnp.where(allowed[:, None], scores, -1e30)
    probs = jax.nn.softmax(scores, axis=-1)
    probs_low = probs.astype(bf16)
    mixed = dots("bhqk,bkhd->bqhd", probs_low, value_low)
    mixed_low = mixed.reshape(size * nrows, columns).astype(bf16)
    mixed_parts = plan.split_rows(mixed_low)
    attn_proj = plan.scatter_rows(lambda part: product(mixed_parts[part], out_whole))
    attn_normed, attn_inverse = norm_forward(attn_proj, attn_gain_wide)
    hidden = tokens.astype(f32) + attn_normed

    team_hidden = plan.gather_rows(hidden.astype(bf16))
    both = product(team_hidden, mlp_whole)
    gate, upward = both[:, :hidden_columns], both[:, hidden_columns:]
    sigmoid_gate = jax.nn.sigmoid(gate)
    activated = gate * sigmoid_gate
    inner_low = (activated * upward).astype(bf16)
    inner_parts = plan.split_rows(inner_low)
    down = plan.scatter_rows(lambda part: product(inner_parts[part], down_whole))
    down_normed, down_inverse = norm_forward(down, mlp_gain_wide)
    block_out = (live_col * (hidden + down_normed)).astype(bf16)

    grad_out = live_col * cotangent.astype(f32)
    grad_down, term_mlp_gain = norm_back(down, down_inverse, mlp_gain_wide, grad_out)
    team_grad_down = plan.gather_rows(grad_down.astype(bf16))
    grad_inner = product_tt(team_grad_down, down_whole)
    grad_gate = grad_inner * upward * sigmoid_gate * (1.0 + gate * (1.0 - sigmoid_gate))
    grad_up = grad_inner * activated
    grad_both = jnp.concatenate([grad_gate.astype(bf16), grad_up.astype(bf16)], axis=1)
    both_parts = plan.split_rows(grad_both)
    grad_hidden = grad_out + plan.scatter_rows(
        lambda part: product_tt(both_parts[part], mlp_whole)
    )
    grad_w_down = plan.scatter_down(inner_rows(inner_low, team_grad_down).astype(bf16))
    grad_w_mlp = plan.scatter_columns(inner_rows(team_hidden, grad_both).astype(bf16))
    grad_w_gate = plan.whole_hidden(grad_w_mlp[..., :hidden_columns]).astype(f32)
    grad_w_up = plan.whole_hidden(grad_w_mlp[..., hidden_columns:]).astype(f32)

    grad_proj, term_attn_gain = norm_back(attn_proj, attn_inverse, attn_gain_wide, grad_hidden)
    team_grad_proj = plan.gather_rows(grad_proj.astype(bf16))
    grad_mixed = product_tt(team_grad_proj, out_whole).astype(bf16).reshape(head_shape)
    grad_w_out = plan.scatter_out(inner_rows(mixed_low, team_grad_proj).astype(bf16))
    grad_probs = dots("bqhd,bkhd->bhqk", grad_mixed, value_low)
    grad_scores = probs * (grad_probs - jnp.sum(probs * grad_probs, axis=-1, keepdims=True))
    grad_scores = grad_scores.astype(bf16)
    grad_query_rot = dots("bhqk,bkhd->bqhd", grad_scores, key_rot) * score_scale
    grad_key_rot = dots("bhqk,bqhd->bkhd", grad_scores, query_rot) * score_scale
    grad_value = dots("bhqk,bqhd->bkhd", probs_low, grad_mixed).astype(bf16)
    flat = (size * nrows, columns)
    grad_query_turned = rotate(grad_query_rot, cosine, -sine).reshape(flat)
    grad_key_turned = rotate(grad_key_rot, cosine, -sine).reshape(flat)
    term_query_gain = jnp.sum(grad_query_turned * query_normed, axis=0)
    term_key_gain = jnp.sum(grad_key_turned * key_normed, axis=0)
    query_scaled = grad_query_turned * query_gain_part
    key_scaled = grad_key_turned * key_gain_part
    means = jnp.stack(
        [jnp.sum(query_scaled * query_normed, axis=-1), jnp.sum(key_scaled * key_normed, axis=-1)],
        axis=-1,
    )
    means = plan.sum_rows(means) / width
    grad_query = query_inverse * (query_scaled - query_normed * means[:, :1])
    grad_key = key_inverse * (key_scaled - key_normed * means[:, 1:])
    grad_raw = jnp.concatenate(
        [grad_query.astype(bf16), grad_key.astype(bf16), grad_value.reshape(flat)], axis=1
    )
    raw_parts = plan.split_rows(grad_raw)
    grad_w_attn = plan.scatter_columns(inner_rows(team_tokens, grad_raw).astype(bf16))
    grad_tokens = grad_hidden + plan.scatter_rows(
        lambda part: product_tt(raw_parts[part], attn_whole)
    )
    grad_w_query, grad_w_key, grad_w_value = (
        plan.whole_columns(grad_w_attn[..., k * columns : (k + 1) * columns]).astype(f32)
        for k in range(3)
    )

    blank = jnp.zeros((width,), f32)
    place = plan.index * columns
    terms = jnp.stack(
        [
            lax.dynamic_update_slice_in_dim(blank, term_query_gain, place, 0),
            lax.dynamic_update_slice_in_dim(blank, term_key_gain, place, 0),
            term_attn_gain,
            term_mlp_gain,
        ]
    )
    gain_grads = lax.psum_scatter(terms, plan.every, scatter_dimension=1, tiled=True)
    return (
        block_out,
        grad_tokens.astype(bf16),
        grad_w_query,
        grad_w_key,
        grad_w_value,
        grad_w_out,
        grad_w_gate,
        grad_w_up,
        grad_w_down,
        gain_grads[0],
        gain_grads[1],
        gain_grads[2],
        gain_grads[3],
    )


def solution(mesh):
    if tuple(mesh.shape.values()) == (8, 4):
        mesh = Mesh(mesh.devices.reshape(2, 2, 2, 2, 2), Cube.every)
        every, make_plan = Cube.every, Cube
    else:
        every = tuple(mesh.axis_names)

        def make_plan():
            return Plain(*every)

    def step(*arrays):
        return local(make_plan, *arrays)

    rows, line = P(every, None), P(every)
    return jax.shard_map(
        step,
        mesh=mesh,
        in_specs=(rows, line) + (rows,) * 7 + (line,) * 4 + (rows,),
        out_specs=(rows,) * 9 + (line,) * 4,
        check_vma=False,
    )
```

time: 4090 us -> 1310 us (0.32)
  waiting for transfers between devices: 3360 us -> 610 us
  matrix products: 288 us -> 180 us
  starting transfers between devices: 0.86 us -> 90.3 us
  other arithmetic: 192 us -> 123 us
    reduce_scatter x1 -> x0, waiting for transfers between devices: 1600 us -> none  [local(): lax.psum_scatter(jnp.concatenate([inner_rows(columns, grad_gate_low), inn...]
    unnamed x9 -> x2, waiting for transfers between devices: 1100 us -> 108 us
    all_gather x4 -> x0, waiting for transfers between devices: 650 us -> none  [the longest x1 350 us: local(): lax.all_gather(mlp_stack, ('fsdp', 'rep'), axis=1, tiled=True)]
    ppermute x0 -> x87, waiting for transfers between devices: none -> 502 us  [the longest x85 502 us: swap(): return lax.ppermute(value, axis, ((0, 1), (1, 0)))]
    concatenate x2 -> x11, other arithmetic: 172 us -> 12.4 us  [the longest x4 6.69 us: gather_rows(): far = swap(jnp.concatenate([low_x, top_z, top_zx, low_zx]), 'c')]
    all_gather x0 -> x1, blocking collectives: none -> 81.3 us  [local(): lax.all_gather(jnp.stack([query_gain, key_gain, attn_gain, mlp_gain]), pl...]
    reshape x3 -> x9, local copies, waits for them, and re-layouts: 82.8 us -> 10.4 us  [the longest x4 4.23 us: team_hidden(): parts = weight.reshape(rows, 2, 2, 2, 2, 2, -1)]
    ppermute x0 -> x87, starting transfers between devices: none -> 71.5 us  [the longest x85 68.3 us: swap(): return lax.ppermute(value, axis, ((0, 1), (1, 0)))]
  transfers between devices with their start and end apart: 7 -> 92, of which waited for: 6 -> 38; matrix products, arithmetic and copies ran while one was open for 13% -> 30% of each run, Pallas kernels for 0% -> 0%
where the time goes in v1:
time: 1310 us; the launch traced here: 1300 us
  waiting for transfers between devices  610 us (47%)
  local copies, waits for them, and re-layouts  201 us (15%)
  matrix products  180 us (14%)
  other arithmetic  123 us (9%)
  starting transfers between devices  90.3 us (7%)
  blocking collectives  81.3 us (6%)
  between operations  16.5 us (1%)
    ppermute x85, waiting for transfers between devices, swap(): return lax.ppermute(value, axis, ((0, 1), (1, 0)))  502 us
    unnamed x2, waiting for transfers between devices  108 us
    unnamed x248, local copies, waits for them, and re-layouts  106 us
    all_gather x1, blocking collectives, local(): lax.all_gather(jnp.stack([query_gain, key_gain, attn_gain, mlp_gain]), pl...  81.3 us
    ppermute x85, starting transfers between devices, swap(): return lax.ppermute(value, axis, ((0, 1), (1, 0)))  68.3 us
    dot_general x6, matrix products, product_tt(): lax.dot_general(left, right, (((1,), (1,)), ((), ())), preferred_element_...  65.9 us
    dot_general x6, matrix products, product(): return jnp.dot(left, right, preferred_element_type=f32)  49.2 us
    dot_general x4, matrix products, inner_rows(): lax.dot_general(left, right, (((0,), (0,)), ((), ())), preferred_element_...  48.3 us
  transfers between devices with their start and end apart: 92, of which 38 were waited for; matrix products, arithmetic and copies ran while one was open for 30% of the time, Pallas kernels for 0%

profile of v1, /device:TPU:0, one launch (start us, length us, event | category | flops | bytes accessed | tf_op | source)
XLA Modules:
  0.0 1302.0 jit_solution(13585861523160253269)
XLA Ops:
  25.3 81.3 %all-gather = bf16[32,64,4]{1,2,0:T(4,128)(2,1)S(1)} all-gather(bf16[1,64,4]{1,2,0:T(4,128)(2,1)S(1)} %maximum_bitcast_fusion), channel_id=1, replica_groups=mesh['y'=2,'x'=2,'c'=2,'zh'=2,'zl'=2] {'y','x','c','zh','zl'}, dimensions={0}, use_global_device_ids=true | all-gather | bytes 16896 | tf_op jit(solution)/shard_map/all_gather | solution.py:293
  133.9 10.8 collective-permute-done.19
  166.6 31.0 %collective-permute-done.9 = bf16[2,2,2,64,768]{4,3,1,0,2:T(8,128)(2,1)S(1)} collective-permute-done((bf16[2,2,2,64,768]{4,3,1,0,2:T(8,128)(2,1)}, bf16[2,2,2,64,768]{4,3,1,0,2:T(8,128)(2,1)S(1)}, u32[]{:S(2)}, u32[]{:S(2)}) %collective-permute-start.9) | collective-permute-done | bytes 786464 | tf_op jit(solution)/shard_map/ppermute | solution.py:79
  205.1 12.9 collective-permute-done.11
  223.3 9.4 fusion.112
  273.3 7.1 subtract_convert_fusion.1
  301.0 46.0 %collective-permute-done.39 = bf16[256,2048]{1,0:T(8,128)(2,1)} collective-permute-done((bf16[256,2048]{1,0:T(8,128)(2,1)}, bf16[256,2048]{1,0:T(8,128)(2,1)}, u32[]{:S(2)}, u32[]{:S(2)}) %collective-permute-start.39) | collective-permute-done | bytes 1048608 | tf_op jit(solution)/shard_map/ppermute | solution.py:79
  349.4 22.8 %collective-permute-done.41 = bf16[256,2048]{1,0:T(8,128)(2,1)} collective-permute-done((bf16[256,2048]{1,0:T(8,128)(2,1)}, bf16[256,2048]{1,0:T(8,128)(2,1)}, u32[]{:S(2)}, u32[]{:S(2)}) %collective-permute-start.41) | collective-permute-done | bytes 1048608 | tf_op jit(solution)/shard_map/ppermute | solution.py:79
  378.0 62.2 %collective-permute-done.36 = bf16[2,2,2,64,2048]{4,3,1,0,2:T(8,128)(2,1)} collective-permute-done((bf16[2,2,2,64,2048]{4,3,1,0,2:T(8,128)(2,1)}, bf16[2,2,2,64,2048]{4,3,1,0,2:T(8,128)(2,1)}, u32[]{:S(2)}, u32[]{:S(2)}) %collective-permute-start.36) | collective-permute-done | bytes 2097184 | tf_op jit(solution)/shard_map/ppermute | solution.py:79
  448.9 21.4 %collective-permute-done.25 = bf16[2,128,2048]{2,1,0:T(8,128)(2,1)S(1)} collective-permute-done((bf16[2,128,2048]{2,1,0:T(8,128)(2,1)S(1)}, bf16[2,128,2048]{2,1,0:T(8,128)(2,1)S(1)}, u32[]{:S(2)}, u32[]{:S(2)}) %collective-permute-start.25) | collective-permute-done | bytes 1048608 | tf_op jit(solution)/shard_map/ppermute | solution.py:79
  476.9 11.1 collective-permute-done.38
  497.8 8.6 collective-permute-done.27
  514.6 8.3 copy.345
  543.4 22.0 %fusion.113 = f32[2048,2048]{0,1:T(8,128)} fusion(bf16[2048,2048]{1,0:T(8,128)(2,1)} %slice_dynamic-update-slice_fusion.4, bf16[2048,2048]{1,0:T(8,128)(2,1)S(1)} %bitcast.384), kind=kOutput, calls=%fused_computation.365 | convolution fusion | flops 17179869184 | bytes 33554432 | tf_op jit(solution)/shard_map/dot_general | solution.py:16
  565.4 7.2 multiply_convert_fusion.2
  592.8 23.3 %collective-permute-done.45 = bf16[2,128,2048]{2,1,0:T(8,128)(2,1)S(1)} collective-permute-done((bf16[2,128,2048]{2,1,0:T(8,128)(2,1)S(1)}, bf16[2,128,2048]{2,1,0:T(8,128)(2,1)S(1)}, u32[]{:S(2)}, u32[]{:S(2)}) %collective-permute-start.45) | collective-permute-done | bytes 1048608 | tf_op jit(solution)/shard_map/ppermute | solution.py:79
  618.9 11.0 collective-permute-done.46
  639.5 11.0 collective-permute-done.47
  662.7 8.3 collective-permute-done.51
  687.0 21.1 %multiply_convert_fusion = (bf16[2048,1024]{0,1:T(8,128)(2,1)}, bf16[2048,1024]{0,1:T(8,128)(2,1)}) fusion(f32[2048,2048]{0,1:T(8,128)} %fusion.113, bf16[2048,2048]{1,0:T(8,128)(2,1)} %slice_dynamic-update-slice_fusion.2, bf16[1024,2048]{1,0:T(8,128)(2,1)} %bitcast.404), kind=kOutput, calls=%fused_computation.11 | convolution fusion | flops 8617197568 | bytes 37748736 | tf_op jit(solution)/shard_map/dot_general | solution.py:20
  708.1 12.2 fusion.11
  720.9 23.9 %fusion.3 = bf16[2048,2048]{1,0:T(8,128)(2,1)} fusion(bf16[2048,2048]{1,0:T(8,128)(2,1)} %slice_dynamic-update-slice_fusion.4, bf16[2048,1024]{0,1:T(8,128)(2,1)} %get-tuple-element.31, bf16[2048,1024]{0,1:T(8,128)(2,1)} %get-tuple-element.32), kind=kOutput, calls=%fused_computation.18 | convolution fusion | flops 17200840704 | bytes 25165824 | tf_op jit(solution)/shard_map/dot_general | solution.py:24
  751.4 11.2 convolution_convert_fusion
  767.1 16.1 %convert_add_fusion.2 = f32[1024,2048]{1,0:T(8,128)} fusion(bf16[1024,2048]{1,0:T(8,128)(2,1)} %collective-permute-done.56, bf16[2048,2048]{1,0:T(8,128)(2,1)} %bitcast.381, bf16[2048,1024]{0,1:T(8,128)(2,1)} %get-tuple-element.32, bf16[2048,1024]{0,1:T(8,128)(2,1)} %get-tuple-element.31), kind=kOutput, calls=%fused_computation.10 | convolution fusion | flops 8602517504 | bytes 29360128 | tf_op jit(solution)/shard_map/dot_general | solution.py:20
  791.9 51.2 %collective-permute-done.83 = bf16[2,2,2,2,64,2048]{5,4,1,0,3,2:T(8,128)(2,1)} collective-permute-done((bf16[2,2,2,2,64,2048]{5,4,1,0,3,2:T(8,128)(2,1)S(1)}, bf16[2,2,2,2,64,2048]{5,4,1,0,3,2:T(8,128)(2,1)}, u32[]{:S(2)}, u32[]{:S(2)}) %collective-permute-start.83) | collective-permute-done | bytes 4194336 | tf_op jit(solution)/shard_map/ppermute | solution.py:79
  854.9 14.0 %collective-permute-done.60 = bf16[128,2048]{1,0:T(8,128)(2,1)S(1)} collective-permute-done((bf16[128,2048]{1,0:T(8,128)(2,1)S(1)}, bf16[128,2048]{1,0:T(8,128)(2,1)S(1)}, u32[]{:S(2)}, u32[]{:S(2)}) %collective-permute-start.60) | collective-permute-done | bytes 524320 | tf_op jit(solution)/shard_map/ppermute | solution.py:79
  874.8 12.3 collective-permute-done.85
  894.4 24.8 %collective-permute-done.64 = bf16[128,2048]{1,0:T(8,128)(2,1)S(1)} collective-permute-done((bf16[128,2048]{1,0:T(8,128)(2,1)}, bf16[128,2048]{1,0:T(8,128)(2,1)S(1)}, u32[]{:S(2)}, u32[]{:S(2)}) %collective-permute-start.64) | collective-permute-done | bytes 524320 | tf_op jit(solution)/shard_map/ppermute | solution.py:79
  921.6 48.7 %collective-permute-done.84 = bf16[2,2,2,64,2048]{4,3,1,0,2:T(8,128)(2,1)S(1)} collective-permute-done((bf16[2,2,2,64,2048]{4,3,1,0,2:T(8,128)(2,1)S(1)}, bf16[2,2,2,64,2048]{4,3,1,0,2:T(8,128)(2,1)S(1)}, u32[]{:S(2)}, u32[]{:S(2)}) %collective-permute-start.84) | collective-permute-done | bytes 2097184 | tf_op jit(solution)/shard_map/ppermute | solution.py:79
  1060.5 7.1 convolution_convert_fusion.4
  1075.7 107.7 %reduce-scatter.4.cloned.1.call-done = f32[64,4]{1,0:T(8,128)} async-done(((f32[2048,4]{1,0:T(8,128)}), f32[64,4]{1,0:T(8,128)}) %reduce-scatter.4.cloned.1.call-update) | async-done | bytes 1040
  1246.8 27.8 %collective-permute-done.74 = bf16[2,128,2048]{2,1,0:T(8,128)(2,1)S(1)} collective-permute-done((bf16[2,128,2048]{2,1,0:T(8,128)(2,1)S(1)}, bf16[2,128,2048]{2,1,0:T(8,128)(2,1)S(1)}, u32[]{:S(2)}, u32[]{:S(2)}) %collective-permute-start.74) | collective-permute-done | bytes 1048608 | tf_op jit(solution)/shard_map/ppermute | solution.py:79
  (619 shorter events, 491.6 us)
Async XLA Ops:
  9.5 121.6 %collective-permute-start = (bf16[128,2048]{1,0:T(8,128)(2,1)}, bf16[128,2048]{1,0:T(8,128)(2,1)}, u32[]{:S(2)}, u32[]{:S(2)}) collective-permute-start(bf16[128,2048]{1,0:T(8,128)(2,1)} %get-tuple-element.87), channel_id=1, source_target_pairs={{0,8},{8,0},{1,9},{9,1},{2,10},{10,2},{3,11},{11,3},{4,12},{12,4},... | collective-permute-start | bytes 1572872 | tf_op jit(solution)/shard_map/ppermute | solution.py:79
  12.4 137.7 %collective-permute-start.2 = (bf16[128,2048]{1,0:T(8,128)(2,1)}, bf16[128,2048]{1,0:T(8,128)(2,1)}, u32[]{:S(2)}, u32[]{:S(2)}) collective-permute-start(bf16[128,2048]{1,0:T(8,128)(2,1)} %get-tuple-element.87), channel_id=1, source_target_pairs={{0,1},{1,0},{2,3},{3,2},{4,5},{5,4},{6,7},{7,6},{8,9},{9,8},{10,11... | collective-permute-start | bytes 1572872 | tf_op jit(solution)/shard_map/ppermute | solution.py:79
  14.0 134.2 %collective-permute-start.1 = (bf16[128,2048]{1,0:T(8,128)(2,1)}, bf16[128,2048]{1,0:T(8,128)(2,1)}, u32[]{:S(2)}, u32[]{:S(2)}) collective-permute-start(bf16[128,2048]{1,0:T(8,128)(2,1)} %get-tuple-element.86), channel_id=1, source_target_pairs={{0,8},{8,0},{1,9},{9,1},{2,10},{10,2},{3,11},{11,3},{4,12},{12,4},... | collective-permute-start | bytes 1572872 | tf_op jit(solution)/shard_map/ppermute | solution.py:79
  14.6 116.7 %collective-permute-start.3 = (bf16[128,2048]{1,0:T(8,128)(2,1)}, bf16[128,2048]{1,0:T(8,128)(2,1)}, u32[]{:S(2)}, u32[]{:S(2)}) collective-permute-start(bf16[128,2048]{1,0:T(8,128)(2,1)} %get-tuple-element.86), channel_id=1, source_target_pairs={{0,1},{1,0},{2,3},{3,2},{4,5},{5,4},{6,7},{7,6},{8,9},{9,8},{10,11... | collective-permute-start | bytes 1572872 | tf_op jit(solution)/shard_map/ppermute | solution.py:79
  17.9 134.2 %all-to-all-start = ((bf16[8,64,768]{2,1,0:T(8,128)(2,1)}), bf16[8,64,768]{2,1,0:T(8,128)(2,1)}, u32[]{:S(2)}, u32[]{:S(2)}) async-start(bf16[8,64,768]{2,1,0:T(8,128)(2,1)} %copy.328), calls=%async_computation | async-start | bytes 1572864 | tf_op jit(solution)/shard_map/all_to_all | solution.py:179
  22.1 95.1 %collective-permute-start.12 = (s32[2]{0:T(128)S(1)}, s32[2]{0:T(128)S(1)}, u32[]{:S(2)}, u32[]{:S(2)}) collective-permute-start(s32[2]{0:T(128)S(1)} %copy-done.85), channel_id=1, source_target_pairs={{0,8},{8,0},{1,9},{9,1},{2,10},{10,2},{3,11},{11,3},{4,12},{12,4},... | collective-permute-start | bytes 32 | tf_op jit(solution)/shard_map/ppermute | solution.py:79
  133.6 67.3 %collective-permute-start.7 = (bf16[256,2048]{1,0:T(8,128)(2,1)}, bf16[256,2048]{1,0:T(8,128)(2,1)}, u32[]{:S(2)}, u32[]{:S(2)}) collective-permute-start(bf16[256,2048]{1,0:T(8,128)(2,1)} %pad_maximum_fusion.23), channel_id=1, source_target_pairs={{0,4},{4,0},{1,5},{5,1},{2,6},{6,2},{3,7},{7,3},{8,12},{12,8},{9,1... | collective-permute-start | bytes 3145736 | tf_op jit(solution)/shard_map/ppermute | solution.py:79
  152.0 195.6 %all-to-all-start.1 = ((bf16[8,64,2048]{2,1,0:T(8,128)(2,1)}), bf16[8,64,2048]{2,1,0:T(8,128)(2,1)}, u32[]{:S(2)}, u32[]{:S(2)}) async-start(bf16[8,64,2048]{2,1,0:T(8,128)(2,1)} %pad_maximum_fusion.13), calls=%async_computation.1 | async-start | bytes 4194304 | tf_op jit(solution)/shard_map/all_to_all | solution.py:179
  160.3 75.7 %collective-permute-start.20 = (bf16[64,2048]{1,0:T(8,128)(2,1)}, bf16[64,2048]{1,0:T(8,128)(2,1)}, u32[]{:S(2)}, u32[]{:S(2)}) collective-permute-start(bf16[64,2048]{1,0:T(8,128)(2,1)} %copy-done.59), channel_id=1, source_target_pairs={{0,16},{16,0},{1,17},{17,1},{2,18},{18,2},{3,19},{19,3},{4,20},{20... | collective-permute-start | bytes 786440 | tf_op jit(solution)/shard_map/ppermute | solution.py:79
  164.8 54.1 %collective-permute-start.8 = (bf16[512,2048]{1,0:T(8,128)(2,1)S(1)}, bf16[512,2048]{1,0:T(8,128)(2,1)S(1)}, u32[]{:S(2)}, u32[]{:S(2)}) collective-permute-start(bf16[512,2048]{1,0:T(8,128)(2,1)S(1)} %pad_maximum_fusion.10), channel_id=1, source_target_pairs={{0,4},{4,0},{1,5},{5,1},{2,6},{6,2},{3,7},{7,3},{8,12},{12,8},{9,1... | collective-permute-start | bytes 6291464 | tf_op jit(solution)/shard_map/ppermute | solution.py:79
  297.8 143.5 %collective-permute-start.22 = (bf16[1024,2048]{1,0:T(8,128)(2,1)}, bf16[1024,2048]{1,0:T(8,128)(2,1)}, u32[]{:S(2)}, u32[]{:S(2)}) collective-permute-start(bf16[1024,2048]{1,0:T(8,128)(2,1)} %convolution_convert_fusion.1), channel_id=1, source_target_pairs={{0,4},{4,0},{1,5},{5,1},{2,6},{6,2},{3,7},{7,3},{8,12},{12,8},{9,1... | collective-permute-start | bytes 12582920 | tf_op jit(solution)/shard_map/ppermute | solution.py:79
  297.8 49.3 %collective-permute-start.39 = (bf16[256,2048]{1,0:T(8,128)(2,1)}, bf16[256,2048]{1,0:T(8,128)(2,1)}, u32[]{:S(2)}, u32[]{:S(2)}) collective-permute-start(bf16[256,2048]{1,0:T(8,128)(2,1)} %param.22), channel_id=1, source_target_pairs={{0,2},{2,0},{1,3},{3,1},{4,6},{6,4},{5,7},{7,5},{8,10},{10,8},{9,1... | collective-permute-start | bytes 3145736 | tf_op jit(solution)/shard_map/ppermute | solution.py:79
  300.1 49.2 %collective-permute-start.40 = (bf16[256,2048]{1,0:T(8,128)(2,1)}, bf16[256,2048]{1,0:T(8,128)(2,1)}, u32[]{:S(2)}, u32[]{:S(2)}) collective-permute-start(bf16[256,2048]{1,0:T(8,128)(2,1)} %param.22), channel_id=1, source_target_pairs={{0,16},{16,0},{1,17},{17,1},{2,18},{18,2},{3,19},{19,3},{4,20},{20... | collective-permute-start | bytes 3145736 | tf_op jit(solution)/shard_map/ppermute | solution.py:79
  347.7 92.6 %collective-permute-start.36 = (bf16[2,2,2,64,2048]{4,3,1,0,2:T(8,128)(2,1)}, bf16[2,2,2,64,2048]{4,3,1,0,2:T(8,128)(2,1)}, u32[]{:S(2)}, u32[]{:S(2)}) collective-permute-start(bf16[2,2,2,64,2048]{4,3,1,0,2:T(8,128)(2,1)} %bitcast.49), channel_id=1, source_target_pairs={{0,2},{2,0},{1,3},{3,1},{4,6},{6,4},{5,7},{7,5},{8,10},{10,8},{9,1... | collective-permute-start | bytes 6291464 | tf_op jit(solution)/shard_map/ppermute | solution.py:79
  377.2 99.7 %collective-permute-start.37 = (bf16[2,2,2,64,2048]{4,3,1,0,2:T(8,128)(2,1)}, bf16[2,2,2,64,2048]{4,3,1,0,2:T(8,128)(2,1)S(1)}, u32[]{:S(2)}, u32[]{:S(2)}) collective-permute-start(bf16[2,2,2,64,2048]{4,3,1,0,2:T(8,128)(2,1)} %bitcast.49), channel_id=1, source_target_pairs={{0,16},{16,0},{1,17},{17,1},{2,18},{18,2},{3,19},{19,3},{4,20},{20... | collective-permute-start | bytes 6291464 | tf_op jit(solution)/shard_map/ppermute | solution.py:79
  440.2 47.8 %collective-permute-start.38 = (bf16[2,2,2,64,2048]{4,3,1,0,2:T(8,128)(2,1)}, bf16[2,2,2,64,2048]{4,3,1,0,2:T(8,128)(2,1)S(1)}, u32[]{:S(2)}, u32[]{:S(2)}) collective-permute-start(bf16[2,2,2,64,2048]{4,3,1,0,2:T(8,128)(2,1)} %collective-permute-done.36), channel_id=1, source_target_pairs={{0,16},{16,0},{1,17},{17,1},{2,18},{18,2},{3,19},{19,3},{4,20},{20... | collective-permute-start | bytes 6291464 | tf_op jit(solution)/shard_map/ppermute | solution.py:79
  720.4 46.8 %collective-permute-start.56 = (bf16[1024,2048]{1,0:T(8,128)(2,1)}, bf16[1024,2048]{1,0:T(8,128)(2,1)}, u32[]{:S(2)}, u32[]{:S(2)}) collective-permute-start(bf16[1024,2048]{1,0:T(8,128)(2,1)} %fusion.11), channel_id=1, source_target_pairs={{0,4},{4,0},{1,5},{5,1},{2,6},{6,2},{3,7},{7,3},{8,12},{12,8},{9,1... | collective-permute-start | bytes 12582920 | tf_op jit(solution)/shard_map/ppermute | solution.py:79
  749.5 93.6 %collective-permute-start.83 = (bf16[2,2,2,2,64,2048]{5,4,1,0,3,2:T(8,128)(2,1)S(1)}, bf16[2,2,2,2,64,2048]{5,4,1,0,3,2:T(8,128)(2,1)}, u32[]{:S(2)}, u32[]{:S(2)}) collective-permute-start(bf16[2,2,2,2,64,2048]{5,4,1,0,3,2:T(8,128)(2,1)S(1)} %bitcast.407), channel_id=1, source_target_pairs={{0,16},{16,0},{1,17},{17,1},{2,18},{18,2},{3,19},{19,3},{4,20},{20... | collective-permute-start | bytes 12582920 | tf_op jit(solution)/shard_map/ppermute | solution.py:79
  766.0 121.1 %collective-permute-start.85 = (bf16[2,256,2048]{2,1,0:T(8,128)(2,1)}, bf16[2,256,2048]{2,1,0:T(8,128)(2,1)}, u32[]{:S(2)}, u32[]{:S(2)}) collective-permute-start(bf16[2,256,2048]{2,1,0:T(8,128)(2,1)} %dynamic-slice_bitcast_fusion), channel_id=1, source_target_pairs={{0,16},{16,0},{1,17},{17,1},{2,18},{18,2},{3,19},{19,3},{4,20},{20... | collective-permute-start | bytes 6291464 | tf_op jit(solution)/shard_map/ppermute | solution.py:79
  786.8 60.3 %collective-permute-start.59 = (bf16[2,128,2048]{2,1,0:T(8,128)(2,1)}, bf16[2,128,2048]{2,1,0:T(8,128)(2,1)}, u32[]{:S(2)}, u32[]{:S(2)}) collective-permute-start(bf16[2,128,2048]{2,1,0:T(8,128)(2,1)} %fusion.52), channel_id=1, source_target_pairs={{0,8},{8,0},{1,9},{9,1},{2,10},{10,2},{3,11},{11,3},{4,12},{12,4},... | collective-permute-start | bytes 3145736 | tf_op jit(solution)/shard_map/ppermute | solution.py:79
  790.6 59.9 %collective-permute-start.57 = (bf16[2,128,2048]{2,1,0:T(8,128)(2,1)}, bf16[2,128,2048]{2,1,0:T(8,128)(2,1)S(1)}, u32[]{:S(2)}, u32[]{:S(2)}) collective-permute-start(bf16[2,128,2048]{2,1,0:T(8,128)(2,1)} %fusion.56), channel_id=1, source_target_pairs={{0,1},{1,0},{2,3},{3,2},{4,5},{5,4},{6,7},{7,6},{8,9},{9,8},{10,11... | collective-permute-start | bytes 3145736 | tf_op jit(solution)/shard_map/ppermute | solution.py:79
  853.3 116.9 %collective-permute-start.84 = (bf16[2,2,2,64,2048]{4,3,1,0,2:T(8,128)(2,1)S(1)}, bf16[2,2,2,64,2048]{4,3,1,0,2:T(8,128)(2,1)S(1)}, u32[]{:S(2)}, u32[]{:S(2)}) collective-permute-start(bf16[2,2,2,64,2048]{4,3,1,0,2:T(8,128)(2,1)S(1)} %fusion.17), channel_id=1, source_target_pairs={{0,2},{2,0},{1,3},{3,1},{4,6},{6,4},{5,7},{7,5},{8,10},{10,8},{9,1... | collective-permute-start | bytes 6291464 | tf_op jit(solution)/shard_map/ppermute | solution.py:79
  890.8 182.1 %collective-permute-start.86 = (bf16[256,2048]{1,0:T(8,128)(2,1)}, bf16[256,2048]{1,0:T(8,128)(2,1)}, u32[]{:S(2)}, u32[]{:S(2)}) collective-permute-start(bf16[256,2048]{1,0:T(8,128)(2,1)} %fusion.49), channel_id=1, source_target_pairs={{0,2},{2,0},{1,3},{3,1},{4,6},{6,4},{5,7},{7,5},{8,10},{10,8},{9,1... | collective-permute-start | bytes 3145736 | tf_op jit(solution)/shard_map/ppermute | solution.py:79
  892.9 85.5 %collective-permute-start.62 = (bf16[128,2048]{1,0:T(8,128)(2,1)}, bf16[128,2048]{1,0:T(8,128)(2,1)}, u32[]{:S(2)}, u32[]{:S(2)}) collective-permute-start(bf16[128,2048]{1,0:T(8,128)(2,1)} %get-tuple-element.78), channel_id=1, source_target_pairs={{0,8},{8,0},{1,9},{9,1},{2,10},{10,2},{3,11},{11,3},{4,12},{12,4},... | collective-permute-start | bytes 1572872 | tf_op jit(solution)/shard_map/ppermute | solution.py:79
  893.3 85.5 %collective-permute-start.63 = (bf16[128,2048]{1,0:T(8,128)(2,1)}, bf16[128,2048]{1,0:T(8,128)(2,1)}, u32[]{:S(2)}, u32[]{:S(2)}) collective-permute-start(bf16[128,2048]{1,0:T(8,128)(2,1)} %get-tuple-element.79), channel_id=1, source_target_pairs={{0,1},{1,0},{2,3},{3,2},{4,5},{5,4},{6,7},{7,6},{8,9},{9,8},{10,11... | collective-permute-start | bytes 1572872 | tf_op jit(solution)/shard_map/ppermute | solution.py:79
  919.2 59.8 %collective-permute-start.65 = (bf16[128,2048]{1,0:T(8,128)(2,1)S(1)}, bf16[128,2048]{1,0:T(8,128)(2,1)}, u32[]{:S(2)}, u32[]{:S(2)}) collective-permute-start(bf16[128,2048]{1,0:T(8,128)(2,1)S(1)} %collective-permute-done.61), channel_id=1, source_target_pairs={{0,1},{1,0},{2,3},{3,2},{4,5},{5,4},{6,7},{7,6},{8,9},{9,8},{10,11... | collective-permute-start | bytes 1572872 | tf_op jit(solution)/shard_map/ppermute | solution.py:79
  974.0 233.0 %all-to-all-start.3 = ((bf16[8,64,2048]{2,1,0:T(8,128)(2,1)}), bf16[8,64,2048]{2,1,0:T(8,128)(2,1)}, u32[]{:S(2)}, u32[]{:S(2)}) async-start(bf16[8,64,2048]{2,1,0:T(8,128)(2,1)} %bitcast.118), calls=%async_computation.3 | async-start | bytes 4194304 | tf_op jit(solution)/shard_map/all_to_all | solution.py:188
  978.3 205.1 %reduce-scatter.4.cloned.1.call-start = ((), (), s32[]{:S(2)}) async-start(), calls=%async_computation.5 | async-start | bytes 1081344
  1060.5 134.3 %collective-permute-start.73 = (bf16[1024,2048]{1,0:T(8,128)(2,1)}, bf16[1024,2048]{1,0:T(8,128)(2,1)}, u32[]{:S(2)}, u32[]{:S(2)}) collective-permute-start(bf16[1024,2048]{1,0:T(8,128)(2,1)} %convolution_convert_fusion.2), channel_id=1, source_target_pairs={{0,4},{4,0},{1,5},{5,1},{2,6},{6,2},{3,7},{7,3},{8,12},{12,8},{9,1... | collective-permute-start | bytes 12582920 | tf_op jit(solution)/shard_map/ppermute | solution.py:79
  1069.1 121.1 %collective-permute-start.78 = (bf16[2,2,2,2,64,768]{5,4,1,0,3,2:T(8,128)(2,1)}, bf16[2,2,2,2,64,768]{5,4,1,0,3,2:T(8,128)(2,1)}, u32[]{:S(2)}, u32[]{:S(2)}) collective-permute-start(bf16[2,2,2,2,64,768]{5,4,1,0,3,2:T(8,128)(2,1)} %bitcast.366), channel_id=1, source_target_pairs={{0,16},{16,0},{1,17},{17,1},{2,18},{18,2},{3,19},{19,3},{4,20},{20... | collective-permute-start | bytes 4718600 | tf_op jit(solution)/shard_map/ppermute | solution.py:79
  1071.9 114.9 %collective-permute-start.81 = (bf16[64,2048]{1,0:T(8,128)(2,1)S(1)}, bf16[64,2048]{1,0:T(8,128)(2,1)S(1)}, u32[]{:S(2)}, u32[]{:S(2)}) collective-permute-start(bf16[64,2048]{1,0:T(8,128)(2,1)S(1)} %fusion.86), channel_id=1, source_target_pairs={{0,2},{2,0},{1,3},{3,1},{4,6},{6,4},{5,7},{7,5},{8,10},{10,8},{9,1... | collective-permute-start | bytes 786440 | tf_op jit(solution)/shard_map/ppermute | solution.py:79
  1234.9 45.3 %all-to-all-start.2 = ((bf16[8,64,768]{2,1,0:T(8,128)(2,1)}), bf16[8,64,768]{2,1,0:T(8,128)(2,1)}, u32[]{:S(2)}, u32[]{:S(2)}) async-start(bf16[8,64,768]{2,1,0:T(8,128)(2,1)} %bitcast.103), calls=%async_computation.2 | async-start | bytes 1572864 | tf_op jit(solution)/shard_map/all_to_all | solution.py:188
  (153 other events, 2975.2 us)
Sparse Core Ops, SparseCore 0:
  1048.3 135.0 reduce-scatter.3

commit v2 on v1

v2 whole, which is shorter than its diff:
```python
import functools

import jax
import jax.numpy as jnp
from jax import lax
from jax.experimental import pallas as pl
from jax.experimental.pallas import tpu as pltpu
from jax.sharding import Mesh, PartitionSpec as P

HEAD_DIM = 128
BLOCK = 128

epsilon = 1e-06
rope_base = 500000.0
f32 = jnp.float32
bf16 = jnp.bfloat16
NO_COST = pl.CostEstimate(flops=0, bytes_accessed=0, transcendentals=0)


def product(left, right):
    return jnp.dot(left, right, preferred_element_type=f32)


def product_tt(left, right):
    return lax.dot_general(left, right, (((1,), (1,)), ((), ())), preferred_element_type=f32)


def inner_rows(left, right):
    return lax.dot_general(left, right, (((0,), (0,)), ((), ())), preferred_element_type=f32)


def norm_forward(values, gain):
    inverse = lax.rsqrt(jnp.mean(values * values, axis=-1, keepdims=True) + epsilon)
    return (values * inverse * gain, inverse)


def norm_back(values, inverse, gain, incoming):
    normed = values * inverse
    scaled = incoming * gain
    gain_term = jnp.sum(incoming * normed, axis=0)
    back = inverse * (scaled - normed * jnp.mean(scaled * normed, axis=-1, keepdims=True))
    return (back, gain_term)


def angles(position):
    half = HEAD_DIM // 2
    freq = rope_base ** (-jnp.arange(half, dtype=f32) / half)
    angle = position.astype(f32).reshape(-1, 1) * freq
    cosine, sine = jnp.cos(angle), jnp.sin(angle)
    return jnp.concatenate([cosine, cosine], axis=1), jnp.concatenate([-sine, sine], axis=1)


def row_layout(lengths):
    nblock = lengths.shape[0]
    row_ids = jnp.arange(nblock * BLOCK, dtype=jnp.int32)
    begin = jnp.arange(nblock, dtype=jnp.int32) * BLOCK
    cover = (
        (lengths[None, :] > 0)
        & (row_ids[:, None] >= begin[None, :])
        & (row_ids[:, None] < begin[None, :] + lengths[None, :])
    )
    live = jnp.any(cover, axis=1)
    owner = jnp.sum(jnp.where(cover, begin[None, :], 0), axis=1)
    return (live, row_ids - owner)


def allowed_keys(lengths_ref, device, nrows):
    rows = lax.broadcasted_iota(jnp.int32, (nrows, nrows), 0)
    keys = lax.broadcasted_iota(jnp.int32, (nrows, nrows), 1)

    def number(ids):
        found = -1 - ids
        for block in range(nrows // BLOCK):
            begin, length = block * BLOCK, lengths_ref[device, block]
            found = jnp.where((ids >= begin) & (ids < begin + length), begin, found)
        return found

    return (number(rows) == number(keys)) & (keys <= rows)


def turn(values, cosine, sine):
    return values * cosine + pltpu.roll(values, HEAD_DIM // 2, 1) * sine


def probabilities(query, key, allowed):
    scores = product_tt(query, key) * HEAD_DIM ** (-0.5)
    scores = jnp.where(allowed, scores, -1e30)
    powers = jnp.exp(scores - jnp.max(scores, axis=-1, keepdims=True))
    return powers / jnp.sum(powers, axis=-1, keepdims=True)


def attend_kernel(
    lengths_ref, raw_ref, inverse_ref, gains_ref, cosine_ref, sine_ref, turned_ref, mixed_ref
):
    nrows, columns = mixed_ref.shape
    allowed = allowed_keys(lengths_ref, pl.program_id(0), nrows)
    cosine, sine = cosine_ref[...], sine_ref[...]
    for head in range(columns // HEAD_DIM):
        here = slice(head * HEAD_DIM, (head + 1) * HEAD_DIM)
        turned = []
        for which in range(2):
            there = slice(which * columns + here.start, which * columns + here.stop)
            normed = raw_ref[:, there] * inverse_ref[:, which : which + 1]
            rotated = turn(normed * gains_ref[which : which + 1, here], cosine, sine).astype(bf16)
            turned_ref[:, there] = rotated
            turned.append(rotated)
        there = slice(2 * columns + here.start, 2 * columns + here.stop)
        value = raw_ref[:, there].astype(bf16)
        turned_ref[:, there] = value
        probs = probabilities(turned[0], turned[1], allowed)
        mixed_ref[:, here] = product(probs.astype(bf16), value).astype(bf16)


def attend_back_kernel(
    lengths_ref, raw_ref, turned_ref, inverse_ref, gains_ref, cosine_ref, sine_ref, grad_ref,
    scaled_ref, grad_value_ref, means_ref, terms_ref,
):
    nrows, columns = grad_ref.shape
    device = pl.program_id(0)
    allowed = allowed_keys(lengths_ref, device, nrows)
    cosine, sine = cosine_ref[...], sine_ref[...]

    @pl.when(device == 0)
    def _():
        terms_ref[...] = jnp.zeros_like(terms_ref)

    sums = [0.0, 0.0]
    for head in range(columns // HEAD_DIM):
        here = slice(head * HEAD_DIM, (head + 1) * HEAD_DIM)
        spots = [slice(k * columns + here.start, k * columns + here.stop) for k in range(3)]
        query, key, value = (turned_ref[:, spot] for spot in spots)
        incoming = grad_ref[:, here]
        probs = probabilities(query, key, allowed)
        grad_probs = product_tt(incoming, value)
        inner = jnp.sum(probs * grad_probs, axis=-1, keepdims=True)
        grad_scores = (probs * (grad_probs - inner)).astype(bf16)
        grad_value_ref[:, here] = inner_rows(probs.astype(bf16), incoming).astype(bf16)
        back = (product(grad_scores, key), inner_rows(grad_scores, query))
        for which in range(2):
            turned = turn(back[which] * HEAD_DIM ** (-0.5), cosine, -sine)
            normed = raw_ref[:, spots[which]] * inverse_ref[:, which : which + 1]
            terms_ref[which : which + 1, here] += jnp.sum(turned * normed, axis=0, keepdims=True)
            scaled = turned * gains_ref[which : which + 1, here]
            scaled_ref[:, spots[which]] = scaled
            sums[which] = sums[which] + jnp.sum(scaled * normed, axis=-1, keepdims=True)
    means_ref[...] = jnp.concatenate(sums, axis=1)


def attend_specs(nrows, columns):
    def rows(wide):
        return pl.BlockSpec((nrows, wide), lambda b: (b, 0))

    lengths = pl.BlockSpec(memory_space=pltpu.SMEM)
    gains = pl.BlockSpec((2, columns), lambda b: (0, 0))
    return rows, lengths, gains


def attend(lengths, raw, inverse, gains, cosine, sine):
    size, nrows = lengths.shape[0], raw.shape[0] // lengths.shape[0]
    columns = raw.shape[1] // 3
    rows, whole, gain = attend_specs(nrows, columns)
    return pl.pallas_call(
        attend_kernel,
        grid=(size,),
        in_specs=[whole, rows(3 * columns), rows(2), gain, rows(HEAD_DIM), rows(HEAD_DIM)],
        out_specs=[rows(3 * columns), rows(columns)],
        out_shape=[
            jax.ShapeDtypeStruct(raw.shape, bf16),
            jax.ShapeDtypeStruct((raw.shape[0], columns), bf16),
        ],
        cost_estimate=NO_COST,
    )(lengths, raw, inverse, gains, cosine, sine)


def attend_back(lengths, raw, turned, inverse, gains, cosine, sine, grad):
    size, nrows = lengths.shape[0], raw.shape[0] // lengths.shape[0]
    columns = raw.shape[1] // 3
    rows, whole, gain = attend_specs(nrows, columns)
    return pl.pallas_call(
        attend_back_kernel,
        grid=(size,),
        in_specs=[
            whole, rows(3 * columns), rows(3 * columns), rows(2), gain,
            rows(HEAD_DIM), rows(HEAD_DIM), rows(columns),
        ],
        out_specs=[rows(2 * columns), rows(columns), rows(2), gain],
        out_shape=[
            jax.ShapeDtypeStruct((raw.shape[0], 2 * columns), f32),
            jax.ShapeDtypeStruct((raw.shape[0], columns), bf16),
            jax.ShapeDtypeStruct((raw.shape[0], 2), f32),
            jax.ShapeDtypeStruct((2, columns), f32),
        ],
        cost_estimate=NO_COST,
    )(lengths, raw, turned, inverse, gains, cosine, sine, grad)


def swap(value, axis):
    return lax.ppermute(value, axis, ((0, 1), (1, 0)))


def sync(*values):
    return lax.optimization_barrier(values)


def pick(value, index, axis):
    return lax.dynamic_index_in_dim(value, index, axis, keepdims=False)


def join_kernel(table_ref, *refs):
    pieces, out, held, sems = refs[:-3], refs[-3], refs[-2], refs[-1]
    loads, stores = [], []
    for k, piece in enumerate(pieces):
        here = pl.ds(pl.multiple_of(table_ref[k] * 64, 64), piece.shape[0])
        loads.append(pltpu.make_async_copy(piece, held.at[here], sems.at[0, k]))
        stores.append(pltpu.make_async_copy(held.at[here], out.at[here], sems.at[1, k]))
        loads[-1].start()
    for load, store in zip(loads, stores):
        load.wait()
        store.start()
    for store in stores:
        store.wait()


def join(*pieces, table=None):
    if table is None:
        begins = [sum(piece.shape[0] for piece in pieces[:k]) // 64 for k in range(len(pieces))]
        table = jnp.array(begins, jnp.int32)
    shape = (sum(piece.shape[0] for piece in pieces), pieces[0].shape[1])
    return pl.pallas_call(
        join_kernel,
        in_specs=[pl.BlockSpec(memory_space=pltpu.SMEM)]
        + [pl.BlockSpec(memory_space=pl.ANY)] * len(pieces),
        out_specs=pl.BlockSpec(memory_space=pl.ANY),
        out_shape=jax.ShapeDtypeStruct(shape, pieces[0].dtype),
        scratch_shapes=[
            pltpu.VMEM(shape, pieces[0].dtype),
            pltpu.SemaphoreType.DMA((2, len(pieces))),
        ],
        compiler_params=pltpu.CompilerParams(vmem_limit_bytes=32 * 2**20),
        cost_estimate=NO_COST,
    )(table, *pieces)


def regroup_kernel(halves, in_ref, out_ref):
    for tile in range(len(halves) // 2):
        parts = [in_ref[:, half * 64 : (half + 1) * 64] for half in halves[2 * tile : 2 * tile + 2]]
        out_ref[:, tile * 128 : (tile + 1) * 128] = jnp.concatenate(parts, axis=1)


def regroup(value, halves):
    rows, width = value.shape
    block = pl.BlockSpec((rows // 2, width), lambda k: (k, 0))
    return pl.pallas_call(
        functools.partial(regroup_kernel, halves),
        grid=(2,),
        in_specs=[block],
        out_specs=block,
        out_shape=jax.ShapeDtypeStruct(value.shape, value.dtype),
        cost_estimate=NO_COST,
    )(value)


def spread_kernel(order, parts_ref, out_ref):
    wide = out_ref.shape[1] // len(order)
    for block, (part, column) in enumerate(order):
        here = slice(block * wide, (block + 1) * wide)
        out_ref[:, here] = parts_ref[part, :, column * wide : (column + 1) * wide].astype(f32)


def spread(parts, order):
    shape = (parts.shape[1], parts.shape[0] * parts.shape[2])
    return pl.pallas_call(
        functools.partial(spread_kernel, order),
        in_specs=[pl.BlockSpec(memory_space=pltpu.VMEM)],
        out_specs=pl.BlockSpec(memory_space=pltpu.VMEM),
        out_shape=jax.ShapeDtypeStruct(shape, f32),
        cost_estimate=NO_COST,
    )(parts)


class Cube:
    every = ("y", "x", "c", "zh", "zl")
    team = ("y", "x")
    z_axes = ("zh", "zl")
    group = ("c", "zh", "zl")

    def __init__(self):
        self.place = [lax.axis_index(axis) for axis in self.every]
        self.core = self.place[2]
        self.z = lax.axis_index(self.z_axes)
        self.size = 4
        self.index = lax.axis_index(self.team)

    def shift(self, value):
        return lax.ppermute(value, self.z_axes, ((0, 1), (1, 2), (2, 3), (3, 0)))

    def rows_first(self, rows):
        half = rows.shape[0] // 2
        top, low = rows[:half], rows[half:]
        return top, low, swap(top, "x"), swap(low, "y")

    def rows_second(self, top, low, top_x, low_y):
        top_y, low_x = swap(top, "y"), swap(low, "x")
        return top, low, top_x, low_x, top_y, low_y, swap(top_x, "y"), swap(low_y, "x")

    def terms_first(self, terms):
        terms = terms.reshape(2, 2, 2, -1, terms.shape[1])
        top, low = swap(terms[1, :, 0], "y"), swap(terms[:, 1, 1], "x")
        return terms[0, :, 0], terms[:, 0, 1], top, low

    def terms_second(self, top, low, top_y, low_x):
        top = top.astype(f32) + top_y.astype(f32)
        low = low.astype(f32) + low_x.astype(f32)
        return top[0], low[0], swap(top[1].astype(bf16), "x"), swap(low[1].astype(bf16), "y")

    def terms_sum(self, top, low, top_x, low_y):
        return jnp.concatenate([top + top_x.astype(f32), low + low_y.astype(f32)])

    def sum_rows(self, rows):
        shape = rows.shape
        rows = rows.reshape((2, 2, -1) + shape[1:])
        for dim, axis in enumerate(self.team):
            rows = rows + jnp.flip(swap(rows, axis), dim)
        return rows.reshape(shape)

    def order(self, mine, other, index, axis):
        first = index == 0
        return jnp.stack([jnp.where(first, mine, other), jnp.where(first, other, mine)], axis)

    def team_columns(self, weight):
        rows = weight.shape[0]
        return weight.reshape(rows, 4, -1).transpose(1, 0, 2)

    def whole_columns(self, parts):
        return spread(parts, [(part, 0) for part in range(4)])

    def send_columns(self, parts):
        return lax.all_to_all(parts, self.team, 0, 0).reshape(-1, parts.shape[2])

    def return_columns(self, block):
        return lax.all_to_all(block.reshape(4, -1, block.shape[1]), self.team, 0, 0)

    def grouped(self, rows):
        return regroup(rows, [spot * 8 + place for place in range(8) for spot in range(4)])

    def ungrouped(self, rows):
        return regroup(rows, [place * 4 + spot for spot in range(4) for place in range(8)])

    def join_group(self, blocks):
        table, pieces = [], []
        for core in range(2):
            for k in range(4):
                unit = blocks[core][k].shape[0] // 64
                table.append(((self.core ^ core) * 4 + (self.z - k) % 4) * unit)
                pieces.append(blocks[core][k])
        return join(*pieces, table=jnp.stack(table).astype(jnp.int32))

    def core_halves(self, values):
        half = values.shape[1] // 2
        return [
            lax.dynamic_slice_in_dim(values, index * half, half, 1)
            for index in (1 - self.core, self.core)
        ]

    def ring_part(self, terms, k):
        rows = terms.shape[0] // 4
        return lax.dynamic_slice_in_dim(terms, (self.z - k) % 4 * rows, rows, 0)

    def small_rows(self, gains, lengths, width):
        small = [jnp.pad(row.astype(bf16), (0, width - row.shape[0])) for row in (*gains, lengths)]
        return jnp.pad(jnp.stack(small), ((0, 16 - len(small)), (0, 0)))

    def small_step(self, small, axis):
        index = self.place[self.every.index(axis)]
        small = self.order(small, swap(small, axis), index, 1)
        return small.reshape(small.shape[0], -1, small.shape[-1])

    def small_end(self, small, count):
        gains = small[:4].reshape(4, -1).astype(f32)
        y, x, c, _, _ = self.place
        ids = [
            (((y ^ dy) * 2 + (x ^ dx)) * 2 + c) * 4 + self.z for dy in range(2) for dx in range(2)
        ]
        lengths = jnp.stack([pick(small[4], i, 0) for i in ids])[:, :count]
        return gains, lengths.astype(jnp.int32)

    def gain_step(self, terms, axis, dim):
        index = self.place[self.every.index(axis)]
        return pick(terms, index, dim) + swap(pick(terms, 1 - index, dim), axis)

    def own_gains(self, terms):
        terms = terms.reshape(terms.shape[0], 2, 2, 2, -1)
        for index in self.place[2:]:
            terms = pick(terms, index, 1)
        return terms


class Plain:
    def __init__(self, team, group):
        self.team, self.group = team, group
        self.every = (team, group)
        self.size = lax.axis_size(team)
        self.index = lax.axis_index(team)

    def gather_rows(self, rows):
        return lax.all_gather(rows, self.team, axis=0, tiled=True)

    def scatter_rows(self, terms):
        return lax.psum_scatter(terms, self.team, scatter_dimension=0, tiled=True).astype(f32)

    def sum_rows(self, rows):
        return lax.psum(rows, self.team)

    def gather_columns(self, weight):
        rows = weight.shape[0]
        parts = weight.reshape(rows, self.size, -1).transpose(1, 0, 2)
        block = lax.all_to_all(parts, self.team, 0, 0)
        whole = lax.all_gather(block, self.group, axis=1, tiled=True)
        return whole.reshape(-1, block.shape[2])

    def scatter_columns(self, terms):
        terms = terms.reshape(self.size, -1, terms.shape[1])
        block = lax.psum_scatter(terms, self.group, scatter_dimension=1, tiled=True)
        parts = lax.all_to_all(block, self.team, 0, 0)
        return parts.transpose(1, 0, 2).reshape(parts.shape[1], -1).astype(f32)

    def gather_group(self, weight):
        return lax.all_gather(weight, self.group, axis=0, tiled=True)

    def scatter_group(self, terms, axis=0):
        block = lax.psum_scatter(terms, self.group, scatter_dimension=axis, tiled=True)
        return block.astype(f32)


def norm_columns(raw, columns):
    parts = [raw[:, k * columns : (k + 1) * columns] for k in (0, 1)]
    return jnp.stack([jnp.sum(part * part, axis=-1) for part in parts], axis=-1)


def raw_back(raw, scaled, inverse, means, grad_value):
    columns = grad_value.shape[1]
    grads = []
    for which in (0, 1):
        here = slice(which * columns, (which + 1) * columns)
        scale = inverse[:, which : which + 1]
        normed = raw[:, here] * scale
        grad = scale * (scaled[:, here] - normed * means[:, which : which + 1])
        grads.append(grad.astype(bf16))
    return jnp.concatenate(grads + [grad_value], axis=1)


def local_plain(
    plan,
    tokens,
    block_lengths,
    w_query,
    w_key,
    w_value,
    w_out,
    w_gate,
    w_up,
    w_down,
    query_gain,
    key_gain,
    attn_gain,
    mlp_gain,
    cotangent,
):
    width = tokens.shape[1]
    columns = width // plan.size
    live, _ = row_layout(block_lengths)
    live_col = live.astype(f32)[:, None]
    lengths = lax.all_gather(block_lengths, plan.team)
    _, position = jax.vmap(row_layout)(lengths)
    cosine, sine = angles(position)
    gains = jnp.stack([query_gain, key_gain, attn_gain, mlp_gain])
    gains = lax.all_gather(gains, plan.every, axis=1, tiled=True).astype(f32)
    part_gains = lax.dynamic_slice_in_dim(gains[:2], plan.index * columns, columns, axis=1)
    attn_gain_wide, mlp_gain_wide = gains[2], gains[3]
    attn_whole = jnp.concatenate(
        [plan.gather_columns(w) for w in (w_query, w_key, w_value)], axis=1
    )
    out_whole = plan.gather_group(w_out)
    gate_whole = plan.gather_columns(w_gate)
    up_whole = plan.gather_columns(w_up)
    down_whole = plan.gather_group(w_down)

    team_tokens = plan.gather_rows(tokens)
    raw = product(team_tokens, attn_whole)
    inverse = lax.rsqrt(plan.sum_rows(norm_columns(raw, columns)) / width + epsilon)
    turned, mixed_low = attend(lengths, raw, inverse, part_gains, cosine, sine)
    attn_proj = plan.scatter_rows(product(mixed_low, out_whole).astype(bf16))
    attn_normed, attn_inverse = norm_forward(attn_proj, attn_gain_wide)
    hidden = tokens.astype(f32) + attn_normed
    team_hidden = plan.gather_rows(hidden.astype(bf16))
    gate = product(team_hidden, gate_whole)
    upward = product(team_hidden, up_whole)
    sigmoid_gate = jax.nn.sigmoid(gate)
    activated = gate * sigmoid_gate
    inner_low = (activated * upward).astype(bf16)
    down = plan.scatter_rows(product(inner_low, down_whole).astype(bf16))
    down_normed, down_inverse = norm_forward(down, mlp_gain_wide)
    block_out = (live_col * (hidden + down_normed)).astype(bf16)

    grad_out = live_col * cotangent.astype(f32)
    grad_down, term_mlp_gain = norm_back(down, down_inverse, mlp_gain_wide, grad_out)
    team_grad_down = plan.gather_rows(grad_down.astype(bf16))
    grad_w_down = plan.scatter_group(inner_rows(inner_low, team_grad_down).astype(bf16))
    grad_inner = product_tt(team_grad_down, down_whole)
    grad_gate = grad_inner * upward * sigmoid_gate * (1.0 + gate * (1.0 - sigmoid_gate))
    grad_up = grad_inner * activated
    grad_gate, grad_up = grad_gate.astype(bf16), grad_up.astype(bf16)
    grad_w_gate = plan.scatter_columns(inner_rows(team_hidden, grad_gate).astype(bf16))
    grad_w_up = plan.scatter_columns(inner_rows(team_hidden, grad_up).astype(bf16))
    grad_from_mlp = product_tt(grad_gate, gate_whole) + product_tt(grad_up, up_whole)
    grad_hidden = grad_out + plan.scatter_rows(grad_from_mlp.astype(bf16))

    grad_proj, term_attn_gain = norm_back(attn_proj, attn_inverse, attn_gain_wide, grad_hidden)
    team_grad_proj = plan.gather_rows(grad_proj.astype(bf16))
    grad_mixed = product_tt(team_grad_proj, out_whole).astype(bf16)
    grad_w_out = plan.scatter_group(inner_rows(mixed_low, team_grad_proj).astype(bf16))
    scaled, grad_value, means, part_terms = attend_back(
        lengths, raw, turned, inverse, part_gains, cosine, sine, grad_mixed
    )
    means = plan.sum_rows(means) / width
    grad_raw = raw_back(raw, scaled, inverse, means, grad_value)
    grad_w_query, grad_w_key, grad_w_value = (
        plan.scatter_columns(
            inner_rows(team_tokens, grad_raw[:, k * columns : (k + 1) * columns]).astype(bf16)
        )
        for k in range(3)
    )
    grad_from_attn = plan.scatter_rows(product_tt(grad_raw, attn_whole).astype(bf16))
    part_grads = plan.scatter_group(part_terms, 1)
    gain_grads = lax.psum_scatter(
        jnp.stack([term_attn_gain, term_mlp_gain]), plan.every, scatter_dimension=1, tiled=True
    )
    return (
        block_out,
        (grad_hidden + grad_from_attn).astype(bf16),
        grad_w_query,
        grad_w_key,
        grad_w_value,
        grad_w_out,
        grad_w_gate,
        grad_w_up,
        grad_w_down,
        part_grads[0],
        part_grads[1],
        gain_grads[0],
        gain_grads[1],
    )


def local_cube(
    tokens,
    block_lengths,
    w_query,
    w_key,
    w_value,
    w_out,
    w_gate,
    w_up,
    w_down,
    query_gain,
    key_gain,
    attn_gain,
    mlp_gain,
    cotangent,
):
    plan = Cube()
    width = tokens.shape[1]
    columns = width // plan.size
    live, _ = row_layout(block_lengths)
    live_col = live.astype(f32)[:, None]

    def group_whole(block):
        return lax.all_gather(block, plan.group, axis=0, tiled=True)

    shard = query_gain.shape[0]
    small = plan.small_rows((query_gain, key_gain, attn_gain, mlp_gain), block_lengths, width)
    packed = group_whole(jnp.concatenate([w_out, small])).reshape(8, -1, width)
    down1 = plan.shift(w_down)
    rows = plan.rows_first(plan.grouped(tokens))
    attn_parts = jnp.concatenate([plan.team_columns(w) for w in (w_query, w_key, w_value)], axis=2)
    attn0 = plan.send_columns(attn_parts)
    down1, attn0, w_gate, *rows = sync(down1, attn0, w_gate, *rows)
    attn1, attn0c = plan.shift(attn0), swap(attn0, "c")
    rows = plan.rows_second(*rows)
    attn1, attn0c, w_gate, *rows = sync(attn1, attn0c, w_gate, *rows)
    gate = plan.send_columns(plan.team_columns(w_gate))
    attn2, attn1c = plan.shift(attn1), swap(attn1, "c")
    team_tokens = join(*rows)
    attn2, attn1c, gate, w_up, team_tokens, packed = sync(
        attn2, attn1c, gate, w_up, team_tokens, packed
    )
    gate_whole = group_whole(gate)
    up = plan.send_columns(plan.team_columns(w_up))
    attn3, attn2c = plan.shift(attn2), swap(attn2, "c")
    out_whole = packed[:, : w_out.shape[0]].reshape(-1, width)
    small = packed[:, w_out.shape[0] : w_out.shape[0] + 5, :shard].transpose(1, 0, 2)
    small = plan.small_step(plan.small_step(small, "x"), "y")
    attn3, attn2c, small, out_whole, up = sync(attn3, attn2c, small, out_whole, up)
    up_whole = group_whole(up)
    gains, lengths = plan.small_end(small, block_lengths.shape[0])
    _, position = jax.vmap(row_layout)(lengths)
    cosine, sine = angles(position)
    part_gains = lax.dynamic_slice_in_dim(gains[:2], plan.index * columns, columns, axis=1)
    attn_gain_wide, mlp_gain_wide = gains[2], gains[3]
    attn3c = swap(attn3, "c")
    attn_whole = plan.join_group([[attn0, attn1, attn2, attn3], [attn0c, attn1c, attn2c, attn3c]])

    raw = product(team_tokens, attn_whole)
    inverse = lax.rsqrt(plan.sum_rows(norm_columns(raw, columns)) / width + epsilon)
    turned, mixed_low = attend(lengths, raw, inverse, part_gains, cosine, sine)
    attn_terms = product(mixed_low, out_whole).astype(bf16)
    attn_terms, down1, team_tokens = sync(attn_terms, down1, team_tokens)
    down2, down0c, down1c = plan.shift(down1), swap(w_down, "c"), swap(down1, "c")
    token_parts = plan.core_halves(team_tokens)
    terms = plan.terms_first(attn_terms)
    terms = plan.terms_second(*terms)
    attn_proj = plan.terms_sum(*terms)
    attn_normed, attn_inverse = norm_forward(attn_proj, attn_gain_wide)
    hidden = tokens.astype(f32) + attn_normed

    rows = plan.rows_first(plan.grouped(hidden.astype(bf16)))
    rows = plan.rows_second(*rows)
    down2, *rows = sync(down2, *rows)
    down3, down2c = plan.shift(down2), swap(down2, "c")
    team_hidden = join(*rows)
    gate = product(team_hidden, gate_whole)
    hidden_parts = plan.core_halves(team_hidden)
    gate, down3, *hidden_parts = sync(gate, down3, *hidden_parts)
    down3c = swap(down3, "c")
    upward = product(team_hidden, up_whole)
    down_whole = plan.join_group([[w_down, down1, down2, down3], [down0c, down1c, down2c, down3c]])
    sigmoid_gate = jax.nn.sigmoid(gate)
    activated = gate * sigmoid_gate
    inner_low = (activated * upward).astype(bf16)
    terms = plan.terms_first(product(inner_low, down_whole).astype(bf16))
    inner_parts = plan.core_halves(inner_low)
    down = plan.terms_sum(*plan.terms_second(*terms))
    down_normed, down_inverse = norm_forward(down, mlp_gain_wide)
    block_out = (live_col * (hidden + down_normed)).astype(bf16)

    grad_out = live_col * cotangent.astype(f32)
    grad_down, term_mlp_gain = norm_back(down, down_inverse, mlp_gain_wide, grad_out)
    rows = plan.rows_second(*plan.rows_first(grad_down.astype(bf16)))
    *inner_parts, mixed_other, mixed_mine = sync(*inner_parts, *plan.core_halves(mixed_low))
    team_grad_down = join(*rows)

    def terms_of(left, right):
        return inner_rows(left, right).astype(bf16)

    def summed(mine, other):
        return (mine.astype(f32) + other.astype(f32)).astype(bf16)

    down_other = swap(terms_of(inner_parts[0], team_grad_down), "c")
    down_mine = terms_of(inner_parts[1], team_grad_down)
    team_grad_down, down_mine = sync(team_grad_down, down_mine)
    grad_inner = product_tt(team_grad_down, down_whole)
    grad_gate = grad_inner * upward * sigmoid_gate * (1.0 + gate * (1.0 - sigmoid_gate))
    grad_up = grad_inner * activated
    grad_gate, grad_up, down_other, down_mine = sync(
        grad_gate.astype(bf16), grad_up.astype(bf16), down_other, down_mine
    )
    down_terms = summed(down_mine, down_other)
    grad_gate, grad_up, down_terms = sync(grad_gate, grad_up, down_terms)
    grad_w_down = lax.psum_scatter(down_terms, plan.z_axes, scatter_dimension=0, tiled=True)
    grad_from_mlp = product_tt(grad_gate, gate_whole) + product_tt(grad_up, up_whole)
    grad_from_mlp, grad_gate, grad_up, *hidden_parts = sync(
        grad_from_mlp.astype(bf16), grad_gate, grad_up, *hidden_parts
    )
    terms = plan.terms_first(grad_from_mlp)
    gate_other = swap(terms_of(hidden_parts[0], grad_gate), "c")
    gate_other, grad_gate, *terms = sync(gate_other, grad_gate, *terms)
    terms = plan.terms_second(*terms)
    gate_terms = summed(terms_of(hidden_parts[1], grad_gate), gate_other)
    gate_terms, grad_up, *terms = sync(gate_terms, grad_up, *terms)
    grad_hidden = grad_out + plan.ungrouped(plan.terms_sum(*terms))

    grad_proj, term_attn_gain = norm_back(attn_proj, attn_inverse, attn_gain_wide, grad_hidden)
    gate_sum = plan.shift(plan.ring_part(gate_terms, 1))
    rows = plan.rows_first(grad_proj.astype(bf16))
    up_other = swap(terms_of(hidden_parts[0], grad_up), "c")
    up_other, grad_up, grad_w_down, *rows = sync(up_other, grad_up, grad_w_down, *rows)
    rows = plan.rows_second(*rows)
    up_terms = summed(terms_of(hidden_parts[1], grad_up), up_other)
    up_terms, gate_sum, *rows = sync(up_terms, gate_sum, *rows)
    up_block = lax.psum_scatter(up_terms, plan.z_axes, scatter_dimension=0, tiled=True)
    gate_sum = plan.shift(summed(plan.ring_part(gate_terms, 2), gate_sum))
    team_grad_proj = join(*rows)
    grad_mixed = product_tt(team_grad_proj, out_whole).astype(bf16)
    scaled, grad_value, means, part_terms = attend_back(
        lengths, raw, turned, inverse, part_gains, cosine, sine, grad_mixed
    )
    gain_terms = jnp.stack([term_attn_gain, term_mlp_gain]).reshape(2, 2, 2, 2, 2, 2, -1)
    means, part_terms, gain_terms, gate_sum, team_grad_proj = sync(
        means, part_terms, gain_terms, gate_sum, team_grad_proj
    )
    gate_sum = plan.shift(summed(plan.ring_part(gate_terms, 3), gate_sum))
    out_other = swap(terms_of(mixed_other, team_grad_proj), "c")
    means = plan.sum_rows(means) / width
    means, out_other = sync(means, out_other)
    out_terms = summed(terms_of(mixed_mine, team_grad_proj), out_other)
    grad_raw = raw_back(raw, scaled, inverse, means, grad_value)
    attn_other = swap(terms_of(token_parts[0], grad_raw), "c")
    attn_mine = terms_of(token_parts[1], grad_raw)
    attn_mine, attn_other, grad_raw, out_terms, part_terms, gain_terms = sync(
        attn_mine, attn_other, grad_raw, out_terms, part_terms, gain_terms
    )
    attn_terms = summed(attn_mine, attn_other)
    attn_sum = plan.shift(plan.ring_part(attn_terms, 1))
    grad_from_attn = product_tt(grad_raw, attn_whole).astype(bf16)
    grad_from_attn, up_block = sync(grad_from_attn, up_block)
    terms = plan.terms_first(grad_from_attn)
    up_block = plan.return_columns(up_block)
    gain_terms = plan.gain_step(gain_terms, "c", 3)
    part_terms = part_terms + swap(part_terms, "c")
    attn_sum, gate_sum, part_terms, gain_terms, up_block, *terms = sync(
        attn_sum, gate_sum, part_terms, gain_terms, up_block, *terms
    )
    attn_sum = plan.shift(summed(plan.ring_part(attn_terms, 2), attn_sum))
    out_sum = plan.shift(plan.ring_part(out_terms, 1))
    terms = plan.terms_second(*terms)
    gate_block = plan.return_columns(summed(plan.ring_part(gate_terms, 0), gate_sum))
    attn_sum, out_sum, gate_block, part_terms, gain_terms, *terms = sync(
        attn_sum, out_sum, gate_block, part_terms, gain_terms, *terms
    )
    attn_sum = plan.shift(summed(plan.ring_part(attn_terms, 3), attn_sum))
    out_sum = plan.shift(summed(plan.ring_part(out_terms, 2), out_sum))
    grad_tokens = grad_hidden + plan.ungrouped(plan.terms_sum(*terms))
    gain_terms = plan.gain_step(plan.gain_step(gain_terms, "x", 2), "y", 1)
    part_terms = part_terms + swap(part_terms, "zh")
    grad_w_gate, grad_w_up = plan.whole_columns(gate_block), plan.whole_columns(up_block)
    attn_sum, out_sum, gain_terms, part_terms, grad_tokens, grad_w_gate, grad_w_up = sync(
        attn_sum, out_sum, gain_terms, part_terms, grad_tokens, grad_w_gate, grad_w_up
    )
    attn_block = plan.return_columns(summed(plan.ring_part(attn_terms, 0), attn_sum))
    out_sum = plan.shift(summed(plan.ring_part(out_terms, 3), out_sum))
    part_grads = plan.own_gains(part_terms + swap(part_terms, "zl"))
    gain_terms = plan.gain_step(plan.gain_step(gain_terms, "zh", 1), "zl", 1)
    attn_block, out_sum, part_grads, gain_terms = sync(attn_block, out_sum, part_grads, gain_terms)
    grad_w_out = plan.ring_part(out_terms, 0).astype(f32) + out_sum.astype(f32)
    grad_w_query, grad_w_key, grad_w_value = (
        plan.whole_columns(attn_block[..., k * columns : (k + 1) * columns]) for k in range(3)
    )
    return (
        block_out,
        grad_tokens.astype(bf16),
        grad_w_query,
        grad_w_key,
        grad_w_value,
        grad_w_out,
        grad_w_gate,
        grad_w_up,
        grad_w_down.astype(f32),
        part_grads[0],
        part_grads[1],
        gain_terms[0],
        gain_terms[1],
    )


def solution(mesh):
    if tuple(mesh.shape.values()) == (8, 4):
        mesh = Mesh(mesh.devices.reshape(2, 2, 2, 2, 2), Cube.every)
        every, step = Cube.every, local_cube
    else:
        every = tuple(mesh.axis_names)

        def step(*arrays):
            return local_plain(Plain(*every), *arrays)

    rows, line = P(every, None), P(every)
    return jax.shard_map(
        step,
        mesh=mesh,
        in_specs=(rows, line) + (rows,) * 7 + (line,) * 4 + (rows,),
        out_specs=(rows,) * 9 + (line,) * 4,
        check_vma=False,
    )
```

time: 1310 us -> 906 us (0.69)
  waiting for transfers between devices: 610 us -> 311 us
  local copies, waits for them, and re-layouts: 201 us -> 82 us
  blocking collectives: 81.3 us -> 0 us
  starting transfers between devices: 90.3 us -> 166 us
  Pallas kernels: 0 us -> 72.5 us
  other arithmetic: 123 us -> 89.3 us
  matrix products: 180 us -> 163 us
    ppermute x85 -> x67, waiting for transfers between devices: 502 us -> 215 us  [swap(): return lax.ppermute(value, axis, ((0, 1), (1, 0)))]
    unnamed x2 -> x5, waiting for transfers between devices: 108 us -> 0.09 us
    all_gather x1 -> x0, blocking collectives: 81.3 us -> none  [local(): lax.all_gather(jnp.stack([query_gain, key_gain, attn_gain, mlp_gain]), pl...]
    ppermute x2 -> x15, starting transfers between devices: 3.2 us -> 84 us  [shift(): return lax.ppermute(value, self.z_axes, ((0, 1), (1, 2), (2, 3), (3, 0)))]
    unnamed x248 -> x158, local copies, waits for them, and re-layouts: 106 us -> 28.3 us
    pallas_call x0 -> x17, Pallas kernels: none -> 72.5 us  [the longest x1 21.5 us: attend_back(): pl.pallas_call(attend_back_kernel, grid=(size,), in_specs=[whole, rows(3...]
    ppermute x2 -> x15, waiting for transfers between devices: 0.01 us -> 71.8 us  [shift(): return lax.ppermute(value, self.z_axes, ((0, 1), (1, 2), (2, 3), (3, 0)))]
    convert_element_type x32 -> x8, local copies, waits for them, and re-layouts: 36.8 us -> 5.27 us  [the longest x4 2.64 us: terms_second(): low[1].astype(bf16)]
  transfers between devices with their start and end apart: 92 -> 93, of which waited for: 38 -> 47; matrix products, arithmetic and copies ran while one was open for 30% -> 26% of each run, Pallas kernels for 0% -> 7%
where the time goes in v2:
time: 906 us; the launch traced here: 900 us
  waiting for transfers between devices  311 us (34%)
  starting transfers between devices  166 us (18%)
  matrix products  163 us (18%)
  other arithmetic  89.3 us (10%)
  local copies, waits for them, and re-layouts  82 us (9%)
  Pallas kernels  72.5 us (8%)
  between operations  15.6 us (2%)
    ppermute x67, waiting for transfers between devices, swap(): return lax.ppermute(value, axis, ((0, 1), (1, 0)))  215 us
    ppermute x15, starting transfers between devices, shift(): return lax.ppermute(value, self.z_axes, ((0, 1), (1, 2), (2, 3), (3, 0)))  84 us
    ppermute x15, waiting for transfers between devices, shift(): return lax.ppermute(value, self.z_axes, ((0, 1), (1, 2), (2, 3), (3, 0)))  71.8 us
    dot_general x5, matrix products, product_tt(): lax.dot_general(left, right, (((1,), (1,)), ((), ())), preferred_element_...  57.9 us
    ppermute x67, starting transfers between devices, swap(): return lax.ppermute(value, axis, ((0, 1), (1, 0)))  57.7 us
    dot_general x10, matrix products, inner_rows(): lax.dot_general(left, right, (((0,), (0,)), ((), ())), preferred_element_...  54.7 us
    dot_general x5, matrix products, product(): return jnp.dot(left, right, preferred_element_type=f32)  50.1 us
    convert_element_type x12, other arithmetic, summed(): return (mine.astype(f32) + other.astype(f32)).astype(bf16)  40.8 us
  transfers between devices with their start and end apart: 93, of which 47 were waited for; matrix products, arithmetic and copies ran while one was open for 26% of the time, Pallas kernels for 7%

profile of v2, /device:TPU:0, one launch (start us, length us, event | category | flops | bytes accessed | tf_op | source)
XLA Modules:
  0.0 899.5 jit_solution(16762354004120062660)
XLA Ops:
  29.4 14.8 %collective-permute-done.1.refs_2_ = bf16[128,2048]{1,0:T(8,128)(2,1)} collective-permute-done((bf16[128,2048]{1,0:T(8,128)(2,1)S(1)}, bf16[128,2048]{1,0:T(8,128)(2,1)}, u32[]{:S(2)}, u32[]{:S(2)}) %collective-permute-start.1) | collective-permute-done | bytes 524320 | tf_op jit(solution)/shard_map/ppermute | solution.py:198
  44.2 11.1 %collective-permute-done.refs_1_ = bf16[256,2048]{1,0:T(8,128)(2,1)S(1)} collective-permute-done((bf16[256,2048]{1,0:T(8,128)(2,1)}, bf16[256,2048]{1,0:T(8,128)(2,1)S(1)}, u32[]{:S(2)}, u32[]{:S(2)}) %collective-permute-start) | collective-permute-done | bytes 1048608 | tf_op jit(solution)/shard_map/ppermute | solution.py:295
  68.5 8.6 collective-permute-done.6.refs_4_
  77.9 10.1 %collective-permute-done.7.refs_6_ = bf16[128,2048]{1,0:T(8,128)(2,1)S(1)} collective-permute-done((bf16[128,2048]{1,0:T(8,128)(2,1)}, bf16[128,2048]{1,0:T(8,128)(2,1)S(1)}, u32[]{:S(2)}, u32[]{:S(2)}) %collective-permute-start.7) | collective-permute-done | bytes 524320 | tf_op jit(solution)/shard_map/ppermute | solution.py:198
  134.9 8.8 collective-permute-done.14
  143.7 10.3 %collective-permute-done.11.refs_3_ = bf16[256,1536]{1,0:T(8,128)(2,1)} collective-permute-done((bf16[256,1536]{1,0:T(8,128)(2,1)}, bf16[256,1536]{1,0:T(8,128)(2,1)}, u32[]{:S(2)}, u32[]{:S(2)}) %collective-permute-start.11) | collective-permute-done | bytes 786464 | tf_op jit(solution)/shard_map/ppermute | solution.py:295
  180.8 12.5 %shard_map.276 = (bf16[1024,1536]{1,0:T(8,128)(2,1)}, bf16[1024,512]{1,0:T(8,128)(2,1)}) custom-call(s32[4,2]{1,0:T(4,128)} %slice_convert_fusion.9.lengths_ref, f32[1024,1536]{1,0:T(8,128)} %copy-done.28, f32[1024,2]{1,0:T(8,128)} %bitcast.269, f32[2,512]{1,0:T(2,128)} %constant_dynamic-slice_fusion.18.gains_ref, f32[1024,128]{1,0:T(8,128)} %pad_maximum_fusion.6.cosine_ref, ...), custom_call_target="tpu_custom_call" | custom-call | tf_op jit(solution)/shard_map/pallas_call | solution.py:162
  198.4 22.9 %collective-permute-done.18 = bf16[2,128,2048]{2,1,0:T(8,128)(2,1)S(1)} collective-permute-done((bf16[2,128,2048]{2,1,0:T(8,128)(2,1)S(1)}, bf16[2,128,2048]{2,1,0:T(8,128)(2,1)S(1)}, u32[]{:S(2)}, u32[]{:S(2)}) %collective-permute-start.18) | collective-permute-done | bytes 1048608 | tf_op jit(solution)/shard_map/ppermute | solution.py:198
  227.2 7.9 collective-permute-start.22
  249.9 10.9 %collective-permute-done.23.refs_2_ = bf16[128,2048]{1,0:T(8,128)(2,1)} collective-permute-done((bf16[128,2048]{1,0:T(8,128)(2,1)S(1)}, bf16[128,2048]{1,0:T(8,128)(2,1)}, u32[]{:S(2)}, u32[]{:S(2)}) %collective-permute-start.23) | collective-permute-done | bytes 524320 | tf_op jit(solution)/shard_map/ppermute | solution.py:198
  262.8 21.3 %collective-permute-done.22.refs_2_ = bf16[256,2048]{1,0:T(8,128)(2,1)} collective-permute-done((bf16[256,2048]{1,0:T(8,128)(2,1)S(1)}, bf16[256,2048]{1,0:T(8,128)(2,1)}, u32[]{:S(2)}, u32[]{:S(2)}) %collective-permute-start.22) | collective-permute-done | bytes 1048608 | tf_op jit(solution)/shard_map/ppermute | solution.py:295
  284.6 25.2 %collective-permute-start.29 = (bf16[256,2048]{1,0:T(8,128)(2,1)}, bf16[256,2048]{1,0:T(8,128)(2,1)}, u32[]{:S(2)}, u32[]{:S(2)}) collective-permute-start(bf16[256,2048]{1,0:T(8,128)(2,1)} %collective-permute-done.22.refs_2_), channel_id=1, source_target_pairs={{0,1},{1,2},{2,3},{3,0},{4,5},{5,6},{6,7},{7,4},{8,9},{9,10},{10,1... | collective-permute-start | bytes 3145736 | tf_op jit(solution)/shard_map/ppermute | solution.py:295
  317.0 14.5 %fusion.52 = f32[1024,2048]{1,0:T(8,128)} fusion(bf16[1024,2048]{1,0:T(8,128)(2,1)} %copy-done, bf16[2048,2048]{1,0:T(8,128)(2,1)} %all-gather.6.cloned.1.call-done), kind=kOutput, calls=%fused_computation.220 | convolution fusion | flops 8589934592 | bytes 20971520 | tf_op jit(solution)/shard_map/dot_general | solution.py:21
  334.5 16.2 %multiply_convert_fusion.2 = (bf16[1024,2048]{1,0:T(8,128)(2,1)S(1)}, f32[1024,2048]{1,0:T(8,128)}) fusion(f32[1024,2048]{1,0:T(8,128)} %fusion.52, bf16[1024,2048]{1,0:T(8,128)(2,1)} %copy-done, bf16[2048,2048]{1,0:T(8,128)(2,1)} %all-gather.8.cloned.1.call-done), kind=kOutput, calls=%fused_computation.6 | convolution fusion | flops 8602517504 | bytes 33554432 | tf_op jit(solution)/shard_map/dot_general | solution.py:21
  354.9 9.2 %convolution_convert_fusion.1 = bf16[1024,2048]{1,0:T(8,128)(2,1)S(1)} fusion(bf16[1024,2048]{1,0:T(8,128)(2,1)S(1)} %get-tuple-element.365, bf16[2048,2048]{1,0:T(8,128)(2,1)S(1)} %shard_map.279), kind=kOutput, calls=%fused_computation.11 | convolution fusion | flops 8592031744 | bytes 16777216 | tf_op jit(solution)/shard_map/dot_general | solution.py:21
  367.4 22.6 %collective-permute-done.34 = bf16[2,128,2048]{2,1,0:T(8,128)(2,1)S(1)} collective-permute-done((bf16[2,128,2048]{2,1,0:T(8,128)(2,1)S(1)}, bf16[2,128,2048]{2,1,0:T(8,128)(2,1)S(1)}, u32[]{:S(2)}, u32[]{:S(2)}) %collective-permute-start.34) | collective-permute-done | bytes 1048608 | tf_op jit(solution)/shard_map/ppermute | solution.py:198
  397.1 10.5 %collective-permute-done.37 = bf16[128,2048]{1,0:T(8,128)(2,1)S(1)} collective-permute-done((bf16[128,2048]{1,0:T(8,128)(2,1)}, bf16[128,2048]{1,0:T(8,128)(2,1)S(1)}, u32[]{:S(2)}, u32[]{:S(2)}) %collective-permute-start.37) | collective-permute-done | bytes 524320 | tf_op jit(solution)/shard_map/ppermute | solution.py:198
  415.0 10.8 %collective-permute-done.38.refs_2_ = bf16[128,2048]{1,0:T(8,128)(2,1)S(1)} collective-permute-done((bf16[128,2048]{1,0:T(8,128)(2,1)S(1)}, bf16[128,2048]{1,0:T(8,128)(2,1)S(1)}, u32[]{:S(2)}, u32[]{:S(2)}) %collective-permute-start.38) | collective-permute-done | bytes 524320 | tf_op jit(solution)/shard_map/ppermute | solution.py:198
  438.6 8.4 collective-permute-done.42.refs_6_
  465.9 18.4 %multiply_convert_fusion = (bf16[1024,2048]{1,0:T(8,128)(2,1)}, bf16[1024,2048]{1,0:T(8,128)(2,1)}) fusion(f32[1024,2048]{1,0:T(8,128)} %fusion.52, f32[1024,2048]{1,0:T(8,128)} %get-tuple-element.366, bf16[1024,2048]{1,0:T(8,128)(2,1)S(1)} %shard_map.280, bf16[2048,2048]{1,0:T(8,128)(2,1)} %copy-done.1), kind=kOutput, calls=%fused_computation.4 | convolution fusion | flops 8617197568 | bytes 37748736 | tf_op jit(solution)/shard_map/dot_general | solution.py:25
  492.2 14.7 %fusion.53 = f32[1024,2048]{1,0:T(8,128)} fusion(bf16[1024,2048]{1,0:T(8,128)(2,1)} %get-tuple-element.229, bf16[2048,2048]{1,0:T(8,128)(2,1)} %all-gather.8.cloned.1.call-done), kind=kOutput, calls=%fused_computation.221 | convolution fusion | flops 8589934592 | bytes 20971520 | tf_op jit(solution)/shard_map/dot_general | solution.py:25
  506.9 13.2 %add_convert_fusion.2 = bf16[1024,2048]{1,0:T(8,128)(2,1)S(1)} fusion(f32[1024,2048]{1,0:T(8,128)} %fusion.53, bf16[1024,2048]{1,0:T(8,128)(2,1)S(1)} %copy-done.74, bf16[2048,2048]{1,0:T(8,128)(2,1)} %all-gather.6.cloned.1.call-done), kind=kOutput, calls=%fused_computation.2 | convolution fusion | flops 8594128896 | bytes 25165824 | tf_op jit(solution)/shard_map/dot_general | solution.py:25
  530.9 22.5 %collective-permute-done.46 = bf16[2,128,2048]{2,1,0:T(8,128)(2,1)S(1)} collective-permute-done((bf16[2,128,2048]{2,1,0:T(8,128)(2,1)}, bf16[2,128,2048]{2,1,0:T(8,128)(2,1)S(1)}, u32[]{:S(2)}, u32[]{:S(2)}) %collective-permute-start.46) | collective-permute-done | bytes 1048608 | tf_op jit(solution)/shard_map/ppermute | solution.py:198
  597.1 9.1 %collective-permute-done.51.refs_2_ = bf16[128,2048]{1,0:T(8,128)(2,1)S(1)} collective-permute-done((bf16[128,2048]{1,0:T(8,128)(2,1)S(1)}, bf16[128,2048]{1,0:T(8,128)(2,1)S(1)}, u32[]{:S(2)}, u32[]{:S(2)}) %collective-permute-start.51) | collective-permute-done | bytes 524320 | tf_op jit(solution)/shard_map/ppermute | solution.py:198
  638.0 9.6 %collective-permute-done.56.refs_6_ = bf16[128,2048]{1,0:T(8,128)(2,1)} collective-permute-done((bf16[128,2048]{1,0:T(8,128)(2,1)S(1)}, bf16[128,2048]{1,0:T(8,128)(2,1)}, u32[]{:S(2)}, u32[]{:S(2)}) %collective-permute-start.56) | collective-permute-done | bytes 524320 | tf_op jit(solution)/shard_map/ppermute | solution.py:198
  658.4 21.5 %shard_map.283 = (f32[1024,1024]{1,0:T(8,128)}, bf16[1024,512]{1,0:T(8,128)(2,1)}, f32[1024,2]{1,0:T(8,128)}, f32[2,512]{1,0:T(2,128)}) custom-call(s32[4,2]{1,0:T(4,128)} %slice_convert_fusion.9.lengths_ref, f32[1024,1536]{1,0:T(8,128)} %copy-done.28, bf16[1024,1536]{1,0:T(8,128)(2,1)} %get-tuple-element.199.turned_ref, f32[1024,2]{1,0:T(8,128)} %bitcast.270, ...), custom_call_target="tpu_custom_call" | custom-call | tf_op jit(solution)/shard_map/pallas_call | solution.py:179
  680.0 12.7 %collective-permute-done.58 = bf16[256,2048]{1,0:T(8,128)(2,1)} collective-permute-done((bf16[256,2048]{1,0:T(8,128)(2,1)}, bf16[256,2048]{1,0:T(8,128)(2,1)}, u32[]{:S(2)}, u32[]{:S(2)}) %collective-permute-start.58) | collective-permute-done | bytes 1048608 | tf_op jit(solution)/shard_map/ppermute | solution.py:295
  718.4 23.4 %collective-permute-start.64 = (bf16[256,2048]{1,0:T(8,128)(2,1)}, bf16[256,2048]{1,0:T(8,128)(2,1)}, u32[]{:S(2)}, u32[]{:S(2)}) collective-permute-start(bf16[256,2048]{1,0:T(8,128)(2,1)} %add_convert_fusion.6), channel_id=1, source_target_pairs={{0,1},{1,2},{2,3},{3,0},{4,5},{5,6},{6,7},{7,4},{8,9},{9,10},{10,1... | collective-permute-start | bytes 3145736 | tf_op jit(solution)/shard_map/ppermute | solution.py:295
  749.9 8.3 convolution_convert_fusion
  782.7 8.5 collective-permute-done.63
  791.2 10.3 %all-to-all-done.3.parts_ref = bf16[4,64,2048]{2,1,0:T(8,128)(2,1)} async-done(((bf16[4,64,2048]{2,1,0:T(8,128)(2,1)}), bf16[4,64,2048]{2,1,0:T(8,128)(2,1)}, u32[]{:S(2)}, u32[]{:S(2)}) %all-to-all-start.3) | async-done | bytes 1048608 | tf_op jit(solution)/shard_map/all_to_all | solution.py:341
  829.5 8.1 collective-permute-done.71
  (519 shorter events, 447.0 us)
Async XLA Ops:
  7.2 110.0 %all-gather.4.cloned.1.call-start = ((), (), s32[]{:S(2)}) async-start(), calls=%async_computation.8 | async-start | bytes 2949120 | tf_op jit(solution)/shard_map/all_gather | solution.py:578
  12.5 42.8 %collective-permute-start = (bf16[256,2048]{1,0:T(8,128)(2,1)}, bf16[256,2048]{1,0:T(8,128)(2,1)S(1)}, u32[]{:S(2)}, u32[]{:S(2)}) collective-permute-start(bf16[256,2048]{1,0:T(8,128)(2,1)} %refs_0_.1), channel_id=1, source_target_pairs={{0,1},{1,2},{2,3},{3,0},{4,5},{5,6},{6,7},{7,4},{8,9},{9,10},{10,1... | collective-permute-start | bytes 3145736 | tf_op jit(solution)/shard_map/ppermute | solution.py:295
  18.5 25.6 %all-to-all-start = ((bf16[4,64,1536]{2,1,0:T(8,128)(2,1)}), bf16[4,64,1536]{2,1,0:T(8,128)(2,1)S(1)}, u32[]{:S(2)}, u32[]{:S(2)}) async-start(bf16[4,64,1536]{2,1,0:T(8,128)(2,1)} %pad_maximum_fusion.5), calls=%async_computation | async-start | bytes 1572864 | tf_op jit(solution)/shard_map/all_to_all | solution.py:338
  57.0 32.6 %collective-permute-start.3 = (bf16[256,1536]{1,0:T(8,128)(2,1)S(1)}, bf16[256,1536]{1,0:T(8,128)(2,1)}, u32[]{:S(2)}, u32[]{:S(2)}) collective-permute-start(bf16[256,1536]{1,0:T(8,128)(2,1)S(1)} %bitcast.266), channel_id=1, source_target_pairs={{0,1},{1,2},{2,3},{3,0},{4,5},{5,6},{6,7},{7,4},{8,9},{9,10},{10,1... | collective-permute-start | bytes 2359304 | tf_op jit(solution)/shard_map/ppermute | solution.py:295
  62.4 27.2 %collective-permute-start.4 = (bf16[256,1536]{1,0:T(8,128)(2,1)S(1)}, bf16[256,1536]{1,0:T(8,128)(2,1)S(1)}, u32[]{:S(2)}, u32[]{:S(2)}) collective-permute-start(bf16[256,1536]{1,0:T(8,128)(2,1)S(1)} %bitcast.267), channel_id=1, source_target_pairs={{0,4},{4,0},{1,5},{5,1},{2,6},{6,2},{3,7},{7,3},{8,12},{12,8},{9,1... | collective-permute-start | bytes 2359304 | tf_op jit(solution)/shard_map/ppermute | solution.py:198
  102.5 214.5 %all-gather.6.cloned.1.call-start = ((), (), s32[]{:S(2)}) async-start(), calls=%async_computation.9 | async-start | bytes 9437184 | tf_op jit(solution)/shard_map/all_gather | solution.py:578
  119.4 34.6 %collective-permute-start.11 = (bf16[256,1536]{1,0:T(8,128)(2,1)}, bf16[256,1536]{1,0:T(8,128)(2,1)}, u32[]{:S(2)}, u32[]{:S(2)}) collective-permute-start(bf16[256,1536]{1,0:T(8,128)(2,1)} %collective-permute-done.9.refs_2_), channel_id=1, source_target_pairs={{0,1},{1,2},{2,3},{3,0},{4,5},{5,6},{6,7},{7,4},{8,9},{9,10},{10,1... | collective-permute-start | bytes 2359304 | tf_op jit(solution)/shard_map/ppermute | solution.py:295
  121.1 33.0 %collective-permute-start.12 = (bf16[256,1536]{1,0:T(8,128)(2,1)}, bf16[256,1536]{1,0:T(8,128)(2,1)}, u32[]{:S(2)}, u32[]{:S(2)}) collective-permute-start(bf16[256,1536]{1,0:T(8,128)(2,1)} %collective-permute-done.9.refs_2_), channel_id=1, source_target_pairs={{0,4},{4,0},{1,5},{5,1},{2,6},{6,2},{3,7},{7,3},{8,12},{12,8},{9,1... | collective-permute-start | bytes 2359304 | tf_op jit(solution)/shard_map/ppermute | solution.py:198
  124.5 29.5 %all-to-all-start.2 = ((bf16[4,64,2048]{2,1,0:T(8,128)(2,1)}), bf16[4,64,2048]{2,1,0:T(8,128)(2,1)}, u32[]{:S(2)}, u32[]{:S(2)}) async-start(bf16[4,64,2048]{2,1,0:T(8,128)(2,1)} %copy.171), calls=%async_computation.2 | async-start | bytes 2097152 | tf_op jit(solution)/shard_map/all_to_all | solution.py:338
  128.8 205.7 %all-gather.8.cloned.1.call-start = ((), (), s32[]{:S(2)}) async-start(), calls=%async_computation.10 | async-start | bytes 9437184 | tf_op jit(solution)/shard_map/all_gather | solution.py:578
  154.1 459.2 %reduce-scatter.3.cloned.1.call-start = ((), (), s32[]{:S(2)}) async-start(), calls=%async_computation.11 | async-start | bytes 5242880 | tf_op jit(solution)/shard_map/reduce_scatter | solution.py:669
  227.2 56.8 %collective-permute-start.22 = (bf16[256,2048]{1,0:T(8,128)(2,1)S(1)}, bf16[256,2048]{1,0:T(8,128)(2,1)}, u32[]{:S(2)}, u32[]{:S(2)}) collective-permute-start(bf16[256,2048]{1,0:T(8,128)(2,1)S(1)} %collective-permute-done.refs_1_), channel_id=1, source_target_pairs={{0,1},{1,2},{2,3},{3,0},{4,5},{5,6},{6,7},{7,4},{8,9},{9,10},{10,1... | collective-permute-start | bytes 3145736 | tf_op jit(solution)/shard_map/ppermute | solution.py:295
  247.7 36.4 %collective-permute-start.24 = (bf16[128,2048]{1,0:T(8,128)(2,1)S(1)}, bf16[128,2048]{1,0:T(8,128)(2,1)}, u32[]{:S(2)}, u32[]{:S(2)}) collective-permute-start(bf16[128,2048]{1,0:T(8,128)(2,1)S(1)} %get-tuple-element.186.refs_1_), channel_id=1, source_target_pairs={{0,8},{8,0},{1,9},{9,1},{2,10},{10,2},{3,11},{11,3},{4,12},{12,4},... | collective-permute-start | bytes 1572872 | tf_op jit(solution)/shard_map/ppermute | solution.py:198
  249.1 35.4 %collective-permute-start.25 = (bf16[128,2048]{1,0:T(8,128)(2,1)S(1)}, bf16[128,2048]{1,0:T(8,128)(2,1)}, u32[]{:S(2)}, u32[]{:S(2)}) collective-permute-start(bf16[128,2048]{1,0:T(8,128)(2,1)S(1)} %get-tuple-element.185.refs_0_), channel_id=1, source_target_pairs={{0,16},{16,0},{1,17},{17,1},{2,18},{18,2},{3,19},{19,3},{4,20},{20... | collective-permute-start | bytes 1572872 | tf_op jit(solution)/shard_map/ppermute | solution.py:198
  284.1 66.6 %collective-permute-start.30 = (bf16[256,2048]{1,0:T(8,128)(2,1)S(1)}, bf16[256,2048]{1,0:T(8,128)(2,1)}, u32[]{:S(2)}, u32[]{:S(2)}) collective-permute-start(bf16[256,2048]{1,0:T(8,128)(2,1)S(1)} %copy-done.11), channel_id=1, source_target_pairs={{0,4},{4,0},{1,5},{5,1},{2,6},{6,2},{3,7},{7,3},{8,12},{12,8},{9,1... | collective-permute-start | bytes 3145736 | tf_op jit(solution)/shard_map/ppermute | solution.py:198
  284.1 66.6 %collective-permute-start.31 = (bf16[256,2048]{1,0:T(8,128)(2,1)S(1)}, bf16[256,2048]{1,0:T(8,128)(2,1)}, u32[]{:S(2)}, u32[]{:S(2)}) collective-permute-start(bf16[256,2048]{1,0:T(8,128)(2,1)S(1)} %collective-permute-done.refs_1_), channel_id=1, source_target_pairs={{0,4},{4,0},{1,5},{5,1},{2,6},{6,2},{3,7},{7,3},{8,12},{12,8},{9,1... | collective-permute-start | bytes 3145736 | tf_op jit(solution)/shard_map/ppermute | solution.py:198
  284.6 49.9 %collective-permute-start.29 = (bf16[256,2048]{1,0:T(8,128)(2,1)}, bf16[256,2048]{1,0:T(8,128)(2,1)}, u32[]{:S(2)}, u32[]{:S(2)}) collective-permute-start(bf16[256,2048]{1,0:T(8,128)(2,1)} %collective-permute-done.22.refs_2_), channel_id=1, source_target_pairs={{0,1},{1,2},{2,3},{3,0},{4,5},{5,6},{6,7},{7,4},{8,9},{9,10},{10,1... | collective-permute-start | bytes 3145736 | tf_op jit(solution)/shard_map/ppermute | solution.py:295
  309.8 40.9 %collective-permute-start.32 = (bf16[256,2048]{1,0:T(8,128)(2,1)}, bf16[256,2048]{1,0:T(8,128)(2,1)}, u32[]{:S(2)}, u32[]{:S(2)}) collective-permute-start(bf16[256,2048]{1,0:T(8,128)(2,1)} %collective-permute-done.22.refs_2_), channel_id=1, source_target_pairs={{0,4},{4,0},{1,5},{5,1},{2,6},{6,2},{3,7},{7,3},{8,12},{12,8},{9,1... | collective-permute-start | bytes 3145736 | tf_op jit(solution)/shard_map/ppermute | solution.py:198
  526.5 28.9 %collective-permute-start.45 = (bf16[1024,2048]{1,0:T(8,128)(2,1)}, bf16[1024,2048]{1,0:T(8,128)(2,1)}, u32[]{:S(2)}, u32[]{:S(2)}) collective-permute-start(bf16[1024,2048]{1,0:T(8,128)(2,1)} %convolution_convert_fusion.6), channel_id=1, source_target_pairs={{0,4},{4,0},{1,5},{5,1},{2,6},{6,2},{3,7},{7,3},{8,12},{12,8},{9,1... | collective-permute-start | bytes 12582920 | tf_op jit(solution)/shard_map/ppermute | solution.py:198
  530.9 227.3 %reduce-scatter.5.cloned.1.call-start = ((), (), s32[]{:S(2)}) async-start(), calls=%async_computation.12 | async-start | bytes 5242880 | tf_op jit(solution)/shard_map/reduce_scatter | solution.py:690
  579.5 33.8 %collective-permute-start.50 = (bf16[1024,2048]{1,0:T(8,128)(2,1)}, bf16[1024,2048]{1,0:T(8,128)(2,1)}, u32[]{:S(2)}, u32[]{:S(2)}) collective-permute-start(bf16[1024,2048]{1,0:T(8,128)(2,1)} %convolution_convert_fusion.5), channel_id=1, source_target_pairs={{0,4},{4,0},{1,5},{5,1},{2,6},{6,2},{3,7},{7,3},{8,12},{12,8},{9,1... | collective-permute-start | bytes 12582920 | tf_op jit(solution)/shard_map/ppermute | solution.py:198
  596.0 35.4 %collective-permute-start.53 = (bf16[256,2048]{1,0:T(8,128)(2,1)}, bf16[256,2048]{1,0:T(8,128)(2,1)}, u32[]{:S(2)}, u32[]{:S(2)}) collective-permute-start(bf16[256,2048]{1,0:T(8,128)(2,1)} %constant_dynamic-slice_fusion.11), channel_id=1, source_target_pairs={{0,1},{1,2},{2,3},{3,0},{4,5},{5,6},{6,7},{7,4},{8,9},{9,10},{10,1... | collective-permute-start | bytes 3145736 | tf_op jit(solution)/shard_map/ppermute | solution.py:295
  650.5 42.2 %collective-permute-start.58 = (bf16[256,2048]{1,0:T(8,128)(2,1)}, bf16[256,2048]{1,0:T(8,128)(2,1)}, u32[]{:S(2)}, u32[]{:S(2)}) collective-permute-start(bf16[256,2048]{1,0:T(8,128)(2,1)} %add_convert_fusion.7), channel_id=1, source_target_pairs={{0,1},{1,2},{2,3},{3,0},{4,5},{5,6},{6,7},{7,4},{8,9},{9,10},{10,1... | collective-permute-start | bytes 3145736 | tf_op jit(solution)/shard_map/ppermute | solution.py:295
  715.5 34.3 %collective-permute-start.62 = (bf16[1024,1536]{1,0:T(8,128)(2,1)}, bf16[1024,1536]{1,0:T(8,128)(2,1)}, u32[]{:S(2)}, u32[]{:S(2)}) collective-permute-start(bf16[1024,1536]{1,0:T(8,128)(2,1)} %convolution_convert_fusion.3), channel_id=1, source_target_pairs={{0,4},{4,0},{1,5},{5,1},{2,6},{6,2},{3,7},{7,3},{8,12},{12,8},{9,1... | collective-permute-start | bytes 9437192 | tf_op jit(solution)/shard_map/ppermute | solution.py:198
  718.4 64.3 %collective-permute-start.64 = (bf16[256,2048]{1,0:T(8,128)(2,1)}, bf16[256,2048]{1,0:T(8,128)(2,1)}, u32[]{:S(2)}, u32[]{:S(2)}) collective-permute-start(bf16[256,2048]{1,0:T(8,128)(2,1)} %add_convert_fusion.6), channel_id=1, source_target_pairs={{0,1},{1,2},{2,3},{3,0},{4,5},{5,6},{6,7},{7,4},{8,9},{9,10},{10,1... | collective-permute-start | bytes 3145736 | tf_op jit(solution)/shard_map/ppermute | solution.py:295
  762.9 38.7 %collective-permute-start.67 = (bf16[2,128,2048]{2,1,0:T(8,128)(2,1)}, bf16[2,128,2048]{2,1,0:T(8,128)(2,1)}, u32[]{:S(2)}, u32[]{:S(2)}) collective-permute-start(bf16[2,128,2048]{2,1,0:T(8,128)(2,1)} %get-tuple-element.311), channel_id=1, source_target_pairs={{0,16},{16,0},{1,17},{17,1},{2,18},{18,2},{3,19},{19,3},{4,20},{20... | collective-permute-start | bytes 3145736 | tf_op jit(solution)/shard_map/ppermute | solution.py:198
  764.9 36.6 %collective-permute-start.68 = (bf16[2,128,2048]{2,1,0:T(8,128)(2,1)}, bf16[2,128,2048]{2,1,0:T(8,128)(2,1)}, u32[]{:S(2)}, u32[]{:S(2)}) collective-permute-start(bf16[2,128,2048]{2,1,0:T(8,128)(2,1)} %get-tuple-element.309), channel_id=1, source_target_pairs={{0,8},{8,0},{1,9},{9,1},{2,10},{10,2},{3,11},{11,3},{4,12},{12,4},... | collective-permute-start | bytes 3145736 | tf_op jit(solution)/shard_map/ppermute | solution.py:198
  771.1 30.5 %all-to-all-start.3 = ((bf16[4,64,2048]{2,1,0:T(8,128)(2,1)}), bf16[4,64,2048]{2,1,0:T(8,128)(2,1)}, u32[]{:S(2)}, u32[]{:S(2)}) async-start(bf16[4,64,2048]{2,1,0:T(8,128)(2,1)} %bitcast.290), calls=%async_computation.5 | async-start | bytes 2097152 | tf_op jit(solution)/shard_map/all_to_all | solution.py:341
  780.5 48.9 %collective-permute-start.70 = (bf16[64,2048]{1,0:T(8,128)(2,1)S(1)}, bf16[64,2048]{1,0:T(8,128)(2,1)}, u32[]{:S(2)}, u32[]{:S(2)}) collective-permute-start(bf16[64,2048]{1,0:T(8,128)(2,1)S(1)} %constant_dynamic-slice_fusion.9), channel_id=1, source_target_pairs={{0,1},{1,2},{2,3},{3,0},{4,5},{5,6},{6,7},{7,4},{8,9},{9,10},{10,1... | collective-permute-start | bytes 786440 | tf_op jit(solution)/shard_map/ppermute | solution.py:295
  803.8 33.8 %collective-permute-start.69 = (bf16[256,1536]{1,0:T(8,128)(2,1)}, bf16[256,1536]{1,0:T(8,128)(2,1)}, u32[]{:S(2)}, u32[]{:S(2)}) collective-permute-start(bf16[256,1536]{1,0:T(8,128)(2,1)} %add_convert_fusion.10), channel_id=1, source_target_pairs={{0,1},{1,2},{2,3},{3,0},{4,5},{5,6},{6,7},{7,4},{8,9},{9,10},{10,1... | collective-permute-start | bytes 2359304 | tf_op jit(solution)/shard_map/ppermute | solution.py:295
  809.1 28.5 %all-to-all-start.4 = ((bf16[4,64,2048]{2,1,0:T(8,128)(2,1)}), bf16[4,64,2048]{2,1,0:T(8,128)(2,1)}, u32[]{:S(2)}, u32[]{:S(2)}) async-start(bf16[4,64,2048]{2,1,0:T(8,128)(2,1)} %bitcast.276), calls=%async_computation.6 | async-start | bytes 2097152 | tf_op jit(solution)/shard_map/all_to_all | solution.py:341
  840.0 26.2 %collective-permute-start.73 = (bf16[256,1536]{1,0:T(8,128)(2,1)}, bf16[256,1536]{1,0:T(8,128)(2,1)}, u32[]{:S(2)}, u32[]{:S(2)}) collective-permute-start(bf16[256,1536]{1,0:T(8,128)(2,1)} %add_convert_fusion.9), channel_id=1, source_target_pairs={{0,1},{1,2},{2,3},{3,0},{4,5},{5,6},{6,7},{7,4},{8,9},{9,10},{10,1... | collective-permute-start | bytes 2359304 | tf_op jit(solution)/shard_map/ppermute | solution.py:295
  (139 other events, 1529.6 us)
Sparse Core Ops, SparseCore 0:
  12.6 51.5 all-gather.3
  117.3 92.5 all-gather.5
  211.5 102.0 all-gather.7
  531.0 82.2 reduce-scatter.2
  653.0 95.6 reduce-scatter.4

commit v3 on v2

--- a/solution.py
+++ b/solution.py
@@ -316,12 +316,14 @@
     def terms_sum(self, top, low, top_x, low_y):
         return jnp.concatenate([top + top_x.astype(f32), low + low_y.astype(f32)])
 
-    def sum_rows(self, rows):
+    def sum_along(self, rows, axis):
         shape = rows.shape
         rows = rows.reshape((2, 2, -1) + shape[1:])
-        for dim, axis in enumerate(self.team):
-            rows = rows + jnp.flip(swap(rows, axis), dim)
+        rows = rows + jnp.flip(swap(rows, axis), self.team.index(axis))
         return rows.reshape(shape)
+
+    def sum_rows(self, rows):
+        return self.sum_along(self.sum_along(rows, "y"), "x")
 
     def order(self, mine, other, index, axis):
         first = index == 0
@@ -362,9 +364,22 @@
             for index in (1 - self.core, self.core)
         ]
 
-    def ring_part(self, terms, k):
-        rows = terms.shape[0] // 4
-        return lax.dynamic_slice_in_dim(terms, (self.z - k) % 4 * rows, rows, 0)
+    def ring_sum(self, k, terms, so_far=None):
+        rows = terms[0].shape[0] // 4
+        part = (self.z - k) % 4
+
+        def pick_rows(term):
+            if isinstance(term, tuple):
+                begin = part % 2 * rows
+                low, high = (lax.dynamic_slice_in_dim(half, begin, rows, 0) for half in term)
+                return jnp.where(part < 2, low, high)
+            return lax.dynamic_slice_in_dim(term, part * rows, rows, 0)
+
+        parts = [pick_rows(term).astype(f32) for term in terms]
+        return sum(parts if so_far is None else parts + [so_far.astype(f32)])
+
+    def ring_step(self, k, terms, so_far=None):
+        return self.shift(self.ring_sum(k, terms, so_far).astype(bf16))
 
     def small_rows(self, gains, lengths, width):
         small = [jnp.pad(row.astype(bf16), (0, width - row.shape[0])) for row in (*gains, lengths)]
@@ -579,15 +594,16 @@
 
     shard = query_gain.shape[0]
     small = plan.small_rows((query_gain, key_gain, attn_gain, mlp_gain), block_lengths, width)
-    packed = group_whole(jnp.concatenate([w_out, small])).reshape(8, -1, width)
-    down1 = plan.shift(w_down)
-    rows = plan.rows_first(plan.grouped(tokens))
     attn_parts = jnp.concatenate([plan.team_columns(w) for w in (w_query, w_key, w_value)], axis=2)
+    attn_parts, own, out_rows, down0 = sync(attn_parts, tokens, w_out, w_down)
+    packed = group_whole(jnp.concatenate([out_rows, small])).reshape(8, -1, width)
+    down1 = plan.shift(down0)
+    rows = plan.rows_first(plan.grouped(own))
     attn0 = plan.send_columns(attn_parts)
-    down1, attn0, w_gate, *rows = sync(down1, attn0, w_gate, *rows)
+    attn0, w_gate, *rows = sync(attn0, w_gate, *rows)
     attn1, attn0c = plan.shift(attn0), swap(attn0, "c")
     rows = plan.rows_second(*rows)
-    attn1, attn0c, w_gate, *rows = sync(attn1, attn0c, w_gate, *rows)
+    attn1, attn0c, down1, w_gate, *rows = sync(attn1, attn0c, down1, w_gate, *rows)
     gate = plan.send_columns(plan.team_columns(w_gate))
     attn2, attn1c = plan.shift(attn1), swap(attn1, "c")
     team_tokens = join(*rows)
@@ -616,7 +632,6 @@
     attn_terms = product(mixed_low, out_whole).astype(bf16)
     attn_terms, down1, team_tokens = sync(attn_terms, down1, team_tokens)
     down2, down0c, down1c = plan.shift(down1), swap(w_down, "c"), swap(down1, "c")
-    token_parts = plan.core_halves(team_tokens)
     terms = plan.terms_first(attn_terms)
     terms = plan.terms_second(*terms)
     attn_proj = plan.terms_sum(*terms)
@@ -625,28 +640,27 @@
 
     rows = plan.rows_first(plan.grouped(hidden.astype(bf16)))
     rows = plan.rows_second(*rows)
-    down2, *rows = sync(down2, *rows)
-    down3, down2c = plan.shift(down2), swap(down2, "c")
     team_hidden = join(*rows)
     gate = product(team_hidden, gate_whole)
     hidden_parts = plan.core_halves(team_hidden)
-    gate, down3, *hidden_parts = sync(gate, down3, *hidden_parts)
+    gate, down2, *hidden_parts = sync(gate, down2, *hidden_parts)
+    down3, down2c = plan.shift(down2), swap(down2, "c")
+    upward = product(team_hidden, up_whole)
+    upward, down3 = sync(upward, down3)
     down3c = swap(down3, "c")
-    upward = product(team_hidden, up_whole)
     down_whole = plan.join_group([[w_down, down1, down2, down3], [down0c, down1c, down2c, down3c]])
     sigmoid_gate = jax.nn.sigmoid(gate)
     activated = gate * sigmoid_gate
     inner_low = (activated * upward).astype(bf16)
     terms = plan.terms_first(product(inner_low, down_whole).astype(bf16))
-    inner_parts = plan.core_halves(inner_low)
-    down = plan.terms_sum(*plan.terms_second(*terms))
+    *inner_parts, top, low, top_y, low_x = sync(*plan.core_halves(inner_low), *terms)
+    down = plan.terms_sum(*plan.terms_second(top, low, top_y, low_x))
     down_normed, down_inverse = norm_forward(down, mlp_gain_wide)
     block_out = (live_col * (hidden + down_normed)).astype(bf16)
 
     grad_out = live_col * cotangent.astype(f32)
     grad_down, term_mlp_gain = norm_back(down, down_inverse, mlp_gain_wide, grad_out)
     rows = plan.rows_second(*plan.rows_first(grad_down.astype(bf16)))
-    *inner_parts, mixed_other, mixed_mine = sync(*inner_parts, *plan.core_halves(mixed_low))
     team_grad_down = join(*rows)
 
     def terms_of(left, right):
@@ -657,91 +671,105 @@
 
     down_other = swap(terms_of(inner_parts[0], team_grad_down), "c")
     down_mine = terms_of(inner_parts[1], team_grad_down)
-    team_grad_down, down_mine = sync(team_grad_down, down_mine)
+    team_grad_down, down_mine, down_other = sync(team_grad_down, down_mine, down_other)
+    down_terms = summed(down_mine, down_other)
+    gain_shape = (2, 2, 2, 2, 2, -1)
+    team_grad_down, down_terms, mlp_terms = sync(team_grad_down, down_terms, term_mlp_gain)
+    mlp_terms = plan.gain_step(mlp_terms.reshape(gain_shape), "c", 2)
+    team_grad_down, mlp_terms = sync(team_grad_down, mlp_terms)
+    grad_w_down = lax.psum_scatter(down_terms, plan.z_axes, scatter_dimension=0, tiled=True)
     grad_inner = product_tt(team_grad_down, down_whole)
     grad_gate = grad_inner * upward * sigmoid_gate * (1.0 + gate * (1.0 - sigmoid_gate))
     grad_up = grad_inner * activated
-    grad_gate, grad_up, down_other, down_mine = sync(
-        grad_gate.astype(bf16), grad_up.astype(bf16), down_other, down_mine
-    )
-    down_terms = summed(down_mine, down_other)
-    grad_gate, grad_up, down_terms = sync(grad_gate, grad_up, down_terms)
-    grad_w_down = lax.psum_scatter(down_terms, plan.z_axes, scatter_dimension=0, tiled=True)
+    grad_gate, grad_up, *hidden_parts = sync(
+        grad_gate.astype(bf16), grad_up.astype(bf16), *hidden_parts
+    )
+    gate_away = terms_of(hidden_parts[0], grad_gate)
+    gate_away, grad_up, other_part = sync(gate_away, grad_up, hidden_parts[0])
+    gate_other = swap(gate_away, "c")
+    up_away = terms_of(other_part, grad_up)
+    up_away, grad_gate, grad_up = sync(up_away, grad_gate, grad_up)
+    up_other = swap(up_away, "c")
     grad_from_mlp = product_tt(grad_gate, gate_whole) + product_tt(grad_up, up_whole)
-    grad_from_mlp, grad_gate, grad_up, *hidden_parts = sync(
-        grad_from_mlp.astype(bf16), grad_gate, grad_up, *hidden_parts
+    grad_from_mlp, grad_gate, grad_up, hidden_part = sync(
+        grad_from_mlp.astype(bf16), grad_gate, grad_up, hidden_parts[1]
     )
     terms = plan.terms_first(grad_from_mlp)
-    gate_other = swap(terms_of(hidden_parts[0], grad_gate), "c")
-    gate_other, grad_gate, *terms = sync(gate_other, grad_gate, *terms)
+    gate_terms = summed(terms_of(hidden_part, grad_gate), gate_other)
+    gate_terms, grad_up, *terms = sync(gate_terms, grad_up, *terms)
+    gate_block = lax.psum_scatter(gate_terms, plan.z_axes, scatter_dimension=0, tiled=True)
     terms = plan.terms_second(*terms)
-    gate_terms = summed(terms_of(hidden_parts[1], grad_gate), gate_other)
-    gate_terms, grad_up, *terms = sync(gate_terms, grad_up, *terms)
+    late_parts = (*plan.core_halves(team_tokens), *plan.core_halves(mixed_low))
+    token_other, token_mine, mixed_other, mixed_mine, grad_up, *terms = sync(
+        *late_parts, grad_up, *terms
+    )
     grad_hidden = grad_out + plan.ungrouped(plan.terms_sum(*terms))
 
     grad_proj, term_attn_gain = norm_back(attn_proj, attn_inverse, attn_gain_wide, grad_hidden)
-    gate_sum = plan.shift(plan.ring_part(gate_terms, 1))
     rows = plan.rows_first(grad_proj.astype(bf16))
-    up_other = swap(terms_of(hidden_parts[0], grad_up), "c")
-    up_other, grad_up, grad_w_down, *rows = sync(up_other, grad_up, grad_w_down, *rows)
+    up_mine = terms_of(hidden_part, grad_up)
+    up_mine, up_other, grad_w_down, *rows = sync(up_mine, up_other, grad_w_down, *rows)
     rows = plan.rows_second(*rows)
-    up_terms = summed(terms_of(hidden_parts[1], grad_up), up_other)
-    up_terms, gate_sum, *rows = sync(up_terms, gate_sum, *rows)
+    up_terms = summed(up_mine, up_other)
+    up_terms, gate_block, *rows = sync(up_terms, gate_block, *rows)
     up_block = lax.psum_scatter(up_terms, plan.z_axes, scatter_dimension=0, tiled=True)
-    gate_sum = plan.shift(summed(plan.ring_part(gate_terms, 2), gate_sum))
     team_grad_proj = join(*rows)
     grad_mixed = product_tt(team_grad_proj, out_whole).astype(bf16)
     scaled, grad_value, means, part_terms = attend_back(
         lengths, raw, turned, inverse, part_gains, cosine, sine, grad_mixed
     )
-    gain_terms = jnp.stack([term_attn_gain, term_mlp_gain]).reshape(2, 2, 2, 2, 2, 2, -1)
-    means, part_terms, gain_terms, gate_sum, team_grad_proj = sync(
-        means, part_terms, gain_terms, gate_sum, team_grad_proj
-    )
-    gate_sum = plan.shift(summed(plan.ring_part(gate_terms, 3), gate_sum))
-    out_other = swap(terms_of(mixed_other, team_grad_proj), "c")
-    means = plan.sum_rows(means) / width
-    means, out_other = sync(means, out_other)
-    out_terms = summed(terms_of(mixed_mine, team_grad_proj), out_other)
+    attn_gain_terms = plan.gain_step(term_attn_gain.reshape(gain_shape), "c", 2)
+    gain_terms = jnp.stack([attn_gain_terms, mlp_terms])
+    gate_block = plan.return_columns(gate_block)
+    means, part_terms, gain_terms, team_grad_proj, gate_block = sync(
+        means, part_terms, gain_terms, team_grad_proj, gate_block
+    )
+    out_away = terms_of(mixed_other, team_grad_proj)
+    means = plan.sum_along(means, "y")
+    means, out_away, team_grad_proj = sync(means, out_away, team_grad_proj)
+    out_mine = terms_of(mixed_mine, team_grad_proj)
+    means = plan.sum_along(means, "x") / width
+    means, out_mine = sync(means, out_mine)
     grad_raw = raw_back(raw, scaled, inverse, means, grad_value)
-    attn_other = swap(terms_of(token_parts[0], grad_raw), "c")
-    attn_mine = terms_of(token_parts[1], grad_raw)
-    attn_mine, attn_other, grad_raw, out_terms, part_terms, gain_terms = sync(
-        attn_mine, attn_other, grad_raw, out_terms, part_terms, gain_terms
-    )
-    attn_terms = summed(attn_mine, attn_other)
-    attn_sum = plan.shift(plan.ring_part(attn_terms, 1))
+    half = token_other.shape[1] // 2
+    attn_other = [swap(terms_of(token_other[:, :half], grad_raw), "c")]
+    attn_other += [swap(terms_of(token_other[:, half:], grad_raw), "c")]
+    out_other = swap(out_away, "c")
+    attn_mine = terms_of(token_mine, grad_raw)
     grad_from_attn = product_tt(grad_raw, attn_whole).astype(bf16)
-    grad_from_attn, up_block = sync(grad_from_attn, up_block)
+    grad_from_attn, attn_mine, part_terms, gain_terms, *attn_other = sync(
+        grad_from_attn, attn_mine, part_terms, gain_terms, *attn_other
+    )
+    attn_terms = (attn_mine, tuple(attn_other))
+    attn_sum = plan.ring_step(1, attn_terms)
     terms = plan.terms_first(grad_from_attn)
+    part_terms = part_terms + swap(part_terms, "c")
+    attn_sum, out_other, part_terms, *terms = sync(attn_sum, out_other, part_terms, *terms)
+    out_terms = (out_mine, out_other)
+    attn_sum = plan.ring_step(2, attn_terms, attn_sum)
+    out_sum = plan.ring_step(1, out_terms)
+    gain_terms = plan.gain_step(gain_terms, "zh", 3)
+    part_terms = part_terms + swap(part_terms, "zh")
+    terms = plan.terms_second(*terms)
+    grad_w_gate = plan.whole_columns(gate_block)
+    attn_sum, out_sum, gain_terms, part_terms, up_block, grad_w_gate, *terms = sync(
+        attn_sum, out_sum, gain_terms, part_terms, up_block, grad_w_gate, *terms
+    )
+    attn_sum = plan.ring_step(3, attn_terms, attn_sum)
+    out_sum = plan.ring_step(2, out_terms, out_sum)
     up_block = plan.return_columns(up_block)
-    gain_terms = plan.gain_step(gain_terms, "c", 3)
-    part_terms = part_terms + swap(part_terms, "c")
-    attn_sum, gate_sum, part_terms, gain_terms, up_block, *terms = sync(
-        attn_sum, gate_sum, part_terms, gain_terms, up_block, *terms
-    )
-    attn_sum = plan.shift(summed(plan.ring_part(attn_terms, 2), attn_sum))
-    out_sum = plan.shift(plan.ring_part(out_terms, 1))
-    terms = plan.terms_second(*terms)
-    gate_block = plan.return_columns(summed(plan.ring_part(gate_terms, 0), gate_sum))
-    attn_sum, out_sum, gate_block, part_terms, gain_terms, *terms = sync(
-        attn_sum, out_sum, gate_block, part_terms, gain_terms, *terms
-    )
-    attn_sum = plan.shift(summed(plan.ring_part(attn_terms, 3), attn_sum))
-    out_sum = plan.shift(summed(plan.ring_part(out_terms, 2), out_sum))
     grad_tokens = grad_hidden + plan.ungrouped(plan.terms_sum(*terms))
+    gain_terms = plan.gain_step(gain_terms, "zl", 3)
+    part_grads = plan.own_gains(part_terms + swap(part_terms, "zl"))
+    attn_sum, out_sum, up_block, gain_terms, part_grads, grad_tokens = sync(
+        attn_sum, out_sum, up_block, gain_terms, part_grads, grad_tokens
+    )
+    attn_block = plan.return_columns(plan.ring_sum(0, attn_terms, attn_sum).astype(bf16))
+    out_sum = plan.ring_step(3, out_terms, out_sum)
     gain_terms = plan.gain_step(plan.gain_step(gain_terms, "x", 2), "y", 1)
-    part_terms = part_terms + swap(part_terms, "zh")
-    grad_w_gate, grad_w_up = plan.whole_columns(gate_block), plan.whole_columns(up_block)
-    attn_sum, out_sum, gain_terms, part_terms, grad_tokens, grad_w_gate, grad_w_up = sync(
-        attn_sum, out_sum, gain_terms, part_terms, grad_tokens, grad_w_gate, grad_w_up
-    )
-    attn_block = plan.return_columns(summed(plan.ring_part(attn_terms, 0), attn_sum))
-    out_sum = plan.shift(summed(plan.ring_part(out_terms, 3), out_sum))
-    part_grads = plan.own_gains(part_terms + swap(part_terms, "zl"))
-    gain_terms = plan.gain_step(plan.gain_step(gain_terms, "zh", 1), "zl", 1)
-    attn_block, out_sum, part_grads, gain_terms = sync(attn_block, out_sum, part_grads, gain_terms)
-    grad_w_out = plan.ring_part(out_terms, 0).astype(f32) + out_sum.astype(f32)
+    grad_w_up = plan.whole_columns(up_block)
+    attn_block, grad_w_up, out_sum, gain_terms = sync(attn_block, grad_w_up, out_sum, gain_terms)
+    grad_w_out = plan.ring_sum(0, out_terms, out_sum)
     grad_w_query, grad_w_key, grad_w_value = (
         plan.whole_columns(attn_block[..., k * columns : (k + 1) * columns]) for k in range(3)
     )

time: 906 us -> 836 us (0.923)
  starting transfers between devices: 166 us -> 96.8 us
  waiting for transfers between devices: 311 us -> 334 us
  local copies, waits for them, and re-layouts: 82 us -> 63.9 us
    ppermute x15 -> x12, starting transfers between devices: 84 us -> 14.6 us  [shift(): return lax.ppermute(value, self.z_axes, ((0, 1), (1, 2), (2, 3), (3, 0)))]
    convert_element_type x12 -> x2, other arithmetic: 40.8 us -> 14 us  [summed(): return (mine.astype(f32) + other.astype(f32)).astype(bf16)]
    ppermute x67 -> x69, waiting for transfers between devices: 215 us -> 238 us  [swap(): return lax.ppermute(value, axis, ((0, 1), (1, 0)))]
    ppermute x15 -> x12, waiting for transfers between devices: 71.8 us -> 93.3 us  [shift(): return lax.ppermute(value, self.z_axes, ((0, 1), (1, 2), (2, 3), (3, 0)))]
    convert_element_type x0 -> x8, other arithmetic: none -> 18.6 us  [the longest x6 10.8 us: ring_step(): return self.shift(self.ring_sum(k, terms, so_far).astype(bf16))]
    all_to_all x3, waiting for transfers between devices: 11.8 us -> 0.01 us  [return_columns(): return lax.all_to_all(block.reshape(4, -1, block.shape[1]), self.team, 0, 0)]
    unnamed x158 -> x150, local copies, waits for them, and re-layouts: 28.3 us -> 19.3 us
    dot_general x10 -> x11, matrix products: 54.7 us -> 60.8 us  [inner_rows(): lax.dot_general(left, right, (((0,), (0,)), ((), ())), preferred_element_...]
  transfers between devices with their start and end apart: 93 -> 93, of which waited for: 47 -> 49; matrix products, arithmetic and copies ran while one was open for 26% -> 31% of each run, Pallas kernels for 7% -> 7%
where the time goes in v3:
time: 836 us; the launch traced here: 829 us
  waiting for transfers between devices  334 us (40%)
  matrix products  167 us (20%)
  starting transfers between devices  96.8 us (12%)
  other arithmetic  81.3 us (10%)
  Pallas kernels  70.2 us (8%)
  local copies, waits for them, and re-layouts  63.9 us (8%)
  between operations  16.1 us (2%)
    ppermute x69, waiting for transfers between devices, swap(): return lax.ppermute(value, axis, ((0, 1), (1, 0)))  238 us
    ppermute x12, waiting for transfers between devices, shift(): return lax.ppermute(value, self.z_axes, ((0, 1), (1, 2), (2, 3), (3, 0)))  93.3 us
    dot_general x11, matrix products, inner_rows(): lax.dot_general(left, right, (((0,), (0,)), ((), ())), preferred_element_...  60.8 us
    dot_general x5, matrix products, product_tt(): lax.dot_general(left, right, (((1,), (1,)), ((), ())), preferred_element_...  56.5 us
    ppermute x69, starting transfers between devices, swap(): return lax.ppermute(value, axis, ((0, 1), (1, 0)))  56 us
    dot_general x5, matrix products, product(): return jnp.dot(left, right, preferred_element_type=f32)  49.3 us
    pallas_call x1, Pallas kernels, attend_back(): pl.pallas_call(attend_back_kernel, grid=(size,), in_specs=[whole, rows(3...  21.6 us
    unnamed x150, local copies, waits for them, and re-layouts  19.3 us
  transfers between devices with their start and end apart: 93, of which 49 were waited for; matrix products, arithmetic and copies ran while one was open for 31% of the time, Pallas kernels for 7%

profile of v3, /device:TPU:0, one launch (start us, length us, event | category | flops | bytes accessed | tf_op | source)
XLA Modules:
  0.0 829.0 jit_solution(10058448258281337518)
XLA Ops:
  25.3 13.3 %collective-permute-done.refs_2_ = bf16[128,2048]{1,0:T(8,128)(2,1)S(1)} collective-permute-done((bf16[128,2048]{1,0:T(8,128)(2,1)S(1)}, bf16[128,2048]{1,0:T(8,128)(2,1)S(1)}, u32[]{:S(2)}, u32[]{:S(2)}) %collective-permute-start) | collective-permute-done | bytes 524320 | tf_op jit(solution)/shard_map/ppermute | solution.py:198
  42.3 28.5 %collective-permute-done.4.refs_1_ = bf16[256,2048]{1,0:T(8,128)(2,1)} collective-permute-done((bf16[256,2048]{1,0:T(8,128)(2,1)S(1)}, bf16[256,2048]{1,0:T(8,128)(2,1)}, u32[]{:S(2)}, u32[]{:S(2)}) %collective-permute-start.4) | collective-permute-done | bytes 1048608 | tf_op jit(solution)/shard_map/ppermute | solution.py:295
  74.6 8.5 %collective-permute-done.7.refs_6_ = bf16[128,2048]{1,0:T(8,128)(2,1)S(1)} collective-permute-done((bf16[128,2048]{1,0:T(8,128)(2,1)S(1)}, bf16[128,2048]{1,0:T(8,128)(2,1)S(1)}, u32[]{:S(2)}, u32[]{:S(2)}) %collective-permute-start.7) | collective-permute-done | bytes 524320 | tf_op jit(solution)/shard_map/ppermute | solution.py:198
  128.2 8.9 %collective-permute-done.14 = bf16[5,16,64]{2,1,0:T(8,128)(2,1)S(1)} collective-permute-done((bf16[5,16,64]{2,1,0:T(8,128)(2,1)S(1)}, bf16[5,16,64]{2,1,0:T(8,128)(2,1)S(1)}, u32[]{:S(2)}, u32[]{:S(2)}) %collective-permute-start.14) | collective-permute-done | bytes 10272 | tf_op jit(solution)/shard_map/ppermute | solution.py:198
  137.1 9.8 %collective-permute-done.11.refs_3_ = bf16[256,1536]{1,0:T(8,128)(2,1)} collective-permute-done((bf16[256,1536]{1,0:T(8,128)(2,1)}, bf16[256,1536]{1,0:T(8,128)(2,1)}, u32[]{:S(2)}, u32[]{:S(2)}) %collective-permute-start.11) | collective-permute-done | bytes 786464 | tf_op jit(solution)/shard_map/ppermute | solution.py:295
  173.5 12.3 %shard_map.276 = (bf16[1024,1536]{1,0:T(8,128)(2,1)}, bf16[1024,512]{1,0:T(8,128)(2,1)}) custom-call(s32[4,2]{1,0:T(4,128)} %slice_convert_fusion.9.lengths_ref, f32[1024,1536]{1,0:T(8,128)} %copy-done.18, f32[1024,2]{1,0:T(8,128)} %bitcast.274, f32[2,512]{1,0:T(2,128)} %constant_dynamic-slice_fusion.21.gains_ref, f32[1024,128]{1,0:T(8,128)} %pad_maximum_fusion.6.cosine_ref, ...), custom_call_target="tpu_custom_call" | custom-call | tf_op jit(solution)/shard_map/pallas_call | solution.py:162
  191.6 22.8 %collective-permute-done.18 = bf16[2,128,2048]{2,1,0:T(8,128)(2,1)S(1)} collective-permute-done((bf16[2,128,2048]{2,1,0:T(8,128)(2,1)S(1)}, bf16[2,128,2048]{2,1,0:T(8,128)(2,1)S(1)}, u32[]{:S(2)}, u32[]{:S(2)}) %collective-permute-start.18) | collective-permute-done | bytes 1048608 | tf_op jit(solution)/shard_map/ppermute | solution.py:198
  219.1 8.2 collective-permute-done.19
  239.4 10.8 %collective-permute-done.22.refs_2_ = bf16[128,2048]{1,0:T(8,128)(2,1)S(1)} collective-permute-done((bf16[128,2048]{1,0:T(8,128)(2,1)S(1)}, bf16[128,2048]{1,0:T(8,128)(2,1)S(1)}, u32[]{:S(2)}, u32[]{:S(2)}) %collective-permute-start.22) | collective-permute-done | bytes 524320 | tf_op jit(solution)/shard_map/ppermute | solution.py:198
  252.3 9.3 %collective-permute-done.23.refs_3_ = bf16[128,2048]{1,0:T(8,128)(2,1)} collective-permute-done((bf16[128,2048]{1,0:T(8,128)(2,1)S(1)}, bf16[128,2048]{1,0:T(8,128)(2,1)}, u32[]{:S(2)}, u32[]{:S(2)}) %collective-permute-start.23) | collective-permute-done | bytes 524320 | tf_op jit(solution)/shard_map/ppermute | solution.py:198
  276.2 14.5 %fusion.51 = f32[1024,2048]{1,0:T(8,128)} fusion(bf16[1024,2048]{1,0:T(8,128)(2,1)} %copy-done.2, bf16[2048,2048]{1,0:T(8,128)(2,1)} %all-gather.6.cloned.1.call-done), kind=kOutput, calls=%fused_computation.220 | convolution fusion | flops 8589934592 | bytes 20971520 | tf_op jit(solution)/shard_map/dot_general | solution.py:21
  290.6 16.9 %collective-permute-done.28.refs_2_ = bf16[256,2048]{1,0:T(8,128)(2,1)} collective-permute-done((bf16[256,2048]{1,0:T(8,128)(2,1)}, bf16[256,2048]{1,0:T(8,128)(2,1)}, u32[]{:S(2)}, u32[]{:S(2)}) %collective-permute-start.28) | collective-permute-done | bytes 1048608 | tf_op jit(solution)/shard_map/ppermute | solution.py:295
  308.1 14.7 %fusion.52 = f32[1024,2048]{1,0:T(8,128)} fusion(bf16[1024,2048]{1,0:T(8,128)(2,1)} %copy-done.2, bf16[2048,2048]{1,0:T(8,128)(2,1)} %all-gather.8.cloned.1.call-done), kind=kOutput, calls=%fused_computation.221 | convolution fusion | flops 8589934592 | bytes 20971520 | tf_op jit(solution)/shard_map/dot_general | solution.py:21
  322.9 9.7 %collective-permute-done.29.refs_3_ = bf16[256,2048]{1,0:T(8,128)(2,1)S(1)} collective-permute-done((bf16[256,2048]{1,0:T(8,128)(2,1)}, bf16[256,2048]{1,0:T(8,128)(2,1)S(1)}, u32[]{:S(2)}, u32[]{:S(2)}) %collective-permute-start.29) | collective-permute-done | bytes 1048608 | tf_op jit(solution)/shard_map/ppermute | solution.py:295
  340.7 9.2 %convolution_convert_fusion.1 = bf16[1024,2048]{1,0:T(8,128)(2,1)S(1)} fusion(bf16[1024,2048]{1,0:T(8,128)(2,1)S(1)} %multiply_convert_fusion.2, bf16[2048,2048]{1,0:T(8,128)(2,1)S(1)} %shard_map.279), kind=kOutput, calls=%fused_computation.10 | convolution fusion | flops 8592031744 | bytes 16777216 | tf_op jit(solution)/shard_map/dot_general | solution.py:21
  356.1 19.9 %collective-permute-done.34 = bf16[2,128,2048]{2,1,0:T(8,128)(2,1)S(1)} collective-permute-done((bf16[2,128,2048]{2,1,0:T(8,128)(2,1)S(1)}, bf16[2,128,2048]{2,1,0:T(8,128)(2,1)S(1)}, u32[]{:S(2)}, u32[]{:S(2)}) %collective-permute-start.34) | collective-permute-done | bytes 1048608 | tf_op jit(solution)/shard_map/ppermute | solution.py:198
  382.6 9.2 %collective-permute-done.36 = bf16[128,2048]{1,0:T(8,128)(2,1)} collective-permute-done((bf16[128,2048]{1,0:T(8,128)(2,1)}, bf16[128,2048]{1,0:T(8,128)(2,1)}, u32[]{:S(2)}, u32[]{:S(2)}) %collective-permute-start.36) | collective-permute-done | bytes 524320 | tf_op jit(solution)/shard_map/ppermute | solution.py:198
  400.8 10.8 %collective-permute-done.38.refs_2_ = bf16[128,2048]{1,0:T(8,128)(2,1)S(1)} collective-permute-done((bf16[128,2048]{1,0:T(8,128)(2,1)S(1)}, bf16[128,2048]{1,0:T(8,128)(2,1)S(1)}, u32[]{:S(2)}, u32[]{:S(2)}) %collective-permute-start.38) | collective-permute-done | bytes 524320 | tf_op jit(solution)/shard_map/ppermute | solution.py:198
  413.9 9.0 %collective-permute-done.39.refs_3_ = bf16[128,2048]{1,0:T(8,128)(2,1)S(1)} collective-permute-done((bf16[128,2048]{1,0:T(8,128)(2,1)S(1)}, bf16[128,2048]{1,0:T(8,128)(2,1)S(1)}, u32[]{:S(2)}, u32[]{:S(2)}) %collective-permute-start.39) | collective-permute-done | bytes 524320 | tf_op jit(solution)/shard_map/ppermute | solution.py:198
  424.5 8.4 %collective-permute-done.42.refs_6_ = bf16[128,2048]{1,0:T(8,128)(2,1)S(1)} collective-permute-done((bf16[128,2048]{1,0:T(8,128)(2,1)S(1)}, bf16[128,2048]{1,0:T(8,128)(2,1)S(1)}, u32[]{:S(2)}, u32[]{:S(2)}) %collective-permute-start.42) | collective-permute-done | bytes 524320 | tf_op jit(solution)/shard_map/ppermute | solution.py:198
  455.6 21.5 %multiply_convert_fusion = (bf16[1024,2048]{1,0:T(8,128)(2,1)}, bf16[1024,2048]{1,0:T(8,128)(2,1)}) fusion(f32[1024,2048]{1,0:T(8,128)} %fusion.51, f32[1024,2048]{1,0:T(8,128)} %fusion.52, bf16[1024,2048]{1,0:T(8,128)(2,1)} %copy-done.5, bf16[2048,2048]{1,0:T(8,128)(2,1)} %copy-done.3), kind=kOutput, calls=%fused_computation.3 | convolution fusion | flops 8617197568 | bytes 37748736 | tf_op jit(solution)/shard_map/dot_general | solution.py:25
  477.1 8.5 %convolution_convert_fusion.6 = bf16[1024,2048]{1,0:T(8,128)(2,1)} fusion(bf16[1024,1024]{1,0:T(8,128)(2,1)S(1)} %copy-done.42, bf16[1024,2048]{1,0:T(8,128)(2,1)} %get-tuple-element.229), kind=kOutput, calls=%fused_computation.15 | convolution fusion | flops 4297064448 | bytes 10485760 | tf_op jit(solution)/shard_map/dot_general | solution.py:29
  492.1 13.3 %fusion.53 = f32[1024,2048]{1,0:T(8,128)} fusion(bf16[1024,2048]{1,0:T(8,128)(2,1)} %get-tuple-element.238, bf16[2048,2048]{1,0:T(8,128)(2,1)S(1)} %bitcast.316), kind=kOutput, calls=%fused_computation.222 | convolution fusion | flops 8589934592 | bytes 20971520 | tf_op jit(solution)/shard_map/dot_general | solution.py:25
  505.5 11.4 %add_convert_fusion.2 = bf16[1024,2048]{1,0:T(8,128)(2,1)S(1)} fusion(f32[1024,2048]{1,0:T(8,128)} %fusion.53, bf16[1024,2048]{1,0:T(8,128)(2,1)S(1)} %copy-done.66, bf16[2048,2048]{1,0:T(8,128)(2,1)S(1)} %bitcast.314), kind=kOutput, calls=%fused_computation.2 | convolution fusion | flops 8594128896 | bytes 25165824 | tf_op jit(solution)/shard_map/dot_general | solution.py:25
  520.4 7.9 add_convert_fusion.1
  528.4 15.6 %collective-permute-done.47 = bf16[2,128,2048]{2,1,0:T(8,128)(2,1)} collective-permute-done((bf16[2,128,2048]{2,1,0:T(8,128)(2,1)}, bf16[2,128,2048]{2,1,0:T(8,128)(2,1)}, u32[]{:S(2)}, u32[]{:S(2)}) %collective-permute-start.47) | collective-permute-done | bytes 1048608 | tf_op jit(solution)/shard_map/ppermute | solution.py:198
  560.2 10.0 %collective-permute-done.50 = bf16[128,2048]{1,0:T(8,128)(2,1)S(1)} collective-permute-done((bf16[128,2048]{1,0:T(8,128)(2,1)S(1)}, bf16[128,2048]{1,0:T(8,128)(2,1)S(1)}, u32[]{:S(2)}, u32[]{:S(2)}) %collective-permute-start.50) | collective-permute-done | bytes 524320 | tf_op jit(solution)/shard_map/ppermute | solution.py:198
  617.3 9.5 %collective-permute-done.56.refs_6_ = bf16[128,2048]{1,0:T(8,128)(2,1)} collective-permute-done((bf16[128,2048]{1,0:T(8,128)(2,1)S(1)}, bf16[128,2048]{1,0:T(8,128)(2,1)}, u32[]{:S(2)}, u32[]{:S(2)}) %collective-permute-start.56) | collective-permute-done | bytes 524320 | tf_op jit(solution)/shard_map/ppermute | solution.py:198
  637.5 21.6 %shard_map.283 = (f32[1024,1024]{1,0:T(8,128)}, bf16[1024,512]{1,0:T(8,128)(2,1)}, f32[1024,2]{1,0:T(8,128)}, f32[2,512]{1,0:T(2,128)}) custom-call(s32[4,2]{1,0:T(4,128)} %slice_convert_fusion.9.lengths_ref, f32[1024,1536]{1,0:T(8,128)} %copy-done.18, bf16[1024,1536]{1,0:T(8,128)(2,1)} %get-tuple-element.208.turned_ref, f32[1024,2]{1,0:T(8,128)} %bitcast.275, ...), custom_call_target="tpu_custom_call" | custom-call | tf_op jit(solution)/shard_map/pallas_call | solution.py:179
  713.0 15.0 %collective-permute-done.70 = f32[2,2,2,2,64]{4,3,2,1,0:T(2,128)S(1)} collective-permute-done((f32[2,2,2,2,64]{4,3,2,1,0:T(2,128)S(1)}, f32[2,2,2,2,64]{4,3,2,1,0:T(2,128)S(1)}, u32[]{:S(2)}, u32[]{:S(2)}) %collective-permute-start.70) | collective-permute-done | bytes 4128 | tf_op jit(solution)/shard_map/ppermute | solution.py:198
  751.6 8.0 collective-permute-done.69
  781.0 15.1 %collective-permute-done.75 = bf16[64,2048]{1,0:T(8,128)(2,1)S(1)} collective-permute-done((bf16[64,2048]{1,0:T(8,128)(2,1)}, bf16[64,2048]{1,0:T(8,128)(2,1)S(1)}, u32[]{:S(2)}, u32[]{:S(2)}) %collective-permute-start.75) | collective-permute-done | bytes 262176 | tf_op jit(solution)/shard_map/ppermute | solution.py:295
  (513 shorter events, 400.5 us)
Async XLA Ops:
  7.2 104.8 %all-gather.4.cloned.1.call-start = ((), (), s32[]{:S(2)}) async-start(), calls=%async_computation.9 | async-start | bytes 2949120 | tf_op jit(solution)/shard_map/all_gather | solution.py:593
  11.3 27.3 %all-to-all-start = ((bf16[4,64,1536]{2,1,0:T(8,128)(2,1)}), bf16[4,64,1536]{2,1,0:T(8,128)(2,1)S(1)}, u32[]{:S(2)}, u32[]{:S(2)}) async-start(bf16[4,64,1536]{2,1,0:T(8,128)(2,1)} %pad_maximum_fusion.5), calls=%async_computation | async-start | bytes 1572864 | tf_op jit(solution)/shard_map/all_to_all | solution.py:340
  23.7 47.1 %collective-permute-start.4 = (bf16[256,2048]{1,0:T(8,128)(2,1)S(1)}, bf16[256,2048]{1,0:T(8,128)(2,1)}, u32[]{:S(2)}, u32[]{:S(2)}) collective-permute-start(bf16[256,2048]{1,0:T(8,128)(2,1)S(1)} %copy-done.7), channel_id=1, source_target_pairs={{0,1},{1,2},{2,3},{3,0},{4,5},{5,6},{6,7},{7,4},{8,9},{9,10},{10,1... | collective-permute-start | bytes 3145736 | tf_op jit(solution)/shard_map/ppermute | solution.py:295
  38.7 33.4 %collective-permute-start.5 = (bf16[128,2048]{1,0:T(8,128)(2,1)S(1)}, bf16[128,2048]{1,0:T(8,128)(2,1)S(1)}, u32[]{:S(2)}, u32[]{:S(2)}) collective-permute-start(bf16[128,2048]{1,0:T(8,128)(2,1)S(1)} %get-tuple-element.176.refs_1_), channel_id=1, source_target_pairs={{0,8},{8,0},{1,9},{9,1},{2,10},{10,2},{3,11},{11,3},{4,12},{12,4},... | collective-permute-start | bytes 1572872 | tf_op jit(solution)/shard_map/ppermute | solution.py:198
  40.1 46.7 %collective-permute-start.2 = (bf16[256,1536]{1,0:T(8,128)(2,1)S(1)}, bf16[256,1536]{1,0:T(8,128)(2,1)}, u32[]{:S(2)}, u32[]{:S(2)}) collective-permute-start(bf16[256,1536]{1,0:T(8,128)(2,1)S(1)} %bitcast.271), channel_id=1, source_target_pairs={{0,1},{1,2},{2,3},{3,0},{4,5},{5,6},{6,7},{7,4},{8,9},{9,10},{10,1... | collective-permute-start | bytes 2359304 | tf_op jit(solution)/shard_map/ppermute | solution.py:295
  41.7 45.1 %collective-permute-start.3 = (bf16[256,1536]{1,0:T(8,128)(2,1)S(1)}, bf16[256,1536]{1,0:T(8,128)(2,1)S(1)}, u32[]{:S(2)}, u32[]{:S(2)}) collective-permute-start(bf16[256,1536]{1,0:T(8,128)(2,1)S(1)} %bitcast.272), channel_id=1, source_target_pairs={{0,4},{4,0},{1,5},{5,1},{2,6},{6,2},{3,7},{7,3},{8,12},{12,8},{9,1... | collective-permute-start | bytes 2359304 | tf_op jit(solution)/shard_map/ppermute | solution.py:198
  41.7 32.1 %collective-permute-start.6 = (bf16[128,2048]{1,0:T(8,128)(2,1)S(1)}, bf16[128,2048]{1,0:T(8,128)(2,1)S(1)}, u32[]{:S(2)}, u32[]{:S(2)}) collective-permute-start(bf16[128,2048]{1,0:T(8,128)(2,1)S(1)} %get-tuple-element.175.refs_0_), channel_id=1, source_target_pairs={{0,16},{16,0},{1,17},{17,1},{2,18},{18,2},{3,19},{19,3},{4,20},{20... | collective-permute-start | bytes 1572872 | tf_op jit(solution)/shard_map/ppermute | solution.py:198
  97.4 178.8 %all-gather.6.cloned.1.call-start = ((), (), s32[]{:S(2)}) async-start(), calls=%async_computation.10 | async-start | bytes 9437184 | tf_op jit(solution)/shard_map/all_gather | solution.py:593
  114.3 32.6 %collective-permute-start.11 = (bf16[256,1536]{1,0:T(8,128)(2,1)}, bf16[256,1536]{1,0:T(8,128)(2,1)}, u32[]{:S(2)}, u32[]{:S(2)}) collective-permute-start(bf16[256,1536]{1,0:T(8,128)(2,1)} %collective-permute-done.9.refs_2_), channel_id=1, source_target_pairs={{0,1},{1,2},{2,3},{3,0},{4,5},{5,6},{6,7},{7,4},{8,9},{9,10},{10,1... | collective-permute-start | bytes 2359304 | tf_op jit(solution)/shard_map/ppermute | solution.py:295
  114.4 32.5 %collective-permute-start.12 = (bf16[256,1536]{1,0:T(8,128)(2,1)}, bf16[256,1536]{1,0:T(8,128)(2,1)}, u32[]{:S(2)}, u32[]{:S(2)}) collective-permute-start(bf16[256,1536]{1,0:T(8,128)(2,1)} %collective-permute-done.9.refs_2_), channel_id=1, source_target_pairs={{0,4},{4,0},{1,5},{5,1},{2,6},{6,2},{3,7},{7,3},{8,12},{12,8},{9,1... | collective-permute-start | bytes 2359304 | tf_op jit(solution)/shard_map/ppermute | solution.py:198
  122.2 186.0 %all-gather.8.cloned.1.call-start = ((), (), s32[]{:S(2)}) async-start(), calls=%async_computation.11 | async-start | bytes 9437184 | tf_op jit(solution)/shard_map/all_gather | solution.py:593
  146.9 454.5 %reduce-scatter.4.cloned.1.call-start = ((), (), s32[]{:S(2)}) async-start(), calls=%async_computation.12 | async-start | bytes 5242880 | tf_op jit(solution)/shard_map/reduce_scatter | solution.py:680
  238.8 29.7 %collective-permute-start.24 = (bf16[128,2048]{1,0:T(8,128)(2,1)S(1)}, bf16[128,2048]{1,0:T(8,128)(2,1)}, u32[]{:S(2)}, u32[]{:S(2)}) collective-permute-start(bf16[128,2048]{1,0:T(8,128)(2,1)S(1)} %get-tuple-element.358.refs_0_), channel_id=1, source_target_pairs={{0,16},{16,0},{1,17},{17,1},{2,18},{18,2},{3,19},{19,3},{4,20},{20... | collective-permute-start | bytes 1572872 | tf_op jit(solution)/shard_map/ppermute | solution.py:198
  252.3 85.0 %collective-permute-start.30 = (bf16[256,2048]{1,0:T(8,128)(2,1)S(1)}, bf16[256,2048]{1,0:T(8,128)(2,1)}, u32[]{:S(2)}, u32[]{:S(2)}) collective-permute-start(bf16[256,2048]{1,0:T(8,128)(2,1)S(1)} %copy-done.7), channel_id=1, source_target_pairs={{0,4},{4,0},{1,5},{5,1},{2,6},{6,2},{3,7},{7,3},{8,12},{12,8},{9,1... | collective-permute-start | bytes 3145736 | tf_op jit(solution)/shard_map/ppermute | solution.py:198
  261.6 46.0 %collective-permute-start.28 = (bf16[256,2048]{1,0:T(8,128)(2,1)}, bf16[256,2048]{1,0:T(8,128)(2,1)}, u32[]{:S(2)}, u32[]{:S(2)}) collective-permute-start(bf16[256,2048]{1,0:T(8,128)(2,1)} %collective-permute-done.4.refs_1_), channel_id=1, source_target_pairs={{0,1},{1,2},{2,3},{3,0},{4,5},{5,6},{6,7},{7,4},{8,9},{9,10},{10,1... | collective-permute-start | bytes 3145736 | tf_op jit(solution)/shard_map/ppermute | solution.py:295
  268.4 68.9 %collective-permute-start.31 = (bf16[256,2048]{1,0:T(8,128)(2,1)}, bf16[256,2048]{1,0:T(8,128)(2,1)}, u32[]{:S(2)}, u32[]{:S(2)}) collective-permute-start(bf16[256,2048]{1,0:T(8,128)(2,1)} %collective-permute-done.4.refs_1_), channel_id=1, source_target_pairs={{0,4},{4,0},{1,5},{5,1},{2,6},{6,2},{3,7},{7,3},{8,12},{12,8},{9,1... | collective-permute-start | bytes 3145736 | tf_op jit(solution)/shard_map/ppermute | solution.py:198
  308.0 29.3 %collective-permute-start.32 = (bf16[256,2048]{1,0:T(8,128)(2,1)}, bf16[256,2048]{1,0:T(8,128)(2,1)}, u32[]{:S(2)}, u32[]{:S(2)}) collective-permute-start(bf16[256,2048]{1,0:T(8,128)(2,1)} %collective-permute-done.28.refs_2_), channel_id=1, source_target_pairs={{0,4},{4,0},{1,5},{5,1},{2,6},{6,2},{3,7},{7,3},{8,12},{12,8},{9,1... | collective-permute-start | bytes 3145736 | tf_op jit(solution)/shard_map/ppermute | solution.py:198
  350.4 25.6 %collective-permute-start.34 = (bf16[2,128,2048]{2,1,0:T(8,128)(2,1)S(1)}, bf16[2,128,2048]{2,1,0:T(8,128)(2,1)S(1)}, u32[]{:S(2)}, u32[]{:S(2)}) collective-permute-start(bf16[2,128,2048]{2,1,0:T(8,128)(2,1)S(1)} %get-tuple-element.339), channel_id=1, source_target_pairs={{0,16},{16,0},{1,17},{17,1},{2,18},{18,2},{3,19},{19,3},{4,20},{20... | collective-permute-start | bytes 3145736 | tf_op jit(solution)/shard_map/ppermute | solution.py:198
  351.8 25.3 %collective-permute-start.35 = (bf16[2,128,2048]{2,1,0:T(8,128)(2,1)S(1)}, bf16[2,128,2048]{2,1,0:T(8,128)(2,1)S(1)}, u32[]{:S(2)}, u32[]{:S(2)}) collective-permute-start(bf16[2,128,2048]{2,1,0:T(8,128)(2,1)S(1)} %get-tuple-element.337), channel_id=1, source_target_pairs={{0,8},{8,0},{1,9},{9,1},{2,10},{10,2},{3,11},{11,3},{4,12},{12,4},... | collective-permute-start | bytes 3145736 | tf_op jit(solution)/shard_map/ppermute | solution.py:198
  454.5 172.3 %reduce-scatter.6.cloned.1.call-start = ((), (), s32[]{:S(2)}) async-start(), calls=%async_computation.13 | async-start | bytes 5242880 | tf_op jit(solution)/shard_map/reduce_scatter | solution.py:700
  492.0 28.4 %collective-permute-start.46 = (bf16[1024,2048]{1,0:T(8,128)(2,1)}, bf16[1024,2048]{1,0:T(8,128)(2,1)}, u32[]{:S(2)}, u32[]{:S(2)}) collective-permute-start(bf16[1024,2048]{1,0:T(8,128)(2,1)} %convolution_convert_fusion.6), channel_id=1, source_target_pairs={{0,4},{4,0},{1,5},{5,1},{2,6},{6,2},{3,7},{7,3},{8,12},{12,8},{9,1... | collective-permute-start | bytes 12582920 | tf_op jit(solution)/shard_map/ppermute | solution.py:198
  518.1 25.9 %collective-permute-start.47 = (bf16[2,128,2048]{2,1,0:T(8,128)(2,1)}, bf16[2,128,2048]{2,1,0:T(8,128)(2,1)}, u32[]{:S(2)}, u32[]{:S(2)}) collective-permute-start(bf16[2,128,2048]{2,1,0:T(8,128)(2,1)} %get-tuple-element.333), channel_id=1, source_target_pairs={{0,16},{16,0},{1,17},{17,1},{2,18},{18,2},{3,19},{19,3},{4,20},{20... | collective-permute-start | bytes 3145736 | tf_op jit(solution)/shard_map/ppermute | solution.py:198
  520.1 25.6 %collective-permute-start.48 = (bf16[2,128,2048]{2,1,0:T(8,128)(2,1)}, bf16[2,128,2048]{2,1,0:T(8,128)(2,1)}, u32[]{:S(2)}, u32[]{:S(2)}) collective-permute-start(bf16[2,128,2048]{2,1,0:T(8,128)(2,1)} %get-tuple-element.331), channel_id=1, source_target_pairs={{0,8},{8,0},{1,9},{9,1},{2,10},{10,2},{3,11},{11,3},{4,12},{12,4},... | collective-permute-start | bytes 3145736 | tf_op jit(solution)/shard_map/ppermute | solution.py:198
  554.2 40.1 %collective-permute-start.51 = (bf16[1024,2048]{1,0:T(8,128)(2,1)}, bf16[1024,2048]{1,0:T(8,128)(2,1)}, u32[]{:S(2)}, u32[]{:S(2)}) collective-permute-start(bf16[1024,2048]{1,0:T(8,128)(2,1)} %convolution_convert_fusion.5), channel_id=1, source_target_pairs={{0,4},{4,0},{1,5},{5,1},{2,6},{6,2},{3,7},{7,3},{8,12},{12,8},{9,1... | collective-permute-start | bytes 12582920 | tf_op jit(solution)/shard_map/ppermute | solution.py:198
  581.3 49.9 %collective-permute-start.58 = (f32[2,2,2,2,64]{4,3,2,1,0:T(2,128)S(1)}, f32[2,2,2,2,64]{4,3,2,1,0:T(2,128)S(1)}, u32[]{:S(2)}, u32[]{:S(2)}) collective-permute-start(f32[2,2,2,2,64]{4,3,2,1,0:T(2,128)S(1)} %fusion.29), channel_id=1, source_target_pairs={{0,4},{4,0},{1,5},{5,1},{2,6},{6,2},{3,7},{7,3},{8,12},{12,8},{9,1... | collective-permute-start | bytes 12296 | tf_op jit(solution)/shard_map/ppermute | solution.py:198
  626.9 32.2 %all-to-all-start.3 = ((bf16[4,64,2048]{2,1,0:T(8,128)(2,1)}), bf16[4,64,2048]{2,1,0:T(8,128)(2,1)}, u32[]{:S(2)}, u32[]{:S(2)}) async-start(bf16[4,64,2048]{2,1,0:T(8,128)(2,1)} %bitcast.294), calls=%async_computation.5 | async-start | bytes 2097152 | tf_op jit(solution)/shard_map/all_to_all | solution.py:343
  631.1 128.4 %reduce-scatter.8.cloned.1.call-start = ((), (), s32[]{:S(2)}) async-start(), calls=%async_computation.14 | async-start | bytes 5242880 | tf_op jit(solution)/shard_map/reduce_scatter | solution.py:715
  672.7 55.3 %collective-permute-start.64 = (bf16[256,2048]{1,0:T(8,128)(2,1)}, bf16[256,2048]{1,0:T(8,128)(2,1)}, u32[]{:S(2)}, u32[]{:S(2)}) collective-permute-start(bf16[256,2048]{1,0:T(8,128)(2,1)} %convolution_convert_fusion.12), channel_id=1, source_target_pairs={{0,4},{4,0},{1,5},{5,1},{2,6},{6,2},{3,7},{7,3},{8,12},{12,8},{9,1... | collective-permute-start | bytes 3145736 | tf_op jit(solution)/shard_map/ppermute | solution.py:198
  701.9 26.1 %collective-permute-start.66 = (bf16[2,128,2048]{2,1,0:T(8,128)(2,1)}, bf16[2,128,2048]{2,1,0:T(8,128)(2,1)}, u32[]{:S(2)}, u32[]{:S(2)}) collective-permute-start(bf16[2,128,2048]{2,1,0:T(8,128)(2,1)} %get-tuple-element.329), channel_id=1, source_target_pairs={{0,16},{16,0},{1,17},{17,1},{2,18},{18,2},{3,19},{19,3},{4,20},{20... | collective-permute-start | bytes 3145736 | tf_op jit(solution)/shard_map/ppermute | solution.py:198
  703.4 25.5 %collective-permute-start.67 = (bf16[2,128,2048]{2,1,0:T(8,128)(2,1)}, bf16[2,128,2048]{2,1,0:T(8,128)(2,1)}, u32[]{:S(2)}, u32[]{:S(2)}) collective-permute-start(bf16[2,128,2048]{2,1,0:T(8,128)(2,1)} %get-tuple-element.327), channel_id=1, source_target_pairs={{0,8},{8,0},{1,9},{9,1},{2,10},{10,2},{3,11},{11,3},{4,12},{12,4},... | collective-permute-start | bytes 3145736 | tf_op jit(solution)/shard_map/ppermute | solution.py:198
  730.9 28.6 %collective-permute-start.73 = (bf16[128,2048]{1,0:T(8,128)(2,1)S(1)}, bf16[128,2048]{1,0:T(8,128)(2,1)}, u32[]{:S(2)}, u32[]{:S(2)}) collective-permute-start(bf16[128,2048]{1,0:T(8,128)(2,1)S(1)} %fusion.20), channel_id=1, source_target_pairs={{0,16},{16,0},{1,17},{17,1},{2,18},{18,2},{3,19},{19,3},{4,20},{20... | collective-permute-start | bytes 1572872 | tf_op jit(solution)/shard_map/ppermute | solution.py:198
  733.3 26.2 %collective-permute-start.68 = (bf16[256,1536]{1,0:T(8,128)(2,1)S(1)}, bf16[256,1536]{1,0:T(8,128)(2,1)}, u32[]{:S(2)}, u32[]{:S(2)}) collective-permute-start(bf16[256,1536]{1,0:T(8,128)(2,1)S(1)} %add_convert_fusion.6), channel_id=1, source_target_pairs={{0,1},{1,2},{2,3},{3,0},{4,5},{5,6},{6,7},{7,4},{8,9},{9,10},{10,1... | collective-permute-start | bytes 2359304 | tf_op jit(solution)/shard_map/ppermute | solution.py:295
  (135 other events, 1509.3 us)
Sparse Core Ops, SparseCore 0:
  11.5 55.6 all-gather.3
  112.2 92.5 all-gather.5
  206.4 91.5 all-gather.7
  454.7 73.2 reduce-scatter.3
  545.8 73.7 reduce-scatter.5
  634.0 75.3 reduce-scatter.7

commit v4 on v3

--- a/solution.py
+++ b/solution.py
@@ -86,7 +86,7 @@
     scores = product_tt(query, key) * HEAD_DIM ** (-0.5)
     scores = jnp.where(allowed, scores, -1e30)
     powers = jnp.exp(scores - jnp.max(scores, axis=-1, keepdims=True))
-    return powers / jnp.sum(powers, axis=-1, keepdims=True)
+    return powers * (1.0 / jnp.sum(powers, axis=-1, keepdims=True))
 
 
 def attend_kernel(
@@ -278,6 +278,112 @@
     )(parts)
 
 
+def proj_back_kernel(
+    halves, top_ref, low_ref, top_x_ref, low_y_ref, live_ref, cotangent_ref, proj_ref, inverse_ref,
+    gain_ref, hidden_ref, grad_top_ref, grad_low_ref, term_ref,
+):
+    parts = ((top_ref, top_x_ref, grad_top_ref), (low_ref, low_y_ref, grad_low_ref))
+    gain = gain_ref[...]
+    term = 0.0
+    for half, (mine_ref, other_ref, grad_ref) in enumerate(parts):
+        total = mine_ref[...] + other_ref[...].astype(f32)
+        blocks = [total[:, k * 64 : (k + 1) * 64] for k in halves]
+        total = jnp.concatenate(blocks, axis=1)
+        total += live_ref[half] * cotangent_ref[half].astype(f32)
+        hidden_ref[half] = total
+        normed = proj_ref[half] * inverse_ref[half]
+        term += jnp.sum(total * normed, axis=0, keepdims=True)
+        scaled = total * gain
+        mean = jnp.mean(scaled * normed, axis=-1, keepdims=True)
+        grad_ref[...] = (inverse_ref[half] * (scaled - normed * mean)).astype(bf16)
+    first = pl.program_id(0) == 0
+    term_ref[...] = jnp.where(first, term, term_ref[...] + term)
+
+
+def ordered(blocks, left_ref, right_ref, left_x_ref, right_y_ref):
+    left = left_ref[...] + left_x_ref[...].astype(f32)
+    right = right_ref[...] + right_y_ref[...].astype(f32)
+    half = left.shape[1] // 64
+    parts = [(left, k) if k < half else (right, k - half) for k in blocks]
+    return jnp.concatenate([part[:, k * 64 : (k + 1) * 64] for part, k in parts], axis=1)
+
+
+def tokens_kernel(blocks, left_ref, right_ref, left_x_ref, right_y_ref, hidden_ref, out_ref):
+    total = ordered(blocks, left_ref, right_ref, left_x_ref, right_y_ref)
+    out_ref[...] = (total + hidden_ref[...]).astype(bf16)
+
+
+def tokens_end(blocks, left, right, left_x, right_y, hidden):
+    rows, width = hidden.shape
+    side = pl.BlockSpec((rows // 4, width // 2), lambda k: (k, 0))
+    whole = pl.BlockSpec((rows // 4, width), lambda k: (k, 0))
+    return pl.pallas_call(
+        functools.partial(tokens_kernel, blocks),
+        grid=(4,),
+        in_specs=[side, side, side, side, whole],
+        out_specs=whole,
+        out_shape=jax.ShapeDtypeStruct((rows, width), bf16),
+        cost_estimate=NO_COST,
+    )(left, right, left_x, right_y, hidden)
+
+
+def proj_back_kernel(
+    blocks, left_ref, right_ref, left_x_ref, right_y_ref, live_ref, cotangent_ref, proj_ref,
+    inverse_ref, gain_ref, hidden_ref, grad_ref, term_ref,
+):
+    total = ordered(blocks, left_ref, right_ref, left_x_ref, right_y_ref)
+    total += live_ref[...] * cotangent_ref[...].astype(f32)
+    hidden_ref[...] = total
+    normed = proj_ref[...] * inverse_ref[...]
+    term = jnp.sum(total * normed, axis=0, keepdims=True)
+    scaled = total * gain_ref[...]
+    mean = jnp.mean(scaled * normed, axis=-1, keepdims=True)
+    grad_ref[...] = (inverse_ref[...] * (scaled - normed * mean)).astype(bf16)
+    first = pl.program_id(0) == 0
+    term_ref[...] = jnp.where(first, term, term_ref[...] + term)
+
+
+def proj_back(blocks, left, right, left_x, right_y, live, cotangent, proj, inverse, gain):
+    rows, width = proj.shape
+    side = pl.BlockSpec((rows // 4, width // 2), lambda k: (k, 0))
+    whole = pl.BlockSpec((rows // 4, width), lambda k: (k, 0))
+    column = pl.BlockSpec((rows // 4, 1), lambda k: (k, 0))
+    line = pl.BlockSpec((1, width), lambda k: (0, 0))
+    hidden, grad, term = pl.pallas_call(
+        functools.partial(proj_back_kernel, blocks),
+        grid=(4,),
+        in_specs=[side, side, side, side, column, whole, whole, column, line],
+        out_specs=[whole, whole, line],
+        out_shape=[
+            jax.ShapeDtypeStruct((rows, width), f32),
+            jax.ShapeDtypeStruct((rows, width), bf16),
+            jax.ShapeDtypeStruct((1, width), f32),
+        ],
+        cost_estimate=NO_COST,
+    )(left, right, left_x, right_y, live, cotangent, proj, inverse, gain.reshape(1, width))
+    return hidden, grad, term[0]
+
+
+def spread_three_kernel(parts_ref, *out_refs):
+    columns = parts_ref.shape[2] // 3
+    for which, out_ref in enumerate(out_refs):
+        there = slice(which * columns, (which + 1) * columns)
+        for part in range(parts_ref.shape[0]):
+            here = slice(part * columns, (part + 1) * columns)
+            out_ref[:, here] = parts_ref[part, :, there].astype(f32)
+
+
+def spread_three(parts):
+    shape = (parts.shape[1], parts.shape[0] * parts.shape[2] // 3)
+    return pl.pallas_call(
+        spread_three_kernel,
+        in_specs=[pl.BlockSpec(memory_space=pltpu.VMEM)],
+        out_specs=[pl.BlockSpec(memory_space=pltpu.VMEM)] * 3,
+        out_shape=[jax.ShapeDtypeStruct(shape, f32)] * 3,
+        cost_estimate=NO_COST,
+    )(parts)
+
+
 class Cube:
     every = ("y", "x", "c", "zh", "zl")
     team = ("y", "x")
@@ -303,18 +409,37 @@
         top_y, low_x = swap(top, "y"), swap(low, "x")
         return top, low, top_x, low_x, top_y, low_y, swap(top_x, "y"), swap(low_y, "x")
 
-    def terms_first(self, terms):
-        terms = terms.reshape(2, 2, 2, -1, terms.shape[1])
-        top, low = swap(terms[1, :, 0], "y"), swap(terms[:, 1, 1], "x")
-        return terms[0, :, 0], terms[:, 0, 1], top, low
-
-    def terms_second(self, top, low, top_y, low_x):
-        top = top.astype(f32) + top_y.astype(f32)
-        low = low.astype(f32) + low_x.astype(f32)
-        return top[0], low[0], swap(top[1].astype(bf16), "x"), swap(low[1].astype(bf16), "y")
-
-    def terms_sum(self, top, low, top_x, low_y):
-        return jnp.concatenate([top + top_x.astype(f32), low + low_y.astype(f32)])
+    def terms_first(self, make, *values):
+        left, right = 0, 1
+
+        def along_x(place):
+            return lambda rows: rows.reshape(2, 2, -1, rows.shape[1])[:, place].reshape(
+                -1, rows.shape[1]
+            )
+
+        def along_y(place):
+            return lambda rows: rows[place * rows.shape[0] // 2 : (place + 1) * rows.shape[0] // 2]
+
+        left_away = make(along_y(1), left, *values).astype(bf16)
+        right_away = make(along_x(1), right, *values).astype(bf16)
+        left_away, right_away, *values = sync(left_away, right_away, *values)
+        left_other, right_other = swap(left_away, "y"), swap(right_away, "x")
+        left_mine = make(along_y(0), left, *values).astype(bf16)
+        right_mine = make(along_x(0), right, *values).astype(bf16)
+        return left_mine, right_mine, left_other, right_other
+
+    def terms_added(self, left_mine, right_mine, left_other, right_other):
+        left = left_mine.astype(f32) + left_other.astype(f32)
+        right = right_mine.astype(f32) + right_other.astype(f32)
+        half = left.shape[0] // 2
+        return left[:half], right[:half], left[half:].astype(bf16), right[half:].astype(bf16)
+
+    def terms_second(self, *terms):
+        left, right, left_away, right_away = self.terms_added(*terms)
+        return left, right, swap(left_away, "x"), swap(right_away, "y")
+
+    def terms_sum(self, left, right, left_x, right_y):
+        return jnp.concatenate([left + left_x.astype(f32), right + right_y.astype(f32)], axis=1)
 
     def sum_along(self, rows, axis):
         shape = rows.shape
@@ -345,8 +470,10 @@
     def grouped(self, rows):
         return regroup(rows, [spot * 8 + place for place in range(8) for spot in range(4)])
 
+    own_order = [place * 4 + spot for spot in range(4) for place in range(8)]
+
     def ungrouped(self, rows):
-        return regroup(rows, [place * 4 + spot for spot in range(4) for place in range(8)])
+        return regroup(rows, self.own_order)
 
     def join_group(self, blocks):
         table, pieces = [], []
@@ -402,6 +529,13 @@
     def gain_step(self, terms, axis, dim):
         index = self.place[self.every.index(axis)]
         return pick(terms, index, dim) + swap(pick(terms, 1 - index, dim), axis)
+
+    def both_step(self, terms, parts, axis, dim):
+        index = self.place[self.every.index(axis)]
+        away = pick(terms, 1 - index, dim)
+        other = swap(jnp.concatenate([away.reshape(-1), parts.reshape(-1)]), axis)
+        terms = pick(terms, index, dim) + other[: away.size].reshape(away.shape)
+        return terms, parts + other[away.size :].reshape(parts.shape)
 
     def own_gains(self, terms):
         terms = terms.reshape(terms.shape[0], 2, 2, 2, -1)
@@ -629,10 +763,17 @@
     raw = product(team_tokens, attn_whole)
     inverse = lax.rsqrt(plan.sum_rows(norm_columns(raw, columns)) / width + epsilon)
     turned, mixed_low = attend(lengths, raw, inverse, part_gains, cosine, sine)
-    attn_terms = product(mixed_low, out_whole).astype(bf16)
-    attn_terms, down1, team_tokens = sync(attn_terms, down1, team_tokens)
+    mixed_low, down1, team_tokens = sync(mixed_low, down1, team_tokens)
     down2, down0c, down1c = plan.shift(down1), swap(w_down, "c"), swap(down1, "c")
-    terms = plan.terms_first(attn_terms)
+    half = width // 2
+
+    def by_columns(rows, side, left, right):
+        return product(rows(left), right[:, side * half : (side + 1) * half])
+
+    def by_rows(rows, side, left, right):
+        return product_tt(rows(left), right[side * half : (side + 1) * half])
+
+    terms = plan.terms_first(by_columns, mixed_low, out_whole)
     terms = plan.terms_second(*terms)
     attn_proj = plan.terms_sum(*terms)
     attn_normed, attn_inverse = norm_forward(attn_proj, attn_gain_wide)
@@ -641,20 +782,18 @@
     rows = plan.rows_first(plan.grouped(hidden.astype(bf16)))
     rows = plan.rows_second(*rows)
     team_hidden = join(*rows)
-    gate = product(team_hidden, gate_whole)
+    gate = product(team_hidden, gate_whole).astype(bf16)
     hidden_parts = plan.core_halves(team_hidden)
     gate, down2, *hidden_parts = sync(gate, down2, *hidden_parts)
     down3, down2c = plan.shift(down2), swap(down2, "c")
-    upward = product(team_hidden, up_whole)
-    upward, down3 = sync(upward, down3)
+    upward = product(team_hidden, up_whole).astype(bf16)
+    inner_low = (jax.nn.silu(gate.astype(f32)) * upward.astype(f32)).astype(bf16)
+    inner_low, down3 = sync(inner_low, down3)
     down3c = swap(down3, "c")
     down_whole = plan.join_group([[w_down, down1, down2, down3], [down0c, down1c, down2c, down3c]])
-    sigmoid_gate = jax.nn.sigmoid(gate)
-    activated = gate * sigmoid_gate
-    inner_low = (activated * upward).astype(bf16)
-    terms = plan.terms_first(product(inner_low, down_whole).astype(bf16))
-    *inner_parts, top, low, top_y, low_x = sync(*plan.core_halves(inner_low), *terms)
-    down = plan.terms_sum(*plan.terms_second(top, low, top_y, low_x))
+    terms = plan.terms_first(by_columns, inner_low, down_whole)
+    *inner_parts, left, right, left_y, right_x = sync(*plan.core_halves(inner_low), *terms)
+    down = plan.terms_sum(*plan.terms_second(left, right, left_y, right_x))
     down_normed, down_inverse = norm_forward(down, mlp_gain_wide)
     block_out = (live_col * (hidden + down_normed)).astype(bf16)
 
@@ -679,8 +818,11 @@
     team_grad_down, mlp_terms = sync(team_grad_down, mlp_terms)
     grad_w_down = lax.psum_scatter(down_terms, plan.z_axes, scatter_dimension=0, tiled=True)
     grad_inner = product_tt(team_grad_down, down_whole)
-    grad_gate = grad_inner * upward * sigmoid_gate * (1.0 + gate * (1.0 - sigmoid_gate))
-    grad_up = grad_inner * activated
+    gate_wide = gate.astype(f32)
+    sigmoid_gate = jax.nn.sigmoid(gate_wide)
+    slope = sigmoid_gate * (1.0 + gate_wide * (1.0 - sigmoid_gate))
+    grad_gate = grad_inner * upward.astype(f32) * slope
+    grad_up = grad_inner * (gate_wide * sigmoid_gate)
     grad_gate, grad_up, *hidden_parts = sync(
         grad_gate.astype(bf16), grad_up.astype(bf16), *hidden_parts
     )
@@ -690,23 +832,30 @@
     up_away = terms_of(other_part, grad_up)
     up_away, grad_gate, grad_up = sync(up_away, grad_gate, grad_up)
     up_other = swap(up_away, "c")
-    grad_from_mlp = product_tt(grad_gate, gate_whole) + product_tt(grad_up, up_whole)
-    grad_from_mlp, grad_gate, grad_up, hidden_part = sync(
-        grad_from_mlp.astype(bf16), grad_gate, grad_up, hidden_parts[1]
-    )
-    terms = plan.terms_first(grad_from_mlp)
+    hidden_part = hidden_parts[1]
+
+    def from_mlp(rows, side, gate_grad, up_grad):
+        return by_rows(rows, side, gate_grad, gate_whole) + by_rows(rows, side, up_grad, up_whole)
+
+    terms = plan.terms_first(from_mlp, grad_gate, grad_up)
+    left, right, left_y, right_x = terms
+    left, right, grad_gate, grad_up, hidden_part, own_tokens, own_mixed = sync(
+        left, right, grad_gate, grad_up, hidden_part, team_tokens, mixed_low
+    )
+    terms = left, right, left_y, right_x
     gate_terms = summed(terms_of(hidden_part, grad_gate), gate_other)
-    gate_terms, grad_up, *terms = sync(gate_terms, grad_up, *terms)
+    late_parts = (*plan.core_halves(own_tokens), *plan.core_halves(own_mixed))
+    gate_terms, grad_up, token_other, token_mine, mixed_other, mixed_mine, *terms = sync(
+        gate_terms, grad_up, *late_parts, *terms
+    )
     gate_block = lax.psum_scatter(gate_terms, plan.z_axes, scatter_dimension=0, tiled=True)
     terms = plan.terms_second(*terms)
-    late_parts = (*plan.core_halves(team_tokens), *plan.core_halves(mixed_low))
-    token_other, token_mine, mixed_other, mixed_mine, grad_up, *terms = sync(
-        *late_parts, grad_up, *terms
-    )
-    grad_hidden = grad_out + plan.ungrouped(plan.terms_sum(*terms))
-
-    grad_proj, term_attn_gain = norm_back(attn_proj, attn_inverse, attn_gain_wide, grad_hidden)
-    rows = plan.rows_first(grad_proj.astype(bf16))
+    grad_up, *terms = sync(grad_up, *terms)
+
+    grad_hidden, grad_proj, term_attn_gain = proj_back(
+        plan.own_order, *terms, live_col, cotangent, attn_proj, attn_inverse, attn_gain_wide
+    )
+    rows = plan.rows_first(grad_proj)
     up_mine = terms_of(hidden_part, grad_up)
     up_mine, up_other, grad_w_down, *rows = sync(up_mine, up_other, grad_w_down, *rows)
     rows = plan.rows_second(*rows)
@@ -731,51 +880,62 @@
     means = plan.sum_along(means, "x") / width
     means, out_mine = sync(means, out_mine)
     grad_raw = raw_back(raw, scaled, inverse, means, grad_value)
-    half = token_other.shape[1] // 2
-    attn_other = [swap(terms_of(token_other[:, :half], grad_raw), "c")]
-    attn_other += [swap(terms_of(token_other[:, half:], grad_raw), "c")]
+    part = token_other.shape[1] // 2
+    attn_other = [swap(terms_of(token_other[:, :part], grad_raw), "c")]
+    attn_other += [swap(terms_of(token_other[:, part:], grad_raw), "c")]
     out_other = swap(out_away, "c")
     attn_mine = terms_of(token_mine, grad_raw)
-    grad_from_attn = product_tt(grad_raw, attn_whole).astype(bf16)
-    grad_from_attn, attn_mine, part_terms, gain_terms, *attn_other = sync(
-        grad_from_attn, attn_mine, part_terms, gain_terms, *attn_other
-    )
-    attn_terms = (attn_mine, tuple(attn_other))
-    attn_sum = plan.ring_step(1, attn_terms)
-    terms = plan.terms_first(grad_from_attn)
     part_terms = part_terms + swap(part_terms, "c")
-    attn_sum, out_other, part_terms, *terms = sync(attn_sum, out_other, part_terms, *terms)
-    out_terms = (out_mine, out_other)
-    attn_sum = plan.ring_step(2, attn_terms, attn_sum)
-    out_sum = plan.ring_step(1, out_terms)
-    gain_terms = plan.gain_step(gain_terms, "zh", 3)
-    part_terms = part_terms + swap(part_terms, "zh")
-    terms = plan.terms_second(*terms)
-    grad_w_gate = plan.whole_columns(gate_block)
-    attn_sum, out_sum, gain_terms, part_terms, up_block, grad_w_gate, *terms = sync(
-        attn_sum, out_sum, gain_terms, part_terms, up_block, grad_w_gate, *terms
-    )
-    attn_sum = plan.ring_step(3, attn_terms, attn_sum)
-    out_sum = plan.ring_step(2, out_terms, out_sum)
+    grad_raw, attn_mine, out_mine, out_other, part_terms, gain_terms, *attn_other = sync(
+        grad_raw, attn_mine, out_mine, out_other, part_terms, gain_terms, *attn_other
+    )
+    attn_terms, out_terms = (attn_mine, tuple(attn_other)), (out_mine, out_other)
+    attn_sum, out_sum = plan.ring_step(1, attn_terms), plan.ring_step(1, out_terms)
+    terms = plan.terms_first(by_rows, grad_raw, attn_whole)
+    gain_terms, part_terms = plan.both_step(gain_terms, part_terms, "zh", 3)
+    attn_sum, out_sum, part_terms, gain_terms, *terms = sync(
+        attn_sum, out_sum, part_terms, gain_terms, *terms
+    )
+    attn_sum = plan.ring_sum(2, attn_terms, attn_sum).astype(bf16)
+    out_sum = plan.ring_sum(2, out_terms, out_sum).astype(bf16)
+    attn_sum, out_sum, part_terms, gain_terms, *terms = sync(
+        attn_sum, out_sum, part_terms, gain_terms, *terms
+    )
+    attn_sum, out_sum = plan.shift(attn_sum), plan.shift(out_sum)
+    gain_terms, part_terms = plan.both_step(gain_terms, part_terms, "zl", 3)
     up_block = plan.return_columns(up_block)
-    grad_tokens = grad_hidden + plan.ungrouped(plan.terms_sum(*terms))
-    gain_terms = plan.gain_step(gain_terms, "zl", 3)
-    part_grads = plan.own_gains(part_terms + swap(part_terms, "zl"))
-    attn_sum, out_sum, up_block, gain_terms, part_grads, grad_tokens = sync(
-        attn_sum, out_sum, up_block, gain_terms, part_grads, grad_tokens
-    )
-    attn_block = plan.return_columns(plan.ring_sum(0, attn_terms, attn_sum).astype(bf16))
-    out_sum = plan.ring_step(3, out_terms, out_sum)
-    gain_terms = plan.gain_step(plan.gain_step(gain_terms, "x", 2), "y", 1)
-    grad_w_up = plan.whole_columns(up_block)
-    attn_block, grad_w_up, out_sum, gain_terms = sync(attn_block, grad_w_up, out_sum, gain_terms)
+    terms = plan.terms_added(*terms)
+    attn_sum, out_sum, gain_terms, part_terms, up_block, *terms = sync(
+        attn_sum, out_sum, gain_terms, part_terms, up_block, *terms
+    )
+    attn_sum = plan.ring_sum(3, attn_terms, attn_sum).astype(bf16)
+    out_sum = plan.ring_sum(3, out_terms, out_sum).astype(bf16)
+    attn_sum, out_sum, gate_block, up_block, left, right, left_away, right_away = sync(
+        attn_sum, out_sum, gate_block, up_block, *terms
+    )
+    attn_sum, out_sum = plan.shift(attn_sum), plan.shift(out_sum)
+    left_x, right_y = swap(left_away, "x"), swap(right_away, "y")
+    grad_w_gate, grad_w_up = plan.whole_columns(gate_block), plan.whole_columns(up_block)
+    gain_terms = plan.gain_step(gain_terms, "x", 2)
+    part_grads = plan.own_gains(part_terms)
+    attn_sum, out_sum, gain_terms, part_grads, grad_w_gate, grad_w_up, left_x, right_y = sync(
+        attn_sum, out_sum, gain_terms, part_grads, grad_w_gate, grad_w_up, left_x, right_y
+    )
+    attn_sum = plan.ring_sum(0, attn_terms, attn_sum).astype(bf16)
+    attn_sum, out_sum, gain_terms, left_x, right_y = sync(
+        attn_sum, out_sum, gain_terms, left_x, right_y
+    )
+    grad_tokens = tokens_end(plan.own_order, left, right, left_x, right_y, grad_hidden)
+    attn_block = plan.return_columns(attn_sum)
+    gain_terms = plan.gain_step(gain_terms, "y", 1)
     grad_w_out = plan.ring_sum(0, out_terms, out_sum)
-    grad_w_query, grad_w_key, grad_w_value = (
-        plan.whole_columns(attn_block[..., k * columns : (k + 1) * columns]) for k in range(3)
-    )
+    attn_block, grad_w_out, gain_terms, grad_tokens = sync(
+        attn_block, grad_w_out, gain_terms, grad_tokens
+    )
+    grad_w_query, grad_w_key, grad_w_value = spread_three(attn_block)
     return (
         block_out,
-        grad_tokens.astype(bf16),
+        grad_tokens,
         grad_w_query,
         grad_w_key,
         grad_w_value,

time: 836 us -> 814 us (0.974)
  waiting for transfers between devices: 334 us -> 314 us
  other arithmetic: 81.3 us -> 66 us
    ppermute x12, waiting for transfers between devices: 93.3 us -> 79.4 us  [shift(): return lax.ppermute(value, self.z_axes, ((0, 1), (1, 2), (2, 3), (3, 0)))]
    pallas_call x0 -> x3, Pallas kernels: none -> 12.5 us  [the longest x1 5.66 us: proj_back(): pl.pallas_call(functools.partial(proj_back_kernel, blocks), grid=(4,), in...]
    slice x1 -> x27, local copies, waits for them, and re-layouts: 0.89 us -> 12.9 us  [the longest x10 4.04 us: along_x(): rows.reshape(2, 2, -1, rows.shape[1])[:, place].reshape(-1, rows.shape[1])]
    ppermute x69 -> x67, waiting for transfers between devices: 238 us -> 228 us  [swap(): return lax.ppermute(value, axis, ((0, 1), (1, 0)))]
    add x18 -> x14, other arithmetic: 16.7 us -> 9.67 us  [the longest x3 4.38 us: terms_added(): right = right_mine.astype(f32) + right_other.astype(f32)]
    unnamed x150 -> x172, local copies, waits for them, and re-layouts: 19.3 us -> 24.2 us
    ppermute x69 -> x67, starting transfers between devices: 56 us -> 58.8 us  [swap(): return lax.ppermute(value, axis, ((0, 1), (1, 0)))]
    dot_general x5 -> x14, matrix products: 56.5 us -> 58.7 us  [product_tt(): lax.dot_general(left, right, (((1,), (1,)), ((), ())), preferred_element_...]
  transfers between devices with their start and end apart: 93 -> 91, of which waited for: 49 -> 49; matrix products, arithmetic and copies ran while one was open for 31% -> 31% of each run, Pallas kernels for 7% -> 8%
where the time goes in v4:
time: 814 us; the launch traced here: 807 us
  waiting for transfers between devices  314 us (39%)
  matrix products  174 us (21%)
  starting transfers between devices  94.3 us (12%)
  local copies, waits for them, and re-layouts  72.1 us (9%)
  Pallas kernels  70.9 us (9%)
  other arithmetic  66 us (8%)
  between operations  16 us (2%)
    ppermute x67, waiting for transfers between devices, swap(): return lax.ppermute(value, axis, ((0, 1), (1, 0)))  228 us
    ppermute x12, waiting for transfers between devices, shift(): return lax.ppermute(value, self.z_axes, ((0, 1), (1, 2), (2, 3), (3, 0)))  79.4 us
    dot_general x11, matrix products, inner_rows(): lax.dot_general(left, right, (((0,), (0,)), ((), ())), preferred_element_...  65.6 us
    ppermute x67, starting transfers between devices, swap(): return lax.ppermute(value, axis, ((0, 1), (1, 0)))  58.8 us
    dot_general x14, matrix products, product_tt(): lax.dot_general(left, right, (((1,), (1,)), ((), ())), preferred_element_...  58.7 us
    dot_general x11, matrix products, product(): return jnp.dot(left, right, preferred_element_type=f32)  49.5 us
    unnamed x172, local copies, waits for them, and re-layouts  24.2 us
    pallas_call x1, Pallas kernels, attend_back(): pl.pallas_call(attend_back_kernel, grid=(size,), in_specs=[whole, rows(3...  20.8 us
  transfers between devices with their start and end apart: 91, of which 49 were waited for; matrix products, arithmetic and copies ran while one was open for 31% of the time, Pallas kernels for 8%

profile of v4, /device:TPU:0, one launch (start us, length us, event | category | flops | bytes accessed | tf_op | source)
XLA Modules:
  0.0 807.0 jit_solution(4439764743988623854)
XLA Ops:
  25.3 13.3 %collective-permute-done.refs_2_ = bf16[128,2048]{1,0:T(8,128)(2,1)S(1)} collective-permute-done((bf16[128,2048]{1,0:T(8,128)(2,1)S(1)}, bf16[128,2048]{1,0:T(8,128)(2,1)S(1)}, u32[]{:S(2)}, u32[]{:S(2)}) %collective-permute-start) | collective-permute-done | bytes 524320 | tf_op jit(solution)/shard_map/ppermute | solution.py:198
  42.3 28.5 %collective-permute-done.4.refs_1_ = bf16[256,2048]{1,0:T(8,128)(2,1)} collective-permute-done((bf16[256,2048]{1,0:T(8,128)(2,1)S(1)}, bf16[256,2048]{1,0:T(8,128)(2,1)}, u32[]{:S(2)}, u32[]{:S(2)}) %collective-permute-start.4) | collective-permute-done | bytes 1048608 | tf_op jit(solution)/shard_map/ppermute | solution.py:401
  74.6 8.5 %collective-permute-done.7.refs_6_ = bf16[128,2048]{1,0:T(8,128)(2,1)S(1)} collective-permute-done((bf16[128,2048]{1,0:T(8,128)(2,1)S(1)}, bf16[128,2048]{1,0:T(8,128)(2,1)S(1)}, u32[]{:S(2)}, u32[]{:S(2)}) %collective-permute-start.7) | collective-permute-done | bytes 524320 | tf_op jit(solution)/shard_map/ppermute | solution.py:198
  122.6 12.2 %collective-permute-done.13 = bf16[5,8,64]{2,0,1:T(8,128)(2,1)S(1)} collective-permute-done((bf16[5,8,64]{2,0,1:T(8,128)(2,1)S(1)}, bf16[5,8,64]{2,0,1:T(8,128)(2,1)S(1)}, u32[]{:S(2)}, u32[]{:S(2)}) %collective-permute-start.13) | collective-permute-done | bytes 5152 | tf_op jit(solution)/shard_map/ppermute | solution.py:198
  152.1 6.6 fusion.129.raw_ref
  169.9 12.4 %shard_map.276 = (bf16[1024,1536]{1,0:T(8,128)(2,1)}, bf16[1024,512]{1,0:T(8,128)(2,1)}) custom-call(s32[4,2]{1,0:T(4,128)} %slice_convert_fusion.9.lengths_ref, f32[1024,1536]{1,0:T(8,128)} %copy-done.19, f32[1024,2]{1,0:T(8,128)} %bitcast.181, f32[2,512]{1,0:T(2,128)} %constant_dynamic-slice_fusion.21.gains_ref, f32[1024,128]{1,0:T(8,128)} %pad_maximum_fusion.4.cosine_ref, ...), custom_call_target="tpu_custom_call" | custom-call | tf_op jit(solution)/shard_map/pallas_call | solution.py:162
  187.9 22.5 %collective-permute-done.18 = bf16[512,1024]{1,0:T(8,128)(2,1)S(1)} collective-permute-done((bf16[512,1024]{1,0:T(8,128)(2,1)S(1)}, bf16[512,1024]{1,0:T(8,128)(2,1)S(1)}, u32[]{:S(2)}, u32[]{:S(2)}) %collective-permute-start.18) | collective-permute-done | bytes 1048608 | tf_op jit(solution)/shard_map/ppermute | solution.py:198
  215.3 7.8 collective-permute-done.19
  236.5 10.8 %collective-permute-done.22.refs_2_ = bf16[128,2048]{1,0:T(8,128)(2,1)S(1)} collective-permute-done((bf16[128,2048]{1,0:T(8,128)(2,1)S(1)}, bf16[128,2048]{1,0:T(8,128)(2,1)S(1)}, u32[]{:S(2)}, u32[]{:S(2)}) %collective-permute-start.22) | collective-permute-done | bytes 524320 | tf_op jit(solution)/shard_map/ppermute | solution.py:198
  249.4 9.2 %collective-permute-done.23.refs_3_ = bf16[128,2048]{1,0:T(8,128)(2,1)} collective-permute-done((bf16[128,2048]{1,0:T(8,128)(2,1)S(1)}, bf16[128,2048]{1,0:T(8,128)(2,1)}, u32[]{:S(2)}, u32[]{:S(2)}) %collective-permute-start.23) | collective-permute-done | bytes 524320 | tf_op jit(solution)/shard_map/ppermute | solution.py:198
  273.4 13.8 %convolution_convert_fusion.1 = bf16[1024,2048]{1,0:T(8,128)(2,1)} fusion(bf16[1024,2048]{1,0:T(8,128)(2,1)} %copy-done.3, bf16[2048,2048]{1,0:T(8,128)(2,1)} %all-gather.6.cloned.1.call-done), kind=kOutput, calls=%fused_computation.26 | convolution fusion | flops 8592031744 | bytes 16777216 | tf_op jit(solution)/shard_map/dot_general | solution.py:21
  287.2 18.4 %collective-permute-done.28.refs_2_ = bf16[256,2048]{1,0:T(8,128)(2,1)} collective-permute-done((bf16[256,2048]{1,0:T(8,128)(2,1)}, bf16[256,2048]{1,0:T(8,128)(2,1)}, u32[]{:S(2)}, u32[]{:S(2)}) %collective-permute-start.28) | collective-permute-done | bytes 1048608 | tf_op jit(solution)/shard_map/ppermute | solution.py:401
  305.6 15.5 %fusion = (bf16[1024,2048]{1,0:T(8,128)(2,1)S(1)}, bf16[1024,2048]{1,0:T(8,128)(2,1)}) fusion(bf16[1024,2048]{1,0:T(8,128)(2,1)} %convolution_convert_fusion.1, bf16[1024,2048]{1,0:T(8,128)(2,1)} %copy-done.3, bf16[2048,2048]{1,0:T(8,128)(2,1)} %all-gather.8.cloned.1.call-done), kind=kOutput, calls=%fused_computation.5 | convolution fusion | flops 8608808960 | bytes 25165824 | tf_op jit(solution)/shard_map/dot_general | solution.py:21
  321.1 8.8 %collective-permute-done.29.refs_3_ = bf16[256,2048]{1,0:T(8,128)(2,1)S(1)} collective-permute-done((bf16[256,2048]{1,0:T(8,128)(2,1)}, bf16[256,2048]{1,0:T(8,128)(2,1)S(1)}, u32[]{:S(2)}, u32[]{:S(2)}) %collective-permute-start.29) | collective-permute-done | bytes 1048608 | tf_op jit(solution)/shard_map/ppermute | solution.py:401
  349.0 18.0 %collective-permute-done.34 = bf16[512,1024]{1,0:T(8,128)(2,1)S(1)} collective-permute-done((bf16[512,1024]{1,0:T(8,128)(2,1)S(1)}, bf16[512,1024]{1,0:T(8,128)(2,1)S(1)}, u32[]{:S(2)}, u32[]{:S(2)}) %collective-permute-start.34) | collective-permute-done | bytes 1048608 | tf_op jit(solution)/shard_map/ppermute | solution.py:198
  373.3 9.8 %collective-permute-done.36 = bf16[256,1024]{1,0:T(8,128)(2,1)} collective-permute-done((bf16[256,1024]{1,0:T(8,128)(2,1)}, bf16[256,1024]{1,0:T(8,128)(2,1)}, u32[]{:S(2)}, u32[]{:S(2)}) %collective-permute-start.36) | collective-permute-done | bytes 524320 | tf_op jit(solution)/shard_map/ppermute | solution.py:198
  394.4 10.8 %collective-permute-done.38.refs_2_ = bf16[128,2048]{1,0:T(8,128)(2,1)S(1)} collective-permute-done((bf16[128,2048]{1,0:T(8,128)(2,1)S(1)}, bf16[128,2048]{1,0:T(8,128)(2,1)S(1)}, u32[]{:S(2)}, u32[]{:S(2)}) %collective-permute-start.38) | collective-permute-done | bytes 524320 | tf_op jit(solution)/shard_map/ppermute | solution.py:198
  407.2 9.2 %collective-permute-done.39.refs_3_ = bf16[128,2048]{1,0:T(8,128)(2,1)S(1)} collective-permute-done((bf16[128,2048]{1,0:T(8,128)(2,1)S(1)}, bf16[128,2048]{1,0:T(8,128)(2,1)S(1)}, u32[]{:S(2)}, u32[]{:S(2)}) %collective-permute-start.39) | collective-permute-done | bytes 524320 | tf_op jit(solution)/shard_map/ppermute | solution.py:198
  417.2 8.2 %collective-permute-done.42.refs_6_ = bf16[128,2048]{1,0:T(8,128)(2,1)S(1)} collective-permute-done((bf16[128,2048]{1,0:T(8,128)(2,1)S(1)}, bf16[128,2048]{1,0:T(8,128)(2,1)S(1)}, u32[]{:S(2)}, u32[]{:S(2)}) %collective-permute-start.42) | collective-permute-done | bytes 524320 | tf_op jit(solution)/shard_map/ppermute | solution.py:198
  433.4 7.0 convolution_convert_fusion.7
  448.3 18.4 %multiply_convert_fusion = (bf16[1024,2048]{1,0:T(8,128)(2,1)S(1)}, bf16[1024,2048]{1,0:T(8,128)(2,1)S(1)}) fusion(bf16[1024,2048]{1,0:T(8,128)(2,1)} %convolution_convert_fusion.1, bf16[1024,2048]{1,0:T(8,128)(2,1)} %get-tuple-element.476, bf16[1024,2048]{1,0:T(8,128)(2,1)} %copy-done.6, bf16[2048,2048]{1,0:T(8,128)(2,1)} %copy-done.4), kind=kOutput, calls=%fused_computation.15 | convolution fusion | flops 8621391872 | bytes 29360128 | tf_op jit(solution)/shard_map/dot_general | solution.py:25
  510.4 7.8 add_convert_fusion.1
  518.2 12.2 %collective-permute-done.47 = bf16[512,1024]{1,0:T(8,128)(2,1)S(1)} collective-permute-done((bf16[512,1024]{1,0:T(8,128)(2,1)}, bf16[512,1024]{1,0:T(8,128)(2,1)S(1)}, u32[]{:S(2)}, u32[]{:S(2)}) %collective-permute-start.47) | collective-permute-done | bytes 1048608 | tf_op jit(solution)/shard_map/ppermute | solution.py:198
  563.9 9.4 %convolution_convert_fusion.3 = bf16[1024,2048]{1,0:T(8,128)(2,1)} fusion(bf16[1024,1024]{1,0:T(8,128)(2,1)} %get-tuple-element.288, bf16[1024,2048]{1,0:T(8,128)(2,1)} %copy-done.40), kind=kOutput, calls=%fused_computation.28 | convolution fusion | flops 4297064448 | bytes 10485760 | tf_op jit(solution)/shard_map/dot_general | solution.py:29
  581.3 7.8 add_convert_fusion
  592.9 9.5 %collective-permute-done.56.refs_6_ = bf16[128,2048]{1,0:T(8,128)(2,1)} collective-permute-done((bf16[128,2048]{1,0:T(8,128)(2,1)S(1)}, bf16[128,2048]{1,0:T(8,128)(2,1)}, u32[]{:S(2)}, u32[]{:S(2)}) %collective-permute-start.56) | collective-permute-done | bytes 524320 | tf_op jit(solution)/shard_map/ppermute | solution.py:198
  616.0 20.8 %shard_map.283 = (f32[1024,1024]{1,0:T(8,128)}, bf16[1024,512]{1,0:T(8,128)(2,1)}, f32[1024,2]{1,0:T(8,128)}, f32[2,512]{1,0:T(2,128)}) custom-call(s32[4,2]{1,0:T(4,128)} %slice_convert_fusion.9.lengths_ref, f32[1024,1536]{1,0:T(8,128)} %copy-done.19, bf16[1024,1536]{1,0:T(8,128)(2,1)} %get-tuple-element.266.turned_ref, f32[1024,2]{1,0:T(8,128)} %bitcast.182, ...), custom_call_target="tpu_custom_call" | custom-call | tf_op jit(solution)/shard_map/pallas_call | solution.py:179
  643.4 7.4 collective-permute-done.59
  673.8 7.5 convolution_convert_fusion.2
  706.1 14.1 %collective-permute-done.67 = f32[2048]{0:T(1024)S(1)} collective-permute-done((f32[2048]{0:T(1024)S(1)}, f32[2048]{0:T(1024)S(1)}, u32[]{:S(2)}, u32[]{:S(2)}) %collective-permute-start.67) | collective-permute-done | bytes 8224 | tf_op jit(solution)/shard_map/ppermute | solution.py:198
  737.7 9.5 %collective-permute-done.72 = f32[1536]{0:T(1024)S(1)} collective-permute-done((f32[1536]{0:T(1024)S(1)}, f32[1536]{0:T(1024)S(1)}, u32[]{:S(2)}, u32[]{:S(2)}) %collective-permute-start.72) | collective-permute-done | bytes 6176 | tf_op jit(solution)/shard_map/ppermute | solution.py:198
  767.3 13.0 %collective-permute-done.74 = bf16[64,2048]{1,0:T(8,128)(2,1)S(1)} collective-permute-done((bf16[64,2048]{1,0:T(8,128)(2,1)}, bf16[64,2048]{1,0:T(8,128)(2,1)S(1)}, u32[]{:S(2)}, u32[]{:S(2)}) %collective-permute-start.74) | collective-permute-done | bytes 262176 | tf_op jit(solution)/shard_map/ppermute | solution.py:401
  (550 shorter events, 402.2 us)
Async XLA Ops:
  7.2 104.8 %all-gather.4.cloned.1.call-start = ((), (), s32[]{:S(2)}) async-start(), calls=%async_computation.9 | async-start | bytes 2949120 | tf_op jit(solution)/shard_map/all_gather | solution.py:727
  11.3 27.3 %all-to-all-start = ((bf16[4,64,1536]{2,1,0:T(8,128)(2,1)}), bf16[4,64,1536]{2,1,0:T(8,128)(2,1)S(1)}, u32[]{:S(2)}, u32[]{:S(2)}) async-start(bf16[4,64,1536]{2,1,0:T(8,128)(2,1)} %pad_maximum_fusion.3), calls=%async_computation | async-start | bytes 1572864 | tf_op jit(solution)/shard_map/all_to_all | solution.py:465
  23.7 47.1 %collective-permute-start.4 = (bf16[256,2048]{1,0:T(8,128)(2,1)S(1)}, bf16[256,2048]{1,0:T(8,128)(2,1)}, u32[]{:S(2)}, u32[]{:S(2)}) collective-permute-start(bf16[256,2048]{1,0:T(8,128)(2,1)S(1)} %copy-done.8), channel_id=1, source_target_pairs={{0,1},{1,2},{2,3},{3,0},{4,5},{5,6},{6,7},{7,4},{8,9},{9,10},{10,1... | collective-permute-start | bytes 3145736 | tf_op jit(solution)/shard_map/ppermute | solution.py:401
  38.7 33.4 %collective-permute-start.5 = (bf16[128,2048]{1,0:T(8,128)(2,1)S(1)}, bf16[128,2048]{1,0:T(8,128)(2,1)S(1)}, u32[]{:S(2)}, u32[]{:S(2)}) collective-permute-start(bf16[128,2048]{1,0:T(8,128)(2,1)S(1)} %get-tuple-element.226.refs_1_), channel_id=1, source_target_pairs={{0,8},{8,0},{1,9},{9,1},{2,10},{10,2},{3,11},{11,3},{4,12},{12,4},... | collective-permute-start | bytes 1572872 | tf_op jit(solution)/shard_map/ppermute | solution.py:198
  40.1 46.7 %collective-permute-start.2 = (bf16[256,1536]{1,0:T(8,128)(2,1)S(1)}, bf16[256,1536]{1,0:T(8,128)(2,1)}, u32[]{:S(2)}, u32[]{:S(2)}) collective-permute-start(bf16[256,1536]{1,0:T(8,128)(2,1)S(1)} %bitcast.176), channel_id=1, source_target_pairs={{0,1},{1,2},{2,3},{3,0},{4,5},{5,6},{6,7},{7,4},{8,9},{9,10},{10,1... | collective-permute-start | bytes 2359304 | tf_op jit(solution)/shard_map/ppermute | solution.py:401
  41.7 45.1 %collective-permute-start.3 = (bf16[256,1536]{1,0:T(8,128)(2,1)S(1)}, bf16[256,1536]{1,0:T(8,128)(2,1)S(1)}, u32[]{:S(2)}, u32[]{:S(2)}) collective-permute-start(bf16[256,1536]{1,0:T(8,128)(2,1)S(1)} %bitcast.177), channel_id=1, source_target_pairs={{0,4},{4,0},{1,5},{5,1},{2,6},{6,2},{3,7},{7,3},{8,12},{12,8},{9,1... | collective-permute-start | bytes 2359304 | tf_op jit(solution)/shard_map/ppermute | solution.py:198
  41.7 32.1 %collective-permute-start.6 = (bf16[128,2048]{1,0:T(8,128)(2,1)S(1)}, bf16[128,2048]{1,0:T(8,128)(2,1)S(1)}, u32[]{:S(2)}, u32[]{:S(2)}) collective-permute-start(bf16[128,2048]{1,0:T(8,128)(2,1)S(1)} %get-tuple-element.225.refs_0_), channel_id=1, source_target_pairs={{0,16},{16,0},{1,17},{17,1},{2,18},{18,2},{3,19},{19,3},{4,20},{20... | collective-permute-start | bytes 1572872 | tf_op jit(solution)/shard_map/ppermute | solution.py:198
  97.4 176.0 %all-gather.6.cloned.1.call-start = ((), (), s32[]{:S(2)}) async-start(), calls=%async_computation.10 | async-start | bytes 9437184 | tf_op jit(solution)/shard_map/all_gather | solution.py:727
  112.0 30.7 %collective-permute-start.11 = (bf16[256,1536]{1,0:T(8,128)(2,1)}, bf16[256,1536]{1,0:T(8,128)(2,1)}, u32[]{:S(2)}, u32[]{:S(2)}) collective-permute-start(bf16[256,1536]{1,0:T(8,128)(2,1)} %collective-permute-done.9.refs_2_), channel_id=1, source_target_pairs={{0,1},{1,2},{2,3},{3,0},{4,5},{5,6},{6,7},{7,4},{8,9},{9,10},{10,1... | collective-permute-start | bytes 2359304 | tf_op jit(solution)/shard_map/ppermute | solution.py:401
  112.1 30.6 %collective-permute-start.12 = (bf16[256,1536]{1,0:T(8,128)(2,1)}, bf16[256,1536]{1,0:T(8,128)(2,1)}, u32[]{:S(2)}, u32[]{:S(2)}) collective-permute-start(bf16[256,1536]{1,0:T(8,128)(2,1)} %collective-permute-done.9.refs_2_), channel_id=1, source_target_pairs={{0,4},{4,0},{1,5},{5,1},{2,6},{6,2},{3,7},{7,3},{8,12},{12,8},{9,1... | collective-permute-start | bytes 2359304 | tf_op jit(solution)/shard_map/ppermute | solution.py:198
  119.9 185.7 %all-gather.8.cloned.1.call-start = ((), (), s32[]{:S(2)}) async-start(), calls=%async_computation.11 | async-start | bytes 9437184 | tf_op jit(solution)/shard_map/all_gather | solution.py:727
  142.7 434.5 %reduce-scatter.4.cloned.1.call-start = ((), (), s32[]{:S(2)}) async-start(), calls=%async_computation.12 | async-start | bytes 5242880 | tf_op jit(solution)/shard_map/reduce_scatter | solution.py:819
  235.2 27.3 %collective-permute-start.24 = (bf16[128,2048]{1,0:T(8,128)(2,1)S(1)}, bf16[128,2048]{1,0:T(8,128)(2,1)}, u32[]{:S(2)}, u32[]{:S(2)}) collective-permute-start(bf16[128,2048]{1,0:T(8,128)(2,1)S(1)} %get-tuple-element.443.refs_0_), channel_id=1, source_target_pairs={{0,16},{16,0},{1,17},{17,1},{2,18},{18,2},{3,19},{19,3},{4,20},{20... | collective-permute-start | bytes 1572872 | tf_op jit(solution)/shard_map/ppermute | solution.py:198
  249.4 83.3 %collective-permute-start.30 = (bf16[256,2048]{1,0:T(8,128)(2,1)S(1)}, bf16[256,2048]{1,0:T(8,128)(2,1)}, u32[]{:S(2)}, u32[]{:S(2)}) collective-permute-start(bf16[256,2048]{1,0:T(8,128)(2,1)S(1)} %copy-done.8), channel_id=1, source_target_pairs={{0,4},{4,0},{1,5},{5,1},{2,6},{6,2},{3,7},{7,3},{8,12},{12,8},{9,1... | collective-permute-start | bytes 3145736 | tf_op jit(solution)/shard_map/ppermute | solution.py:198
  258.6 47.0 %collective-permute-start.28 = (bf16[256,2048]{1,0:T(8,128)(2,1)}, bf16[256,2048]{1,0:T(8,128)(2,1)}, u32[]{:S(2)}, u32[]{:S(2)}) collective-permute-start(bf16[256,2048]{1,0:T(8,128)(2,1)} %collective-permute-done.4.refs_1_), channel_id=1, source_target_pairs={{0,1},{1,2},{2,3},{3,0},{4,5},{5,6},{6,7},{7,4},{8,9},{9,10},{10,1... | collective-permute-start | bytes 3145736 | tf_op jit(solution)/shard_map/ppermute | solution.py:401
  262.5 70.2 %collective-permute-start.31 = (bf16[256,2048]{1,0:T(8,128)(2,1)}, bf16[256,2048]{1,0:T(8,128)(2,1)}, u32[]{:S(2)}, u32[]{:S(2)}) collective-permute-start(bf16[256,2048]{1,0:T(8,128)(2,1)} %collective-permute-done.4.refs_1_), channel_id=1, source_target_pairs={{0,4},{4,0},{1,5},{5,1},{2,6},{6,2},{3,7},{7,3},{8,12},{12,8},{9,1... | collective-permute-start | bytes 3145736 | tf_op jit(solution)/shard_map/ppermute | solution.py:198
  305.6 27.1 %collective-permute-start.32 = (bf16[256,2048]{1,0:T(8,128)(2,1)}, bf16[256,2048]{1,0:T(8,128)(2,1)}, u32[]{:S(2)}, u32[]{:S(2)}) collective-permute-start(bf16[256,2048]{1,0:T(8,128)(2,1)} %collective-permute-done.28.refs_2_), channel_id=1, source_target_pairs={{0,4},{4,0},{1,5},{5,1},{2,6},{6,2},{3,7},{7,3},{8,12},{12,8},{9,1... | collective-permute-start | bytes 3145736 | tf_op jit(solution)/shard_map/ppermute | solution.py:198
  341.3 25.6 %collective-permute-start.34 = (bf16[512,1024]{1,0:T(8,128)(2,1)S(1)}, bf16[512,1024]{1,0:T(8,128)(2,1)S(1)}, u32[]{:S(2)}, u32[]{:S(2)}) collective-permute-start(bf16[512,1024]{1,0:T(8,128)(2,1)S(1)} %fusion.78), channel_id=1, source_target_pairs={{0,16},{16,0},{1,17},{17,1},{2,18},{18,2},{3,19},{19,3},{4,20},{20... | collective-permute-start | bytes 3145736 | tf_op jit(solution)/shard_map/ppermute | solution.py:198
  343.0 25.3 %collective-permute-start.35 = (bf16[512,1024]{1,0:T(8,128)(2,1)S(1)}, bf16[512,1024]{1,0:T(8,128)(2,1)S(1)}, u32[]{:S(2)}, u32[]{:S(2)}) collective-permute-start(bf16[512,1024]{1,0:T(8,128)(2,1)S(1)} %fusion.83), channel_id=1, source_target_pairs={{0,8},{8,0},{1,9},{9,1},{2,10},{10,2},{3,11},{11,3},{4,12},{12,4},... | collective-permute-start | bytes 3145736 | tf_op jit(solution)/shard_map/ppermute | solution.py:198
  447.3 158.2 %reduce-scatter.6.cloned.1.call-start = ((), (), s32[]{:S(2)}) async-start(), calls=%async_computation.13 | async-start | bytes 5242880 | tf_op jit(solution)/shard_map/reduce_scatter | solution.py:851
  479.7 30.7 %collective-permute-start.46 = (bf16[1024,2048]{1,0:T(8,128)(2,1)}, bf16[1024,2048]{1,0:T(8,128)(2,1)}, u32[]{:S(2)}, u32[]{:S(2)}) collective-permute-start(bf16[1024,2048]{1,0:T(8,128)(2,1)} %convolution_convert_fusion.5), channel_id=1, source_target_pairs={{0,4},{4,0},{1,5},{5,1},{2,6},{6,2},{3,7},{7,3},{8,12},{12,8},{9,1... | collective-permute-start | bytes 12582920 | tf_op jit(solution)/shard_map/ppermute | solution.py:198
  504.9 25.4 %collective-permute-start.47 = (bf16[512,1024]{1,0:T(8,128)(2,1)}, bf16[512,1024]{1,0:T(8,128)(2,1)S(1)}, u32[]{:S(2)}, u32[]{:S(2)}) collective-permute-start(bf16[512,1024]{1,0:T(8,128)(2,1)} %add_convert_fusion.6), channel_id=1, source_target_pairs={{0,16},{16,0},{1,17},{17,1},{2,18},{18,2},{3,19},{19,3},{4,20},{20... | collective-permute-start | bytes 3145736 | tf_op jit(solution)/shard_map/ppermute | solution.py:198
  505.8 25.2 %collective-permute-start.48 = (bf16[512,1024]{1,0:T(8,128)(2,1)}, bf16[512,1024]{1,0:T(8,128)(2,1)S(1)}, u32[]{:S(2)}, u32[]{:S(2)}) collective-permute-start(bf16[512,1024]{1,0:T(8,128)(2,1)} %add_convert_fusion.5), channel_id=1, source_target_pairs={{0,8},{8,0},{1,9},{9,1},{2,10},{10,2},{3,11},{11,3},{4,12},{12,4},... | collective-permute-start | bytes 3145736 | tf_op jit(solution)/shard_map/ppermute | solution.py:198
  531.9 41.4 %collective-permute-start.51 = (bf16[1024,2048]{1,0:T(8,128)(2,1)}, bf16[1024,2048]{1,0:T(8,128)(2,1)}, u32[]{:S(2)}, u32[]{:S(2)}) collective-permute-start(bf16[1024,2048]{1,0:T(8,128)(2,1)} %convolution_convert_fusion.4), channel_id=1, source_target_pairs={{0,4},{4,0},{1,5},{5,1},{2,6},{6,2},{3,7},{7,3},{8,12},{12,8},{9,1... | collective-permute-start | bytes 12582920 | tf_op jit(solution)/shard_map/ppermute | solution.py:198
  560.5 49.2 %collective-permute-start.58 = (f32[2,2,2,2,64]{4,3,2,1,0:T(2,128)S(1)}, f32[2,2,2,2,64]{4,3,2,1,0:T(2,128)S(1)}, u32[]{:S(2)}, u32[]{:S(2)}) collective-permute-start(f32[2,2,2,2,64]{4,3,2,1,0:T(2,128)S(1)} %fusion.112), channel_id=1, source_target_pairs={{0,4},{4,0},{1,5},{5,1},{2,6},{6,2},{3,7},{7,3},{8,12},{12,8},{9,1... | collective-permute-start | bytes 12296 | tf_op jit(solution)/shard_map/ppermute | solution.py:198
  605.4 31.4 %all-to-all-start.3 = ((bf16[4,64,2048]{2,1,0:T(8,128)(2,1)}), bf16[4,64,2048]{2,1,0:T(8,128)(2,1)}, u32[]{:S(2)}, u32[]{:S(2)}) async-start(bf16[4,64,2048]{2,1,0:T(8,128)(2,1)} %bitcast.212), calls=%async_computation.5 | async-start | bytes 2097152 | tf_op jit(solution)/shard_map/all_to_all | solution.py:468
  609.7 114.9 %reduce-scatter.8.cloned.1.call-start = ((), (), s32[]{:S(2)}) async-start(), calls=%async_computation.14 | async-start | bytes 5242880 | tf_op jit(solution)/shard_map/reduce_scatter | solution.py:864
  688.2 32.1 %collective-permute-start.68 = (bf16[512,1024]{1,0:T(8,128)(2,1)}, bf16[512,1024]{1,0:T(8,128)(2,1)}, u32[]{:S(2)}, u32[]{:S(2)}) collective-permute-start(bf16[512,1024]{1,0:T(8,128)(2,1)} %fusion.62), channel_id=1, source_target_pairs={{0,16},{16,0},{1,17},{17,1},{2,18},{18,2},{3,19},{19,3},{4,20},{20... | collective-permute-start | bytes 3145736 | tf_op jit(solution)/shard_map/ppermute | solution.py:198
  689.7 30.7 %collective-permute-start.69 = (bf16[512,1024]{1,0:T(8,128)(2,1)}, bf16[512,1024]{1,0:T(8,128)(2,1)}, u32[]{:S(2)}, u32[]{:S(2)}) collective-permute-start(bf16[512,1024]{1,0:T(8,128)(2,1)} %fusion.67), channel_id=1, source_target_pairs={{0,8},{8,0},{1,9},{9,1},{2,10},{10,2},{3,11},{11,3},{4,12},{12,4},... | collective-permute-start | bytes 3145736 | tf_op jit(solution)/shard_map/ppermute | solution.py:198
  693.2 27.1 %collective-permute-start.65 = (bf16[256,1536]{1,0:T(8,128)(2,1)}, bf16[256,1536]{1,0:T(8,128)(2,1)}, u32[]{:S(2)}, u32[]{:S(2)}) collective-permute-start(bf16[256,1536]{1,0:T(8,128)(2,1)} %add_convert_fusion.10), channel_id=1, source_target_pairs={{0,1},{1,2},{2,3},{3,0},{4,5},{5,6},{6,7},{7,4},{8,9},{9,10},{10,1... | collective-permute-start | bytes 2359304 | tf_op jit(solution)/shard_map/ppermute | solution.py:401
  724.5 25.8 %collective-permute-start.70 = (bf16[256,1536]{1,0:T(8,128)(2,1)}, bf16[256,1536]{1,0:T(8,128)(2,1)}, u32[]{:S(2)}, u32[]{:S(2)}) collective-permute-start(bf16[256,1536]{1,0:T(8,128)(2,1)} %add_convert_fusion.9), channel_id=1, source_target_pairs={{0,1},{1,2},{2,3},{3,0},{4,5},{5,6},{6,7},{7,4},{8,9},{9,10},{10,1... | collective-permute-start | bytes 2359304 | tf_op jit(solution)/shard_map/ppermute | solution.py:401
  724.5 25.8 %all-to-all-start.4 = ((bf16[4,64,2048]{2,1,0:T(8,128)(2,1)}), bf16[4,64,2048]{2,1,0:T(8,128)(2,1)S(1)}, u32[]{:S(2)}, u32[]{:S(2)}) async-start(bf16[4,64,2048]{2,1,0:T(8,128)(2,1)} %bitcast.211), calls=%async_computation.7 | async-start | bytes 2097152 | tf_op jit(solution)/shard_map/all_to_all | solution.py:468
  (143 other events, 1350.2 us)
Sparse Core Ops, SparseCore 0:
  11.5 55.6 all-gather.3
  112.2 90.5 all-gather.5
  204.4 95.0 all-gather.7
  447.4 73.7 reduce-scatter.3
  531.1 74.3 reduce-scatter.5
  612.5 77.7 reduce-scatter.7

commit v5 on v4

--- a/solution.py
+++ b/solution.py
@@ -278,60 +278,37 @@
     )(parts)
 
 
-def proj_back_kernel(
-    halves, top_ref, low_ref, top_x_ref, low_y_ref, live_ref, cotangent_ref, proj_ref, inverse_ref,
-    gain_ref, hidden_ref, grad_top_ref, grad_low_ref, term_ref,
-):
-    parts = ((top_ref, top_x_ref, grad_top_ref), (low_ref, low_y_ref, grad_low_ref))
-    gain = gain_ref[...]
-    term = 0.0
-    for half, (mine_ref, other_ref, grad_ref) in enumerate(parts):
-        total = mine_ref[...] + other_ref[...].astype(f32)
-        blocks = [total[:, k * 64 : (k + 1) * 64] for k in halves]
-        total = jnp.concatenate(blocks, axis=1)
-        total += live_ref[half] * cotangent_ref[half].astype(f32)
-        hidden_ref[half] = total
-        normed = proj_ref[half] * inverse_ref[half]
-        term += jnp.sum(total * normed, axis=0, keepdims=True)
-        scaled = total * gain
-        mean = jnp.mean(scaled * normed, axis=-1, keepdims=True)
-        grad_ref[...] = (inverse_ref[half] * (scaled - normed * mean)).astype(bf16)
-    first = pl.program_id(0) == 0
-    term_ref[...] = jnp.where(first, term, term_ref[...] + term)
-
-
-def ordered(blocks, left_ref, right_ref, left_x_ref, right_y_ref):
-    left = left_ref[...] + left_x_ref[...].astype(f32)
-    right = right_ref[...] + right_y_ref[...].astype(f32)
+def ordered(blocks, *refs):
+    left = sum(ref[...].astype(f32) for ref in refs[0::2])
+    right = sum(ref[...].astype(f32) for ref in refs[1::2])
     half = left.shape[1] // 64
     parts = [(left, k) if k < half else (right, k - half) for k in blocks]
     return jnp.concatenate([part[:, k * 64 : (k + 1) * 64] for part, k in parts], axis=1)
 
 
-def tokens_kernel(blocks, left_ref, right_ref, left_x_ref, right_y_ref, hidden_ref, out_ref):
-    total = ordered(blocks, left_ref, right_ref, left_x_ref, right_y_ref)
-    out_ref[...] = (total + hidden_ref[...]).astype(bf16)
-
-
-def tokens_end(blocks, left, right, left_x, right_y, hidden):
+def tokens_kernel(blocks, *refs):
+    *sides, hidden_ref, out_ref = refs
+    out_ref[...] = (ordered(blocks, *sides) + hidden_ref[...]).astype(bf16)
+
+
+def tokens_end(blocks, sides, hidden):
     rows, width = hidden.shape
     side = pl.BlockSpec((rows // 4, width // 2), lambda k: (k, 0))
     whole = pl.BlockSpec((rows // 4, width), lambda k: (k, 0))
     return pl.pallas_call(
         functools.partial(tokens_kernel, blocks),
         grid=(4,),
-        in_specs=[side, side, side, side, whole],
+        in_specs=[side] * len(sides) + [whole],
         out_specs=whole,
         out_shape=jax.ShapeDtypeStruct((rows, width), bf16),
         cost_estimate=NO_COST,
-    )(left, right, left_x, right_y, hidden)
-
-
-def proj_back_kernel(
-    blocks, left_ref, right_ref, left_x_ref, right_y_ref, live_ref, cotangent_ref, proj_ref,
-    inverse_ref, gain_ref, hidden_ref, grad_ref, term_ref,
-):
-    total = ordered(blocks, left_ref, right_ref, left_x_ref, right_y_ref)
+    )(*sides, hidden)
+
+
+def proj_back_kernel(blocks, *refs):
+    *sides, live_ref, cotangent_ref, proj_ref, inverse_ref, gain_ref = refs[:-3]
+    hidden_ref, grad_ref, term_ref = refs[-3:]
+    total = ordered(blocks, *sides)
     total += live_ref[...] * cotangent_ref[...].astype(f32)
     hidden_ref[...] = total
     normed = proj_ref[...] * inverse_ref[...]
@@ -343,7 +320,7 @@
     term_ref[...] = jnp.where(first, term, term_ref[...] + term)
 
 
-def proj_back(blocks, left, right, left_x, right_y, live, cotangent, proj, inverse, gain):
+def proj_back(blocks, sides, live, cotangent, proj, inverse, gain):
     rows, width = proj.shape
     side = pl.BlockSpec((rows // 4, width // 2), lambda k: (k, 0))
     whole = pl.BlockSpec((rows // 4, width), lambda k: (k, 0))
@@ -352,7 +329,7 @@
     hidden, grad, term = pl.pallas_call(
         functools.partial(proj_back_kernel, blocks),
         grid=(4,),
-        in_specs=[side, side, side, side, column, whole, whole, column, line],
+        in_specs=[side] * len(sides) + [column, whole, whole, column, line],
         out_specs=[whole, whole, line],
         out_shape=[
             jax.ShapeDtypeStruct((rows, width), f32),
@@ -360,7 +337,7 @@
             jax.ShapeDtypeStruct((1, width), f32),
         ],
         cost_estimate=NO_COST,
-    )(left, right, left_x, right_y, live, cotangent, proj, inverse, gain.reshape(1, width))
+    )(*sides, live, cotangent, proj, inverse, gain.reshape(1, width))
     return hidden, grad, term[0]
 
 
@@ -429,17 +406,22 @@
         return left_mine, right_mine, left_other, right_other
 
     def terms_added(self, left_mine, right_mine, left_other, right_other):
-        left = left_mine.astype(f32) + left_other.astype(f32)
-        right = right_mine.astype(f32) + right_other.astype(f32)
-        half = left.shape[0] // 2
-        return left[:half], right[:half], left[half:].astype(bf16), right[half:].astype(bf16)
+        half = left_mine.shape[0] // 2
+        left_away = left_mine[half:].astype(f32) + left_other[half:].astype(f32)
+        right_away = right_mine[half:].astype(f32) + right_other[half:].astype(f32)
+        stay = (left_mine, right_mine, left_other, right_other)
+        return (*stay, left_away.astype(bf16), right_away.astype(bf16))
 
     def terms_second(self, *terms):
-        left, right, left_away, right_away = self.terms_added(*terms)
-        return left, right, swap(left_away, "x"), swap(right_away, "y")
-
-    def terms_sum(self, left, right, left_x, right_y):
-        return jnp.concatenate([left + left_x.astype(f32), right + right_y.astype(f32)], axis=1)
+        *stay, left_away, right_away = self.terms_added(*terms)
+        return (*stay, swap(left_away, "x"), swap(right_away, "y"))
+
+    def terms_sum(self, left_mine, right_mine, left_other, right_other, left_x, right_y):
+        half = left_x.shape[0]
+        left = (left_mine[:half], left_other[:half], left_x)
+        right = (right_mine[:half], right_other[:half], right_y)
+        sums = [sum(part.astype(f32) for part in parts) for parts in (left, right)]
+        return jnp.concatenate(sums, axis=1)
 
     def sum_along(self, rows, axis):
         shape = rows.shape
@@ -596,6 +578,45 @@
         grad = scale * (scaled[:, here] - normed * means[:, which : which + 1])
         grads.append(grad.astype(bf16))
     return jnp.concatenate(grads + [grad_value], axis=1)
+
+
+def pair_kernel(first_y, second_y, first_x, second_x, first_w, second_w, left_ref, right_ref):
+    def terms(first, second):
+        first, second = (ref[...].reshape(-1, ref.shape[-1]) for ref in (first, second))
+        total = product_tt(first, first_w[...]) + product_tt(second, second_w[...])
+        return total.astype(bf16)
+
+    step = pl.program_id(0)
+
+    @pl.when(step < pl.num_programs(0) // 2)
+    def _():
+        left_ref[...] = terms(first_y, second_y)
+
+    @pl.when(step >= pl.num_programs(0) // 2)
+    def _():
+        right_ref[...] = terms(first_x, second_x)
+
+
+def pair_terms(place, first, second, first_whole, second_whole):
+    rows, inner = first.shape
+    width = first_whole.shape[0]
+    quarter, tile = rows // 4, 256
+    steps = width // tile
+    along_y = pl.BlockSpec((1, 2, quarter, inner), lambda k: (place, 0, 0, 0))
+    along_x = pl.BlockSpec((2, 1, quarter, inner), lambda k: (0, place, 0, 0))
+    weight = pl.BlockSpec((tile, inner), lambda k: (k, 0))
+    left = pl.BlockSpec((rows // 2, tile), lambda k: (0, jnp.minimum(k, steps // 2 - 1)))
+    right = pl.BlockSpec((rows // 2, tile), lambda k: (0, jnp.maximum(k - steps // 2, 0)))
+    first, second = (value.reshape(2, 2, quarter, inner) for value in (first, second))
+    return pl.pallas_call(
+        pair_kernel,
+        grid=(steps,),
+        in_specs=[along_y, along_y, along_x, along_x, weight, weight],
+        out_specs=[left, right],
+        out_shape=[jax.ShapeDtypeStruct((rows // 2, width // 2), bf16)] * 2,
+        compiler_params=pltpu.CompilerParams(vmem_limit_bytes=40 * 2**20),
+        cost_estimate=NO_COST,
+    )(first, second, first, second, first_whole, second_whole)
 
 
 def local_plain(
@@ -834,14 +855,12 @@
     up_other = swap(up_away, "c")
     hidden_part = hidden_parts[1]
 
-    def from_mlp(rows, side, gate_grad, up_grad):
-        return by_rows(rows, side, gate_grad, gate_whole) + by_rows(rows, side, up_grad, up_whole)
-
-    terms = plan.terms_first(from_mlp, grad_gate, grad_up)
-    left, right, left_y, right_x = terms
-    left, right, grad_gate, grad_up, hidden_part, own_tokens, own_mixed = sync(
-        left, right, grad_gate, grad_up, hidden_part, team_tokens, mixed_low
-    )
+    left_away, right_away = pair_terms(1, grad_gate, grad_up, gate_whole, up_whole)
+    left_away, right_away, grad_gate, grad_up, hidden_part, own_tokens, own_mixed = sync(
+        left_away, right_away, grad_gate, grad_up, hidden_part, team_tokens, mixed_low
+    )
+    left_y, right_x = swap(left_away, "y"), swap(right_away, "x")
+    left, right = pair_terms(0, grad_gate, grad_up, gate_whole, up_whole)
     terms = left, right, left_y, right_x
     gate_terms = summed(terms_of(hidden_part, grad_gate), gate_other)
     late_parts = (*plan.core_halves(own_tokens), *plan.core_halves(own_mixed))
@@ -853,7 +872,7 @@
     grad_up, *terms = sync(grad_up, *terms)
 
     grad_hidden, grad_proj, term_attn_gain = proj_back(
-        plan.own_order, *terms, live_col, cotangent, attn_proj, attn_inverse, attn_gain_wide
+        plan.own_order, terms, live_col, cotangent, attn_proj, attn_inverse, attn_gain_wide
     )
     rows = plan.rows_first(grad_proj)
     up_mine = terms_of(hidden_part, grad_up)
@@ -910,7 +929,7 @@
     )
     attn_sum = plan.ring_sum(3, attn_terms, attn_sum).astype(bf16)
     out_sum = plan.ring_sum(3, out_terms, out_sum).astype(bf16)
-    attn_sum, out_sum, gate_block, up_block, left, right, left_away, right_away = sync(
+    attn_sum, out_sum, gate_block, up_block, *sides, left_away, right_away = sync(
         attn_sum, out_sum, gate_block, up_block, *terms
     )
     attn_sum, out_sum = plan.shift(attn_sum), plan.shift(out_sum)
@@ -925,7 +944,7 @@
     attn_sum, out_sum, gain_terms, left_x, right_y = sync(
         attn_sum, out_sum, gain_terms, left_x, right_y
     )
-    grad_tokens = tokens_end(plan.own_order, left, right, left_x, right_y, grad_hidden)
+    grad_tokens = tokens_end(plan.own_order, (*sides, left_x, right_y), grad_hidden)
     attn_block = plan.return_columns(attn_sum)
     gain_terms = plan.gain_step(gain_terms, "y", 1)
     grad_w_out = plan.ring_sum(0, out_terms, out_sum)

time: 814 us -> 803 us (0.986)
  Pallas kernels: 70.9 us -> 98.9 us
  matrix products: 174 us -> 153 us
  local copies, waits for them, and re-layouts: 72.1 us -> 53.6 us
    pallas_call x0 -> x2, Pallas kernels: none -> 27.6 us  [pair_terms(): pl.pallas_call(pair_kernel, grid=(steps,), in_specs=[along_y, along_y, al...]
    dot_general x14 -> x6, matrix products: 58.7 us -> 35 us  [product_tt(): lax.dot_general(left, right, (((1,), (1,)), ((), ())), preferred_element_...]
    convert_element_type x0 -> x8, other arithmetic: none -> 10.6 us  [terms_added(): return (*stay, left_away.astype(bf16), right_away.astype(bf16))]
    slice x12 -> x0, local copies, waits for them, and re-layouts: 8.83 us -> none  [the longest x4 2.67 us: terms_added(): left[half:].astype(bf16)]
    unnamed x172 -> x158, local copies, waits for them, and re-layouts: 24.2 us -> 19.5 us
  transfers between devices with their start and end apart: 91 -> 91, of which waited for: 49 -> 47; matrix products, arithmetic and copies ran while one was open for 31% -> 28% of each run, Pallas kernels for 8% -> 11%
where the time goes in v5:
time: 803 us; the launch traced here: 797 us
  waiting for transfers between devices  316 us (39%)
  matrix products  153 us (19%)
  Pallas kernels  98.9 us (12%)
  starting transfers between devices  89.6 us (11%)
  other arithmetic  70.3 us (9%)
  local copies, waits for them, and re-layouts  53.6 us (7%)
  between operations  15.9 us (2%)
    ppermute x67, waiting for transfers between devices, swap(): return lax.ppermute(value, axis, ((0, 1), (1, 0)))  226 us
    ppermute x12, waiting for transfers between devices, shift(): return lax.ppermute(value, self.z_axes, ((0, 1), (1, 2), (2, 3), (3, 0)))  80.7 us
    dot_general x11, matrix products, inner_rows(): lax.dot_general(left, right, (((0,), (0,)), ((), ())), preferred_element_...  68 us
    ppermute x67, starting transfers between devices, swap(): return lax.ppermute(value, axis, ((0, 1), (1, 0)))  55.6 us
    dot_general x11, matrix products, product(): return jnp.dot(left, right, preferred_element_type=f32)  49.7 us
    dot_general x6, matrix products, product_tt(): lax.dot_general(left, right, (((1,), (1,)), ((), ())), preferred_element_...  35 us
    pallas_call x2, Pallas kernels, pair_terms(): pl.pallas_call(pair_kernel, grid=(steps,), in_specs=[along_y, along_y, al...  27.6 us
    pallas_call x1, Pallas kernels, attend_back(): pl.pallas_call(attend_back_kernel, grid=(size,), in_specs=[whole, rows(3...  20.8 us
  transfers between devices with their start and end apart: 91, of which 47 were waited for; matrix products, arithmetic and copies ran while one was open for 28% of the time, Pallas kernels for 11%

profile of v5, /device:TPU:0, one launch (start us, length us, event | category | flops | bytes accessed | tf_op | source)
XLA Modules:
  0.0 797.4 jit_solution(13453579723143262991)
XLA Ops:
  25.3 13.4 %collective-permute-done.refs_2_ = bf16[128,2048]{1,0:T(8,128)(2,1)S(1)} collective-permute-done((bf16[128,2048]{1,0:T(8,128)(2,1)S(1)}, bf16[128,2048]{1,0:T(8,128)(2,1)S(1)}, u32[]{:S(2)}, u32[]{:S(2)}) %collective-permute-start) | collective-permute-done | bytes 524320 | tf_op jit(solution)/shard_map/ppermute | solution.py:198
  42.4 28.5 %collective-permute-done.4.refs_1_ = bf16[256,2048]{1,0:T(8,128)(2,1)} collective-permute-done((bf16[256,2048]{1,0:T(8,128)(2,1)S(1)}, bf16[256,2048]{1,0:T(8,128)(2,1)}, u32[]{:S(2)}, u32[]{:S(2)}) %collective-permute-start.4) | collective-permute-done | bytes 1048608 | tf_op jit(solution)/shard_map/ppermute | solution.py:378
  74.6 8.5 %collective-permute-done.7.refs_6_ = bf16[128,2048]{1,0:T(8,128)(2,1)S(1)} collective-permute-done((bf16[128,2048]{1,0:T(8,128)(2,1)S(1)}, bf16[128,2048]{1,0:T(8,128)(2,1)S(1)}, u32[]{:S(2)}, u32[]{:S(2)}) %collective-permute-start.7) | collective-permute-done | bytes 524320 | tf_op jit(solution)/shard_map/ppermute | solution.py:198
  119.3 12.2 %collective-permute-done.13 = bf16[5,8,64]{2,0,1:T(8,128)(2,1)S(1)} collective-permute-done((bf16[5,8,64]{2,0,1:T(8,128)(2,1)S(1)}, bf16[5,8,64]{2,0,1:T(8,128)(2,1)S(1)}, u32[]{:S(2)}, u32[]{:S(2)}) %collective-permute-start.13) | collective-permute-done | bytes 5152 | tf_op jit(solution)/shard_map/ppermute | solution.py:198
  168.3 12.4 %shard_map.276 = (bf16[1024,1536]{1,0:T(8,128)(2,1)}, bf16[1024,512]{1,0:T(8,128)(2,1)}) custom-call(s32[4,2]{1,0:T(4,128)} %slice_convert_fusion.1.lengths_ref, f32[1024,1536]{1,0:T(8,128)} %copy-done.24, f32[1024,2]{1,0:T(8,128)} %bitcast.193, f32[2,512]{1,0:T(2,128)} %constant_dynamic-slice_fusion.21.gains_ref, f32[1024,128]{1,0:T(8,128)} %pad_maximum_fusion.4.cosine_ref, ...), custom_call_target="tpu_custom_call" | custom-call | tf_op jit(solution)/shard_map/pallas_call | solution.py:162
  186.6 22.3 %collective-permute-done.18 = bf16[512,1024]{1,0:T(8,128)(2,1)S(1)} collective-permute-done((bf16[512,1024]{1,0:T(8,128)(2,1)S(1)}, bf16[512,1024]{1,0:T(8,128)(2,1)S(1)}, u32[]{:S(2)}, u32[]{:S(2)}) %collective-permute-start.18) | collective-permute-done | bytes 1048608 | tf_op jit(solution)/shard_map/ppermute | solution.py:198
  213.1 7.9 collective-permute-done.19
  236.4 10.8 %collective-permute-done.22.refs_2_ = bf16[128,2048]{1,0:T(8,128)(2,1)S(1)} collective-permute-done((bf16[128,2048]{1,0:T(8,128)(2,1)S(1)}, bf16[128,2048]{1,0:T(8,128)(2,1)S(1)}, u32[]{:S(2)}, u32[]{:S(2)}) %collective-permute-start.22) | collective-permute-done | bytes 524320 | tf_op jit(solution)/shard_map/ppermute | solution.py:198
  249.2 9.3 %collective-permute-done.23.refs_3_ = bf16[128,2048]{1,0:T(8,128)(2,1)} collective-permute-done((bf16[128,2048]{1,0:T(8,128)(2,1)S(1)}, bf16[128,2048]{1,0:T(8,128)(2,1)}, u32[]{:S(2)}, u32[]{:S(2)}) %collective-permute-start.23) | collective-permute-done | bytes 524320 | tf_op jit(solution)/shard_map/ppermute | solution.py:198
  273.4 13.8 %convolution_convert_fusion.1 = bf16[1024,2048]{1,0:T(8,128)(2,1)} fusion(bf16[1024,2048]{1,0:T(8,128)(2,1)} %copy-done.6, bf16[2048,2048]{1,0:T(8,128)(2,1)} %all-gather.6.cloned.1.call-done.first_w), kind=kOutput, calls=%fused_computation.26 | convolution fusion | flops 8592031744 | bytes 16777216 | tf_op jit(solution)/shard_map/dot_general | solution.py:21
  287.2 15.4 %collective-permute-done.28.refs_2_ = bf16[256,2048]{1,0:T(8,128)(2,1)} collective-permute-done((bf16[256,2048]{1,0:T(8,128)(2,1)}, bf16[256,2048]{1,0:T(8,128)(2,1)}, u32[]{:S(2)}, u32[]{:S(2)}) %collective-permute-start.28) | collective-permute-done | bytes 1048608 | tf_op jit(solution)/shard_map/ppermute | solution.py:378
  302.6 15.6 %fusion = (bf16[1024,2048]{1,0:T(8,128)(2,1)S(1)}, bf16[1024,2048]{1,0:T(8,128)(2,1)}) fusion(bf16[1024,2048]{1,0:T(8,128)(2,1)} %convolution_convert_fusion.1, bf16[1024,2048]{1,0:T(8,128)(2,1)} %copy-done.6, bf16[2048,2048]{1,0:T(8,128)(2,1)} %all-gather.8.cloned.1.call-done.second_w), kind=kOutput, calls=%fused_computation.5 | convolution fusion | flops 8608808960 | bytes 25165824 | tf_op jit(solution)/shard_map/dot_general | solution.py:21
  318.2 8.6 %collective-permute-done.29.refs_3_ = bf16[256,2048]{1,0:T(8,128)(2,1)S(1)} collective-permute-done((bf16[256,2048]{1,0:T(8,128)(2,1)}, bf16[256,2048]{1,0:T(8,128)(2,1)S(1)}, u32[]{:S(2)}, u32[]{:S(2)}) %collective-permute-start.29) | collective-permute-done | bytes 1048608 | tf_op jit(solution)/shard_map/ppermute | solution.py:378
  346.1 18.0 %collective-permute-done.34 = bf16[512,1024]{1,0:T(8,128)(2,1)S(1)} collective-permute-done((bf16[512,1024]{1,0:T(8,128)(2,1)S(1)}, bf16[512,1024]{1,0:T(8,128)(2,1)S(1)}, u32[]{:S(2)}, u32[]{:S(2)}) %collective-permute-start.34) | collective-permute-done | bytes 1048608 | tf_op jit(solution)/shard_map/ppermute | solution.py:198
  369.3 10.6 %collective-permute-done.36 = bf16[256,1024]{1,0:T(8,128)(2,1)} collective-permute-done((bf16[256,1024]{1,0:T(8,128)(2,1)}, bf16[256,1024]{1,0:T(8,128)(2,1)}, u32[]{:S(2)}, u32[]{:S(2)}) %collective-permute-start.36) | collective-permute-done | bytes 524320 | tf_op jit(solution)/shard_map/ppermute | solution.py:198
  391.6 10.8 %collective-permute-done.38.refs_2_ = bf16[128,2048]{1,0:T(8,128)(2,1)S(1)} collective-permute-done((bf16[128,2048]{1,0:T(8,128)(2,1)S(1)}, bf16[128,2048]{1,0:T(8,128)(2,1)S(1)}, u32[]{:S(2)}, u32[]{:S(2)}) %collective-permute-start.38) | collective-permute-done | bytes 524320 | tf_op jit(solution)/shard_map/ppermute | solution.py:198
  404.5 9.2 %collective-permute-done.39.refs_3_ = bf16[128,2048]{1,0:T(8,128)(2,1)S(1)} collective-permute-done((bf16[128,2048]{1,0:T(8,128)(2,1)S(1)}, bf16[128,2048]{1,0:T(8,128)(2,1)S(1)}, u32[]{:S(2)}, u32[]{:S(2)}) %collective-permute-start.39) | collective-permute-done | bytes 524320 | tf_op jit(solution)/shard_map/ppermute | solution.py:198
  414.4 8.4 %collective-permute-done.42.refs_6_ = bf16[128,2048]{1,0:T(8,128)(2,1)S(1)} collective-permute-done((bf16[128,2048]{1,0:T(8,128)(2,1)S(1)}, bf16[128,2048]{1,0:T(8,128)(2,1)S(1)}, u32[]{:S(2)}, u32[]{:S(2)}) %collective-permute-start.42) | collective-permute-done | bytes 524320 | tf_op jit(solution)/shard_map/ppermute | solution.py:198
  445.7 19.5 %multiply_convert_fusion = (bf16[1024,2048]{1,0:T(8,128)(2,1)}, bf16[1024,2048]{1,0:T(8,128)(2,1)S(1)}) fusion(bf16[1024,2048]{1,0:T(8,128)(2,1)} %convolution_convert_fusion.1, bf16[1024,2048]{1,0:T(8,128)(2,1)} %get-tuple-element.488, bf16[1024,2048]{1,0:T(8,128)(2,1)} %copy-done.9, bf16[2048,2048]{1,0:T(8,128)(2,1)} %copy-done.7), kind=kOutput, calls=%fused_computation.15 | convolution fusion | flops 8621391872 | bytes 29360128 | tf_op jit(solution)/shard_map/dot_general | solution.py:25
  471.7 8.5 %convolution_convert_fusion.4 = bf16[1024,2048]{1,0:T(8,128)(2,1)} fusion(bf16[1024,1024]{1,0:T(8,128)(2,1)S(1)} %copy-done.44, bf16[1024,2048]{1,0:T(8,128)(2,1)} %get-tuple-element.309), kind=kOutput, calls=%fused_computation.29 | convolution fusion | flops 4297064448 | bytes 10485760 | tf_op jit(solution)/shard_map/dot_general | solution.py:29
  480.1 13.8 %shard_map.281 = (bf16[512,1024]{1,0:T(8,128)(2,1)}, bf16[512,1024]{1,0:T(8,128)(2,1)S(1)}) custom-call(bf16[2,2,256,2048]{3,2,1,0:T(8,128)(2,1)S(1)} %bitcast.180, bf16[2,2,256,2048]{3,2,1,0:T(8,128)(2,1)S(1)} %bitcast.176, bf16[2,2,256,2048]{3,2,1,0:T(8,128)(2,1)S(1)} %bitcast.181, bf16[2,2,256,2048]{3,2,1,0:T(8,128)(2,1)S(1)} %bitcast.177, ...), custom_call_target="tpu_custom_call" | custom-call | tf_op jit(solution)/shard_map/pallas_call | solution.py:611
  495.6 13.8 %shard_map.282 = (bf16[512,1024]{1,0:T(8,128)(2,1)S(1)}, bf16[512,1024]{1,0:T(8,128)(2,1)S(1)}) custom-call(bf16[2,2,256,2048]{3,2,1,0:T(8,128)(2,1)S(1)} %bitcast.182, bf16[2,2,256,2048]{3,2,1,0:T(8,128)(2,1)S(1)} %bitcast.178, bf16[2,2,256,2048]{3,2,1,0:T(8,128)(2,1)S(1)} %bitcast.183, bf16[2,2,256,2048]{3,2,1,0:T(8,128)(2,1)S(1)} %bitcast.179, ...), custom_call_target="tpu_custom_call" | custom-call | tf_op jit(solution)/shard_map/pallas_call | solution.py:611
  513.2 7.8 add_convert_fusion.1
  529.7 8.0 %collective-permute-done.50.refs_5_ = bf16[256,1024]{1,0:T(8,128)(2,1)S(1)} collective-permute-done((bf16[256,1024]{1,0:T(8,128)(2,1)}, bf16[256,1024]{1,0:T(8,128)(2,1)S(1)}, u32[]{:S(2)}, u32[]{:S(2)}) %collective-permute-start.50) | collective-permute-done | bytes 524320 | tf_op jit(solution)/shard_map/ppermute | solution.py:198
  551.5 9.5 %convolution_convert_fusion.3 = bf16[1024,2048]{1,0:T(8,128)(2,1)} fusion(bf16[1024,1024]{1,0:T(8,128)(2,1)} %get-tuple-element.294, bf16[1024,2048]{1,0:T(8,128)(2,1)} %get-tuple-element.309), kind=kOutput, calls=%fused_computation.28 | convolution fusion | flops 4297064448 | bytes 10485760 | tf_op jit(solution)/shard_map/dot_general | solution.py:29
  569.0 7.8 add_convert_fusion
  580.8 9.5 %collective-permute-done.56.refs_6_ = bf16[128,2048]{1,0:T(8,128)(2,1)} collective-permute-done((bf16[128,2048]{1,0:T(8,128)(2,1)S(1)}, bf16[128,2048]{1,0:T(8,128)(2,1)}, u32[]{:S(2)}, u32[]{:S(2)}) %collective-permute-start.56) | collective-permute-done | bytes 524320 | tf_op jit(solution)/shard_map/ppermute | solution.py:198
  590.3 7.7 reduce-scatter.6.cloned.1.call-done
  608.5 20.8 %shard_map.285 = (f32[1024,1024]{1,0:T(8,128)}, bf16[1024,512]{1,0:T(8,128)(2,1)}, f32[1024,2]{1,0:T(8,128)}, f32[2,512]{1,0:T(2,128)}) custom-call(s32[4,2]{1,0:T(4,128)} %slice_convert_fusion.1.lengths_ref, f32[1024,1536]{1,0:T(8,128)} %copy-done.24, bf16[1024,1536]{1,0:T(8,128)(2,1)} %get-tuple-element.272.turned_ref, f32[1024,2]{1,0:T(8,128)} %bitcast.194, ...), custom_call_target="tpu_custom_call" | custom-call | tf_op jit(solution)/shard_map/pallas_call | solution.py:179
  697.8 14.9 %collective-permute-done.67 = f32[2048]{0:T(1024)S(1)} collective-permute-done((f32[2048]{0:T(1024)S(1)}, f32[2048]{0:T(1024)S(1)}, u32[]{:S(2)}, u32[]{:S(2)}) %collective-permute-start.67) | collective-permute-done | bytes 8224 | tf_op jit(solution)/shard_map/ppermute | solution.py:198
  727.1 12.7 %collective-permute-done.72 = f32[1536]{0:T(1024)S(1)} collective-permute-done((f32[1536]{0:T(1024)S(1)}, f32[1536]{0:T(1024)S(1)}, u32[]{:S(2)}, u32[]{:S(2)}) %collective-permute-start.72) | collective-permute-done | bytes 6176 | tf_op jit(solution)/shard_map/ppermute | solution.py:198
  758.6 12.6 %collective-permute-done.74 = bf16[64,2048]{1,0:T(8,128)(2,1)S(1)} collective-permute-done((bf16[64,2048]{1,0:T(8,128)(2,1)S(1)}, bf16[64,2048]{1,0:T(8,128)(2,1)S(1)}, u32[]{:S(2)}, u32[]{:S(2)}) %collective-permute-start.74) | collective-permute-done | bytes 262176 | tf_op jit(solution)/shard_map/ppermute | solution.py:378
  (512 shorter events, 378.8 us)
Async XLA Ops:
  7.2 102.6 %all-gather.4.cloned.1.call-start = ((), (), s32[]{:S(2)}) async-start(), calls=%async_computation.9 | async-start | bytes 2949120 | tf_op jit(solution)/shard_map/all_gather | solution.py:748
  11.4 27.4 %all-to-all-start = ((bf16[4,64,1536]{2,1,0:T(8,128)(2,1)}), bf16[4,64,1536]{2,1,0:T(8,128)(2,1)S(1)}, u32[]{:S(2)}, u32[]{:S(2)}) async-start(bf16[4,64,1536]{2,1,0:T(8,128)(2,1)} %pad_maximum_fusion.3), calls=%async_computation | async-start | bytes 1572864 | tf_op jit(solution)/shard_map/all_to_all | solution.py:447
  23.8 47.1 %collective-permute-start.4 = (bf16[256,2048]{1,0:T(8,128)(2,1)S(1)}, bf16[256,2048]{1,0:T(8,128)(2,1)}, u32[]{:S(2)}, u32[]{:S(2)}) collective-permute-start(bf16[256,2048]{1,0:T(8,128)(2,1)S(1)} %copy-done.13), channel_id=1, source_target_pairs={{0,1},{1,2},{2,3},{3,0},{4,5},{5,6},{6,7},{7,4},{8,9},{9,10},{10,1... | collective-permute-start | bytes 3145736 | tf_op jit(solution)/shard_map/ppermute | solution.py:378
  38.8 33.3 %collective-permute-start.5 = (bf16[128,2048]{1,0:T(8,128)(2,1)S(1)}, bf16[128,2048]{1,0:T(8,128)(2,1)S(1)}, u32[]{:S(2)}, u32[]{:S(2)}) collective-permute-start(bf16[128,2048]{1,0:T(8,128)(2,1)S(1)} %get-tuple-element.232.refs_1_), channel_id=1, source_target_pairs={{0,8},{8,0},{1,9},{9,1},{2,10},{10,2},{3,11},{11,3},{4,12},{12,4},... | collective-permute-start | bytes 1572872 | tf_op jit(solution)/shard_map/ppermute | solution.py:198
  40.2 46.7 %collective-permute-start.2 = (bf16[256,1536]{1,0:T(8,128)(2,1)S(1)}, bf16[256,1536]{1,0:T(8,128)(2,1)}, u32[]{:S(2)}, u32[]{:S(2)}) collective-permute-start(bf16[256,1536]{1,0:T(8,128)(2,1)S(1)} %bitcast.188), channel_id=1, source_target_pairs={{0,1},{1,2},{2,3},{3,0},{4,5},{5,6},{6,7},{7,4},{8,9},{9,10},{10,1... | collective-permute-start | bytes 2359304 | tf_op jit(solution)/shard_map/ppermute | solution.py:378
  41.9 45.0 %collective-permute-start.3 = (bf16[256,1536]{1,0:T(8,128)(2,1)S(1)}, bf16[256,1536]{1,0:T(8,128)(2,1)S(1)}, u32[]{:S(2)}, u32[]{:S(2)}) collective-permute-start(bf16[256,1536]{1,0:T(8,128)(2,1)S(1)} %bitcast.189), channel_id=1, source_target_pairs={{0,4},{4,0},{1,5},{5,1},{2,6},{6,2},{3,7},{7,3},{8,12},{12,8},{9,1... | collective-permute-start | bytes 2359304 | tf_op jit(solution)/shard_map/ppermute | solution.py:198
  41.9 32.0 %collective-permute-start.6 = (bf16[128,2048]{1,0:T(8,128)(2,1)S(1)}, bf16[128,2048]{1,0:T(8,128)(2,1)S(1)}, u32[]{:S(2)}, u32[]{:S(2)}) collective-permute-start(bf16[128,2048]{1,0:T(8,128)(2,1)S(1)} %get-tuple-element.231.refs_0_), channel_id=1, source_target_pairs={{0,16},{16,0},{1,17},{17,1},{2,18},{18,2},{3,19},{19,3},{4,20},{20... | collective-permute-start | bytes 1572872 | tf_op jit(solution)/shard_map/ppermute | solution.py:198
  94.3 179.0 %all-gather.6.cloned.1.call-start = ((), (), s32[]{:S(2)}) async-start(), calls=%async_computation.10 | async-start | bytes 9437184 | tf_op jit(solution)/shard_map/all_gather | solution.py:748
  109.9 31.5 %collective-permute-start.11 = (bf16[256,1536]{1,0:T(8,128)(2,1)}, bf16[256,1536]{1,0:T(8,128)(2,1)}, u32[]{:S(2)}, u32[]{:S(2)}) collective-permute-start(bf16[256,1536]{1,0:T(8,128)(2,1)} %collective-permute-done.9.refs_2_), channel_id=1, source_target_pairs={{0,1},{1,2},{2,3},{3,0},{4,5},{5,6},{6,7},{7,4},{8,9},{9,10},{10,1... | collective-permute-start | bytes 2359304 | tf_op jit(solution)/shard_map/ppermute | solution.py:378
  110.0 31.5 %collective-permute-start.12 = (bf16[256,1536]{1,0:T(8,128)(2,1)}, bf16[256,1536]{1,0:T(8,128)(2,1)}, u32[]{:S(2)}, u32[]{:S(2)}) collective-permute-start(bf16[256,1536]{1,0:T(8,128)(2,1)} %collective-permute-done.9.refs_2_), channel_id=1, source_target_pairs={{0,4},{4,0},{1,5},{5,1},{2,6},{6,2},{3,7},{7,3},{8,12},{12,8},{9,1... | collective-permute-start | bytes 2359304 | tf_op jit(solution)/shard_map/ppermute | solution.py:198
  116.6 186.0 %all-gather.8.cloned.1.call-start = ((), (), s32[]{:S(2)}) async-start(), calls=%async_computation.11 | async-start | bytes 9437184 | tf_op jit(solution)/shard_map/all_gather | solution.py:748
  141.4 423.5 %reduce-scatter.4.cloned.1.call-start = ((), (), s32[]{:S(2)}) async-start(), calls=%async_computation.12 | async-start | bytes 5242880 | tf_op jit(solution)/shard_map/reduce_scatter | solution.py:840
  234.9 25.6 %collective-permute-start.24 = (bf16[128,2048]{1,0:T(8,128)(2,1)S(1)}, bf16[128,2048]{1,0:T(8,128)(2,1)}, u32[]{:S(2)}, u32[]{:S(2)}) collective-permute-start(bf16[128,2048]{1,0:T(8,128)(2,1)S(1)} %get-tuple-element.455.refs_0_), channel_id=1, source_target_pairs={{0,16},{16,0},{1,17},{17,1},{2,18},{18,2},{3,19},{19,3},{4,20},{20... | collective-permute-start | bytes 1572872 | tf_op jit(solution)/shard_map/ppermute | solution.py:198
  249.2 80.4 %collective-permute-start.30 = (bf16[256,2048]{1,0:T(8,128)(2,1)S(1)}, bf16[256,2048]{1,0:T(8,128)(2,1)}, u32[]{:S(2)}, u32[]{:S(2)}) collective-permute-start(bf16[256,2048]{1,0:T(8,128)(2,1)S(1)} %copy-done.13), channel_id=1, source_target_pairs={{0,4},{4,0},{1,5},{5,1},{2,6},{6,2},{3,7},{7,3},{8,12},{12,8},{9,1... | collective-permute-start | bytes 3145736 | tf_op jit(solution)/shard_map/ppermute | solution.py:198
  258.5 44.0 %collective-permute-start.28 = (bf16[256,2048]{1,0:T(8,128)(2,1)}, bf16[256,2048]{1,0:T(8,128)(2,1)}, u32[]{:S(2)}, u32[]{:S(2)}) collective-permute-start(bf16[256,2048]{1,0:T(8,128)(2,1)} %collective-permute-done.4.refs_1_), channel_id=1, source_target_pairs={{0,1},{1,2},{2,3},{3,0},{4,5},{5,6},{6,7},{7,4},{8,9},{9,10},{10,1... | collective-permute-start | bytes 3145736 | tf_op jit(solution)/shard_map/ppermute | solution.py:378
  260.5 69.1 %collective-permute-start.31 = (bf16[256,2048]{1,0:T(8,128)(2,1)}, bf16[256,2048]{1,0:T(8,128)(2,1)}, u32[]{:S(2)}, u32[]{:S(2)}) collective-permute-start(bf16[256,2048]{1,0:T(8,128)(2,1)} %collective-permute-done.4.refs_1_), channel_id=1, source_target_pairs={{0,4},{4,0},{1,5},{5,1},{2,6},{6,2},{3,7},{7,3},{8,12},{12,8},{9,1... | collective-permute-start | bytes 3145736 | tf_op jit(solution)/shard_map/ppermute | solution.py:198
  302.6 27.1 %collective-permute-start.32 = (bf16[256,2048]{1,0:T(8,128)(2,1)}, bf16[256,2048]{1,0:T(8,128)(2,1)}, u32[]{:S(2)}, u32[]{:S(2)}) collective-permute-start(bf16[256,2048]{1,0:T(8,128)(2,1)} %collective-permute-done.28.refs_2_), channel_id=1, source_target_pairs={{0,4},{4,0},{1,5},{5,1},{2,6},{6,2},{3,7},{7,3},{8,12},{12,8},{9,1... | collective-permute-start | bytes 3145736 | tf_op jit(solution)/shard_map/ppermute | solution.py:198
  338.4 25.6 %collective-permute-start.34 = (bf16[512,1024]{1,0:T(8,128)(2,1)S(1)}, bf16[512,1024]{1,0:T(8,128)(2,1)S(1)}, u32[]{:S(2)}, u32[]{:S(2)}) collective-permute-start(bf16[512,1024]{1,0:T(8,128)(2,1)S(1)} %fusion.54), channel_id=1, source_target_pairs={{0,16},{16,0},{1,17},{17,1},{2,18},{18,2},{3,19},{19,3},{4,20},{20... | collective-permute-start | bytes 3145736 | tf_op jit(solution)/shard_map/ppermute | solution.py:198
  340.1 25.3 %collective-permute-start.35 = (bf16[512,1024]{1,0:T(8,128)(2,1)S(1)}, bf16[512,1024]{1,0:T(8,128)(2,1)S(1)}, u32[]{:S(2)}, u32[]{:S(2)}) collective-permute-start(bf16[512,1024]{1,0:T(8,128)(2,1)S(1)} %fusion.59), channel_id=1, source_target_pairs={{0,8},{8,0},{1,9},{9,1},{2,10},{10,2},{3,11},{11,3},{4,12},{12,4},... | collective-permute-start | bytes 3145736 | tf_op jit(solution)/shard_map/ppermute | solution.py:198
  444.7 153.3 %reduce-scatter.6.cloned.1.call-start = ((), (), s32[]{:S(2)}) async-start(), calls=%async_computation.13 | async-start | bytes 5242880 | tf_op jit(solution)/shard_map/reduce_scatter | solution.py:870
  471.5 41.7 %collective-permute-start.46 = (bf16[1024,2048]{1,0:T(8,128)(2,1)}, bf16[1024,2048]{1,0:T(8,128)(2,1)}, u32[]{:S(2)}, u32[]{:S(2)}) collective-permute-start(bf16[1024,2048]{1,0:T(8,128)(2,1)} %convolution_convert_fusion.5), channel_id=1, source_target_pairs={{0,4},{4,0},{1,5},{5,1},{2,6},{6,2},{3,7},{7,3},{8,12},{12,8},{9,1... | collective-permute-start | bytes 12582920 | tf_op jit(solution)/shard_map/ppermute | solution.py:198
  494.0 27.0 %collective-permute-start.47 = (bf16[512,1024]{1,0:T(8,128)(2,1)}, bf16[512,1024]{1,0:T(8,128)(2,1)}, u32[]{:S(2)}, u32[]{:S(2)}) collective-permute-start(bf16[512,1024]{1,0:T(8,128)(2,1)} %get-tuple-element.302), channel_id=1, source_target_pairs={{0,16},{16,0},{1,17},{17,1},{2,18},{18,2},{3,19},{19,3},{4,20},{20... | collective-permute-start | bytes 3145736 | tf_op jit(solution)/shard_map/ppermute | solution.py:198
  494.6 26.4 %collective-permute-start.48 = (bf16[512,1024]{1,0:T(8,128)(2,1)S(1)}, bf16[512,1024]{1,0:T(8,128)(2,1)}, u32[]{:S(2)}, u32[]{:S(2)}) collective-permute-start(bf16[512,1024]{1,0:T(8,128)(2,1)S(1)} %get-tuple-element.303), channel_id=1, source_target_pairs={{0,8},{8,0},{1,9},{9,1},{2,10},{10,2},{3,11},{11,3},{4,12},{12,4},... | collective-permute-start | bytes 3145736 | tf_op jit(solution)/shard_map/ppermute | solution.py:198
  521.0 39.9 %collective-permute-start.51 = (bf16[1024,2048]{1,0:T(8,128)(2,1)}, bf16[1024,2048]{1,0:T(8,128)(2,1)}, u32[]{:S(2)}, u32[]{:S(2)}) collective-permute-start(bf16[1024,2048]{1,0:T(8,128)(2,1)} %convolution_convert_fusion.4), channel_id=1, source_target_pairs={{0,4},{4,0},{1,5},{5,1},{2,6},{6,2},{3,7},{7,3},{8,12},{12,8},{9,1... | collective-permute-start | bytes 12582920 | tf_op jit(solution)/shard_map/ppermute | solution.py:198
  548.4 53.9 %collective-permute-start.58 = (f32[2,2,2,2,64]{4,3,2,1,0:T(2,128)S(1)}, f32[2,2,2,2,64]{4,3,2,1,0:T(2,128)S(1)}, u32[]{:S(2)}, u32[]{:S(2)}) collective-permute-start(f32[2,2,2,2,64]{4,3,2,1,0:T(2,128)S(1)} %fusion.80), channel_id=1, source_target_pairs={{0,4},{4,0},{1,5},{5,1},{2,6},{6,2},{3,7},{7,3},{8,12},{12,8},{9,1... | collective-permute-start | bytes 12296 | tf_op jit(solution)/shard_map/ppermute | solution.py:198
  598.0 31.4 %all-to-all-start.3 = ((bf16[4,64,2048]{2,1,0:T(8,128)(2,1)}), bf16[4,64,2048]{2,1,0:T(8,128)(2,1)}, u32[]{:S(2)}, u32[]{:S(2)}) async-start(bf16[4,64,2048]{2,1,0:T(8,128)(2,1)} %bitcast.216), calls=%async_computation.5 | async-start | bytes 2097152 | tf_op jit(solution)/shard_map/all_to_all | solution.py:450
  602.2 115.0 %reduce-scatter.8.cloned.1.call-start = ((), (), s32[]{:S(2)}) async-start(), calls=%async_computation.14 | async-start | bytes 5242880 | tf_op jit(solution)/shard_map/reduce_scatter | solution.py:883
  680.8 32.1 %collective-permute-start.68 = (bf16[512,1024]{1,0:T(8,128)(2,1)}, bf16[512,1024]{1,0:T(8,128)(2,1)}, u32[]{:S(2)}, u32[]{:S(2)}) collective-permute-start(bf16[512,1024]{1,0:T(8,128)(2,1)} %fusion.38), channel_id=1, source_target_pairs={{0,16},{16,0},{1,17},{17,1},{2,18},{18,2},{3,19},{19,3},{4,20},{20... | collective-permute-start | bytes 3145736 | tf_op jit(solution)/shard_map/ppermute | solution.py:198
  682.2 30.7 %collective-permute-start.69 = (bf16[512,1024]{1,0:T(8,128)(2,1)}, bf16[512,1024]{1,0:T(8,128)(2,1)}, u32[]{:S(2)}, u32[]{:S(2)}) collective-permute-start(bf16[512,1024]{1,0:T(8,128)(2,1)} %fusion.43), channel_id=1, source_target_pairs={{0,8},{8,0},{1,9},{9,1},{2,10},{10,2},{3,11},{11,3},{4,12},{12,4},... | collective-permute-start | bytes 3145736 | tf_op jit(solution)/shard_map/ppermute | solution.py:198
  685.7 27.1 %collective-permute-start.65 = (bf16[256,1536]{1,0:T(8,128)(2,1)}, bf16[256,1536]{1,0:T(8,128)(2,1)}, u32[]{:S(2)}, u32[]{:S(2)}) collective-permute-start(bf16[256,1536]{1,0:T(8,128)(2,1)} %add_convert_fusion.6), channel_id=1, source_target_pairs={{0,1},{1,2},{2,3},{3,0},{4,5},{5,6},{6,7},{7,4},{8,9},{9,10},{10,1... | collective-permute-start | bytes 2359304 | tf_op jit(solution)/shard_map/ppermute | solution.py:378
  717.2 25.8 %collective-permute-start.70 = (bf16[256,1536]{1,0:T(8,128)(2,1)}, bf16[256,1536]{1,0:T(8,128)(2,1)}, u32[]{:S(2)}, u32[]{:S(2)}) collective-permute-start(bf16[256,1536]{1,0:T(8,128)(2,1)} %add_convert_fusion.5), channel_id=1, source_target_pairs={{0,1},{1,2},{2,3},{3,0},{4,5},{5,6},{6,7},{7,4},{8,9},{9,10},{10,1... | collective-permute-start | bytes 2359304 | tf_op jit(solution)/shard_map/ppermute | solution.py:378
  717.2 25.8 %all-to-all-start.4 = ((bf16[4,64,2048]{2,1,0:T(8,128)(2,1)}), bf16[4,64,2048]{2,1,0:T(8,128)(2,1)S(1)}, u32[]{:S(2)}, u32[]{:S(2)}) async-start(bf16[4,64,2048]{2,1,0:T(8,128)(2,1)} %bitcast.215), calls=%async_computation.7 | async-start | bytes 2097152 | tf_op jit(solution)/shard_map/all_to_all | solution.py:450
  (136 other events, 1468.8 us)
Sparse Core Ops, SparseCore 0:
  11.5 55.5 all-gather.3
  110.0 90.5 all-gather.5
  202.2 93.6 all-gather.7
  444.8 73.5 reduce-scatter.3
  521.2 76.7 reduce-scatter.5
  605.0 77.7 reduce-scatter.7

commit v6 on v5

--- a/solution.py
+++ b/solution.py
@@ -879,10 +879,11 @@
     up_mine, up_other, grad_w_down, *rows = sync(up_mine, up_other, grad_w_down, *rows)
     rows = plan.rows_second(*rows)
     up_terms = summed(up_mine, up_other)
-    up_terms, gate_block, *rows = sync(up_terms, gate_block, *rows)
+    up_terms, *rows = sync(up_terms, *rows)
     up_block = lax.psum_scatter(up_terms, plan.z_axes, scatter_dimension=0, tiled=True)
     team_grad_proj = join(*rows)
     grad_mixed = product_tt(team_grad_proj, out_whole).astype(bf16)
+    grad_mixed, gate_block = sync(grad_mixed, gate_block)
     scaled, grad_value, means, part_terms = attend_back(
         lengths, raw, turned, inverse, part_gains, cosine, sine, grad_mixed
     )

time: 803 us -> 799 us (level)
    unnamed x158 -> x162, local copies, waits for them, and re-layouts: 19.5 us -> 21.4 us
  transfers between devices with their start and end apart: 91 -> 91, of which waited for: 47 -> 48; matrix products, arithmetic and copies ran while one was open for 28% -> 28% of each run, Pallas kernels for 11% -> 12%
where the time goes in v6:
time: 799 us; the launch traced here: 794 us
  waiting for transfers between devices  313 us (39%)
  matrix products  152 us (19%)
  Pallas kernels  98.9 us (12%)
  starting transfers between devices  89.2 us (11%)
  other arithmetic  68.8 us (9%)
  local copies, waits for them, and re-layouts  55.6 us (7%)
  between operations  15.9 us (2%)
    ppermute x67, waiting for transfers between devices, swap(): return lax.ppermute(value, axis, ((0, 1), (1, 0)))  226 us
    ppermute x12, waiting for transfers between devices, shift(): return lax.ppermute(value, self.z_axes, ((0, 1), (1, 2), (2, 3), (3, 0)))  80.8 us
    dot_general x11, matrix products, inner_rows(): lax.dot_general(left, right, (((0,), (0,)), ((), ())), preferred_element_...  67.7 us
    ppermute x67, starting transfers between devices, swap(): return lax.ppermute(value, axis, ((0, 1), (1, 0)))  55.9 us
    dot_general x11, matrix products, product(): return jnp.dot(left, right, preferred_element_type=f32)  49.7 us
    dot_general x6, matrix products, product_tt(): lax.dot_general(left, right, (((1,), (1,)), ((), ())), preferred_element_...  34.9 us
    pallas_call x2, Pallas kernels, pair_terms(): pl.pallas_call(pair_kernel, grid=(steps,), in_specs=[along_y, along_y, al...  27.6 us
    unnamed x162, local copies, waits for them, and re-layouts  21.4 us
  transfers between devices with their start and end apart: 91, of which 48 were waited for; matrix products, arithmetic and copies ran while one was open for 28% of the time, Pallas kernels for 12%

profile of v6, /device:TPU:0, one launch (start us, length us, event | category | flops | bytes accessed | tf_op | source)
XLA Modules:
  0.0 793.7 jit_solution(3667607406088628227)
XLA Ops:
  25.3 13.4 %collective-permute-done.refs_2_ = bf16[128,2048]{1,0:T(8,128)(2,1)S(1)} collective-permute-done((bf16[128,2048]{1,0:T(8,128)(2,1)S(1)}, bf16[128,2048]{1,0:T(8,128)(2,1)S(1)}, u32[]{:S(2)}, u32[]{:S(2)}) %collective-permute-start) | collective-permute-done | bytes 524320 | tf_op jit(solution)/shard_map/ppermute | solution.py:198
  42.4 28.5 %collective-permute-done.4.refs_1_ = bf16[256,2048]{1,0:T(8,128)(2,1)} collective-permute-done((bf16[256,2048]{1,0:T(8,128)(2,1)S(1)}, bf16[256,2048]{1,0:T(8,128)(2,1)}, u32[]{:S(2)}, u32[]{:S(2)}) %collective-permute-start.4) | collective-permute-done | bytes 1048608 | tf_op jit(solution)/shard_map/ppermute | solution.py:378
  74.6 8.5 %collective-permute-done.7.refs_6_ = bf16[128,2048]{1,0:T(8,128)(2,1)S(1)} collective-permute-done((bf16[128,2048]{1,0:T(8,128)(2,1)S(1)}, bf16[128,2048]{1,0:T(8,128)(2,1)S(1)}, u32[]{:S(2)}, u32[]{:S(2)}) %collective-permute-start.7) | collective-permute-done | bytes 524320 | tf_op jit(solution)/shard_map/ppermute | solution.py:198
  119.3 12.2 %collective-permute-done.13 = bf16[5,8,64]{2,0,1:T(8,128)(2,1)S(1)} collective-permute-done((bf16[5,8,64]{2,0,1:T(8,128)(2,1)S(1)}, bf16[5,8,64]{2,0,1:T(8,128)(2,1)S(1)}, u32[]{:S(2)}, u32[]{:S(2)}) %collective-permute-start.13) | collective-permute-done | bytes 5152 | tf_op jit(solution)/shard_map/ppermute | solution.py:198
  168.3 12.4 %shard_map.276 = (bf16[1024,1536]{1,0:T(8,128)(2,1)}, bf16[1024,512]{1,0:T(8,128)(2,1)}) custom-call(s32[4,2]{1,0:T(4,128)} %slice_convert_fusion.1.lengths_ref, f32[1024,1536]{1,0:T(8,128)} %copy-done.24, f32[1024,2]{1,0:T(8,128)} %bitcast.193, f32[2,512]{1,0:T(2,128)} %constant_dynamic-slice_fusion.21.gains_ref, f32[1024,128]{1,0:T(8,128)} %pad_maximum_fusion.4.cosine_ref, ...), custom_call_target="tpu_custom_call" | custom-call | tf_op jit(solution)/shard_map/pallas_call | solution.py:162
  186.6 22.3 %collective-permute-done.18 = bf16[512,1024]{1,0:T(8,128)(2,1)S(1)} collective-permute-done((bf16[512,1024]{1,0:T(8,128)(2,1)S(1)}, bf16[512,1024]{1,0:T(8,128)(2,1)S(1)}, u32[]{:S(2)}, u32[]{:S(2)}) %collective-permute-start.18) | collective-permute-done | bytes 1048608 | tf_op jit(solution)/shard_map/ppermute | solution.py:198
  213.1 7.9 collective-permute-done.19
  236.3 10.8 %collective-permute-done.22.refs_2_ = bf16[128,2048]{1,0:T(8,128)(2,1)S(1)} collective-permute-done((bf16[128,2048]{1,0:T(8,128)(2,1)S(1)}, bf16[128,2048]{1,0:T(8,128)(2,1)S(1)}, u32[]{:S(2)}, u32[]{:S(2)}) %collective-permute-start.22) | collective-permute-done | bytes 524320 | tf_op jit(solution)/shard_map/ppermute | solution.py:198
  249.2 9.3 %collective-permute-done.23.refs_3_ = bf16[128,2048]{1,0:T(8,128)(2,1)} collective-permute-done((bf16[128,2048]{1,0:T(8,128)(2,1)S(1)}, bf16[128,2048]{1,0:T(8,128)(2,1)}, u32[]{:S(2)}, u32[]{:S(2)}) %collective-permute-start.23) | collective-permute-done | bytes 524320 | tf_op jit(solution)/shard_map/ppermute | solution.py:198
  273.3 13.8 %convolution_convert_fusion.1 = bf16[1024,2048]{1,0:T(8,128)(2,1)} fusion(bf16[1024,2048]{1,0:T(8,128)(2,1)} %copy-done.6, bf16[2048,2048]{1,0:T(8,128)(2,1)} %all-gather.6.cloned.1.call-done.first_w), kind=kOutput, calls=%fused_computation.26 | convolution fusion | flops 8592031744 | bytes 16777216 | tf_op jit(solution)/shard_map/dot_general | solution.py:21
  287.1 15.4 %collective-permute-done.28.refs_2_ = bf16[256,2048]{1,0:T(8,128)(2,1)} collective-permute-done((bf16[256,2048]{1,0:T(8,128)(2,1)}, bf16[256,2048]{1,0:T(8,128)(2,1)}, u32[]{:S(2)}, u32[]{:S(2)}) %collective-permute-start.28) | collective-permute-done | bytes 1048608 | tf_op jit(solution)/shard_map/ppermute | solution.py:378
  302.6 15.6 %fusion = (bf16[1024,2048]{1,0:T(8,128)(2,1)S(1)}, bf16[1024,2048]{1,0:T(8,128)(2,1)}) fusion(bf16[1024,2048]{1,0:T(8,128)(2,1)} %convolution_convert_fusion.1, bf16[1024,2048]{1,0:T(8,128)(2,1)} %copy-done.6, bf16[2048,2048]{1,0:T(8,128)(2,1)} %all-gather.8.cloned.1.call-done.second_w), kind=kOutput, calls=%fused_computation.5 | convolution fusion | flops 8608808960 | bytes 25165824 | tf_op jit(solution)/shard_map/dot_general | solution.py:21
  318.2 8.6 %collective-permute-done.29.refs_3_ = bf16[256,2048]{1,0:T(8,128)(2,1)S(1)} collective-permute-done((bf16[256,2048]{1,0:T(8,128)(2,1)}, bf16[256,2048]{1,0:T(8,128)(2,1)S(1)}, u32[]{:S(2)}, u32[]{:S(2)}) %collective-permute-start.29) | collective-permute-done | bytes 1048608 | tf_op jit(solution)/shard_map/ppermute | solution.py:378
  346.1 18.0 %collective-permute-done.34 = bf16[512,1024]{1,0:T(8,128)(2,1)S(1)} collective-permute-done((bf16[512,1024]{1,0:T(8,128)(2,1)S(1)}, bf16[512,1024]{1,0:T(8,128)(2,1)S(1)}, u32[]{:S(2)}, u32[]{:S(2)}) %collective-permute-start.34) | collective-permute-done | bytes 1048608 | tf_op jit(solution)/shard_map/ppermute | solution.py:198
  369.3 10.6 %collective-permute-done.36 = bf16[256,1024]{1,0:T(8,128)(2,1)} collective-permute-done((bf16[256,1024]{1,0:T(8,128)(2,1)}, bf16[256,1024]{1,0:T(8,128)(2,1)}, u32[]{:S(2)}, u32[]{:S(2)}) %collective-permute-start.36) | collective-permute-done | bytes 524320 | tf_op jit(solution)/shard_map/ppermute | solution.py:198
  391.6 10.8 %collective-permute-done.38.refs_2_ = bf16[128,2048]{1,0:T(8,128)(2,1)S(1)} collective-permute-done((bf16[128,2048]{1,0:T(8,128)(2,1)S(1)}, bf16[128,2048]{1,0:T(8,128)(2,1)S(1)}, u32[]{:S(2)}, u32[]{:S(2)}) %collective-permute-start.38) | collective-permute-done | bytes 524320 | tf_op jit(solution)/shard_map/ppermute | solution.py:198
  404.5 9.2 %collective-permute-done.39.refs_3_ = bf16[128,2048]{1,0:T(8,128)(2,1)S(1)} collective-permute-done((bf16[128,2048]{1,0:T(8,128)(2,1)S(1)}, bf16[128,2048]{1,0:T(8,128)(2,1)S(1)}, u32[]{:S(2)}, u32[]{:S(2)}) %collective-permute-start.39) | collective-permute-done | bytes 524320 | tf_op jit(solution)/shard_map/ppermute | solution.py:198
  414.4 8.4 %collective-permute-done.42.refs_6_ = bf16[128,2048]{1,0:T(8,128)(2,1)S(1)} collective-permute-done((bf16[128,2048]{1,0:T(8,128)(2,1)S(1)}, bf16[128,2048]{1,0:T(8,128)(2,1)S(1)}, u32[]{:S(2)}, u32[]{:S(2)}) %collective-permute-start.42) | collective-permute-done | bytes 524320 | tf_op jit(solution)/shard_map/ppermute | solution.py:198
  445.7 19.5 %multiply_convert_fusion = (bf16[1024,2048]{1,0:T(8,128)(2,1)}, bf16[1024,2048]{1,0:T(8,128)(2,1)S(1)}) fusion(bf16[1024,2048]{1,0:T(8,128)(2,1)} %convolution_convert_fusion.1, bf16[1024,2048]{1,0:T(8,128)(2,1)} %get-tuple-element.490, bf16[1024,2048]{1,0:T(8,128)(2,1)} %copy-done.10, bf16[2048,2048]{1,0:T(8,128)(2,1)} %copy-done.7), kind=kOutput, calls=%fused_computation.15 | convolution fusion | flops 8621391872 | bytes 29360128 | tf_op jit(solution)/shard_map/dot_general | solution.py:25
  471.6 8.5 %convolution_convert_fusion.4 = bf16[1024,2048]{1,0:T(8,128)(2,1)} fusion(bf16[1024,1024]{1,0:T(8,128)(2,1)S(1)} %copy-done.45, bf16[1024,2048]{1,0:T(8,128)(2,1)} %get-tuple-element.310), kind=kOutput, calls=%fused_computation.29 | convolution fusion | flops 4297064448 | bytes 10485760 | tf_op jit(solution)/shard_map/dot_general | solution.py:29
  480.1 13.8 %shard_map.281 = (bf16[512,1024]{1,0:T(8,128)(2,1)}, bf16[512,1024]{1,0:T(8,128)(2,1)S(1)}) custom-call(bf16[2,2,256,2048]{3,2,1,0:T(8,128)(2,1)S(1)} %bitcast.180, bf16[2,2,256,2048]{3,2,1,0:T(8,128)(2,1)S(1)} %bitcast.176, bf16[2,2,256,2048]{3,2,1,0:T(8,128)(2,1)S(1)} %bitcast.181, bf16[2,2,256,2048]{3,2,1,0:T(8,128)(2,1)S(1)} %bitcast.177, ...), custom_call_target="tpu_custom_call" | custom-call | tf_op jit(solution)/shard_map/pallas_call | solution.py:611
  495.6 13.8 %shard_map.282 = (bf16[512,1024]{1,0:T(8,128)(2,1)S(1)}, bf16[512,1024]{1,0:T(8,128)(2,1)S(1)}) custom-call(bf16[2,2,256,2048]{3,2,1,0:T(8,128)(2,1)S(1)} %bitcast.182, bf16[2,2,256,2048]{3,2,1,0:T(8,128)(2,1)S(1)} %bitcast.178, bf16[2,2,256,2048]{3,2,1,0:T(8,128)(2,1)S(1)} %bitcast.183, bf16[2,2,256,2048]{3,2,1,0:T(8,128)(2,1)S(1)} %bitcast.179, ...), custom_call_target="tpu_custom_call" | custom-call | tf_op jit(solution)/shard_map/pallas_call | solution.py:611
  513.2 7.8 add_convert_fusion.1
  528.4 8.4 %collective-permute-done.50.refs_5_ = bf16[256,1024]{1,0:T(8,128)(2,1)S(1)} collective-permute-done((bf16[256,1024]{1,0:T(8,128)(2,1)S(1)}, bf16[256,1024]{1,0:T(8,128)(2,1)S(1)}, u32[]{:S(2)}, u32[]{:S(2)}) %collective-permute-start.50) | collective-permute-done | bytes 524320 | tf_op jit(solution)/shard_map/ppermute | solution.py:198
  548.7 9.4 %convolution_convert_fusion.3 = bf16[1024,2048]{1,0:T(8,128)(2,1)} fusion(bf16[1024,1024]{1,0:T(8,128)(2,1)} %get-tuple-element.295, bf16[1024,2048]{1,0:T(8,128)(2,1)} %get-tuple-element.310), kind=kOutput, calls=%fused_computation.28 | convolution fusion | flops 4297064448 | bytes 10485760 | tf_op jit(solution)/shard_map/dot_general | solution.py:29
  565.1 7.9 add_convert_fusion
  576.9 8.4 %collective-permute-done.56.refs_6_ = bf16[128,2048]{1,0:T(8,128)(2,1)} collective-permute-done((bf16[128,2048]{1,0:T(8,128)(2,1)S(1)}, bf16[128,2048]{1,0:T(8,128)(2,1)}, u32[]{:S(2)}, u32[]{:S(2)}) %collective-permute-start.56) | collective-permute-done | bytes 524320 | tf_op jit(solution)/shard_map/ppermute | solution.py:198
  604.2 21.1 %shard_map.285 = (f32[1024,1024]{1,0:T(8,128)}, bf16[1024,512]{1,0:T(8,128)(2,1)}, f32[1024,2]{1,0:T(8,128)}, f32[2,512]{1,0:T(2,128)}) custom-call(s32[4,2]{1,0:T(4,128)} %slice_convert_fusion.1.lengths_ref, f32[1024,1536]{1,0:T(8,128)} %copy-done.24, bf16[1024,1536]{1,0:T(8,128)(2,1)} %get-tuple-element.273.turned_ref, f32[1024,2]{1,0:T(8,128)} %bitcast.194, ...), custom_call_target="tpu_custom_call" | custom-call | tf_op jit(solution)/shard_map/pallas_call | solution.py:179
  631.9 8.0 %collective-permute-done.59 = f32[2,2,256,2]{3,2,1,0:T(8,128)S(1)} collective-permute-done((f32[2,2,256,2]{3,2,1,0:T(8,128)}, f32[2,2,256,2]{3,2,1,0:T(8,128)S(1)}, u32[]{:S(2)}, u32[]{:S(2)}) %collective-permute-start.59) | collective-permute-done | bytes 8224 | tf_op jit(solution)/shard_map/ppermute | solution.py:198
  694.4 14.8 %collective-permute-done.67 = f32[2048]{0:T(1024)S(1)} collective-permute-done((f32[2048]{0:T(1024)S(1)}, f32[2048]{0:T(1024)S(1)}, u32[]{:S(2)}, u32[]{:S(2)}) %collective-permute-start.67) | collective-permute-done | bytes 8224 | tf_op jit(solution)/shard_map/ppermute | solution.py:198
  723.6 12.7 %collective-permute-done.72 = f32[1536]{0:T(1024)S(1)} collective-permute-done((f32[1536]{0:T(1024)S(1)}, f32[1536]{0:T(1024)S(1)}, u32[]{:S(2)}, u32[]{:S(2)}) %collective-permute-start.72) | collective-permute-done | bytes 6176 | tf_op jit(solution)/shard_map/ppermute | solution.py:198
  755.0 12.6 %collective-permute-done.74 = bf16[64,2048]{1,0:T(8,128)(2,1)S(1)} collective-permute-done((bf16[64,2048]{1,0:T(8,128)(2,1)S(1)}, bf16[64,2048]{1,0:T(8,128)(2,1)S(1)}, u32[]{:S(2)}, u32[]{:S(2)}) %collective-permute-start.74) | collective-permute-done | bytes 262176 | tf_op jit(solution)/shard_map/ppermute | solution.py:378
  (516 shorter events, 375.4 us)
Async XLA Ops:
  7.2 102.6 %all-gather.4.cloned.1.call-start = ((), (), s32[]{:S(2)}) async-start(), calls=%async_computation.9 | async-start | bytes 2949120 | tf_op jit(solution)/shard_map/all_gather | solution.py:748
  11.4 27.4 %all-to-all-start = ((bf16[4,64,1536]{2,1,0:T(8,128)(2,1)}), bf16[4,64,1536]{2,1,0:T(8,128)(2,1)S(1)}, u32[]{:S(2)}, u32[]{:S(2)}) async-start(bf16[4,64,1536]{2,1,0:T(8,128)(2,1)} %pad_maximum_fusion.3), calls=%async_computation | async-start | bytes 1572864 | tf_op jit(solution)/shard_map/all_to_all | solution.py:447
  23.8 47.1 %collective-permute-start.4 = (bf16[256,2048]{1,0:T(8,128)(2,1)S(1)}, bf16[256,2048]{1,0:T(8,128)(2,1)}, u32[]{:S(2)}, u32[]{:S(2)}) collective-permute-start(bf16[256,2048]{1,0:T(8,128)(2,1)S(1)} %copy-done.13), channel_id=1, source_target_pairs={{0,1},{1,2},{2,3},{3,0},{4,5},{5,6},{6,7},{7,4},{8,9},{9,10},{10,1... | collective-permute-start | bytes 3145736 | tf_op jit(solution)/shard_map/ppermute | solution.py:378
  38.8 33.3 %collective-permute-start.5 = (bf16[128,2048]{1,0:T(8,128)(2,1)S(1)}, bf16[128,2048]{1,0:T(8,128)(2,1)S(1)}, u32[]{:S(2)}, u32[]{:S(2)}) collective-permute-start(bf16[128,2048]{1,0:T(8,128)(2,1)S(1)} %get-tuple-element.233.refs_1_), channel_id=1, source_target_pairs={{0,8},{8,0},{1,9},{9,1},{2,10},{10,2},{3,11},{11,3},{4,12},{12,4},... | collective-permute-start | bytes 1572872 | tf_op jit(solution)/shard_map/ppermute | solution.py:198
  40.2 46.7 %collective-permute-start.2 = (bf16[256,1536]{1,0:T(8,128)(2,1)S(1)}, bf16[256,1536]{1,0:T(8,128)(2,1)}, u32[]{:S(2)}, u32[]{:S(2)}) collective-permute-start(bf16[256,1536]{1,0:T(8,128)(2,1)S(1)} %bitcast.188), channel_id=1, source_target_pairs={{0,1},{1,2},{2,3},{3,0},{4,5},{5,6},{6,7},{7,4},{8,9},{9,10},{10,1... | collective-permute-start | bytes 2359304 | tf_op jit(solution)/shard_map/ppermute | solution.py:378
  41.9 45.0 %collective-permute-start.3 = (bf16[256,1536]{1,0:T(8,128)(2,1)S(1)}, bf16[256,1536]{1,0:T(8,128)(2,1)S(1)}, u32[]{:S(2)}, u32[]{:S(2)}) collective-permute-start(bf16[256,1536]{1,0:T(8,128)(2,1)S(1)} %bitcast.189), channel_id=1, source_target_pairs={{0,4},{4,0},{1,5},{5,1},{2,6},{6,2},{3,7},{7,3},{8,12},{12,8},{9,1... | collective-permute-start | bytes 2359304 | tf_op jit(solution)/shard_map/ppermute | solution.py:198
  41.9 32.0 %collective-permute-start.6 = (bf16[128,2048]{1,0:T(8,128)(2,1)S(1)}, bf16[128,2048]{1,0:T(8,128)(2,1)S(1)}, u32[]{:S(2)}, u32[]{:S(2)}) collective-permute-start(bf16[128,2048]{1,0:T(8,128)(2,1)S(1)} %get-tuple-element.232.refs_0_), channel_id=1, source_target_pairs={{0,16},{16,0},{1,17},{17,1},{2,18},{18,2},{3,19},{19,3},{4,20},{20... | collective-permute-start | bytes 1572872 | tf_op jit(solution)/shard_map/ppermute | solution.py:198
  94.3 179.0 %all-gather.6.cloned.1.call-start = ((), (), s32[]{:S(2)}) async-start(), calls=%async_computation.10 | async-start | bytes 9437184 | tf_op jit(solution)/shard_map/all_gather | solution.py:748
  109.9 31.5 %collective-permute-start.11 = (bf16[256,1536]{1,0:T(8,128)(2,1)}, bf16[256,1536]{1,0:T(8,128)(2,1)}, u32[]{:S(2)}, u32[]{:S(2)}) collective-permute-start(bf16[256,1536]{1,0:T(8,128)(2,1)} %collective-permute-done.9.refs_2_), channel_id=1, source_target_pairs={{0,1},{1,2},{2,3},{3,0},{4,5},{5,6},{6,7},{7,4},{8,9},{9,10},{10,1... | collective-permute-start | bytes 2359304 | tf_op jit(solution)/shard_map/ppermute | solution.py:378
  110.0 31.5 %collective-permute-start.12 = (bf16[256,1536]{1,0:T(8,128)(2,1)}, bf16[256,1536]{1,0:T(8,128)(2,1)}, u32[]{:S(2)}, u32[]{:S(2)}) collective-permute-start(bf16[256,1536]{1,0:T(8,128)(2,1)} %collective-permute-done.9.refs_2_), channel_id=1, source_target_pairs={{0,4},{4,0},{1,5},{5,1},{2,6},{6,2},{3,7},{7,3},{8,12},{12,8},{9,1... | collective-permute-start | bytes 2359304 | tf_op jit(solution)/shard_map/ppermute | solution.py:198
  116.6 186.0 %all-gather.8.cloned.1.call-start = ((), (), s32[]{:S(2)}) async-start(), calls=%async_computation.11 | async-start | bytes 9437184 | tf_op jit(solution)/shard_map/all_gather | solution.py:748
  141.4 419.6 %reduce-scatter.4.cloned.1.call-start = ((), (), s32[]{:S(2)}) async-start(), calls=%async_computation.12 | async-start | bytes 5242880 | tf_op jit(solution)/shard_map/reduce_scatter | solution.py:840
  185.7 25.0 %collective-permute-start.20 = (bf16[512,1024]{1,0:T(8,128)(2,1)S(1)}, bf16[512,1024]{1,0:T(8,128)(2,1)S(1)}, u32[]{:S(2)}, u32[]{:S(2)}) collective-permute-start(bf16[512,1024]{1,0:T(8,128)(2,1)S(1)} %convolution_convert_fusion.14), channel_id=1, source_target_pairs={{0,8},{8,0},{1,9},{9,1},{2,10},{10,2},{3,11},{11,3},{4,12},{12,4},... | collective-permute-start | bytes 3145736 | tf_op jit(solution)/shard_map/ppermute | solution.py:198
  234.9 25.6 %collective-permute-start.24 = (bf16[128,2048]{1,0:T(8,128)(2,1)S(1)}, bf16[128,2048]{1,0:T(8,128)(2,1)}, u32[]{:S(2)}, u32[]{:S(2)}) collective-permute-start(bf16[128,2048]{1,0:T(8,128)(2,1)S(1)} %get-tuple-element.457.refs_0_), channel_id=1, source_target_pairs={{0,16},{16,0},{1,17},{17,1},{2,18},{18,2},{3,19},{19,3},{4,20},{20... | collective-permute-start | bytes 1572872 | tf_op jit(solution)/shard_map/ppermute | solution.py:198
  249.2 80.5 %collective-permute-start.30 = (bf16[256,2048]{1,0:T(8,128)(2,1)S(1)}, bf16[256,2048]{1,0:T(8,128)(2,1)}, u32[]{:S(2)}, u32[]{:S(2)}) collective-permute-start(bf16[256,2048]{1,0:T(8,128)(2,1)S(1)} %copy-done.13), channel_id=1, source_target_pairs={{0,4},{4,0},{1,5},{5,1},{2,6},{6,2},{3,7},{7,3},{8,12},{12,8},{9,1... | collective-permute-start | bytes 3145736 | tf_op jit(solution)/shard_map/ppermute | solution.py:198
  258.5 44.1 %collective-permute-start.28 = (bf16[256,2048]{1,0:T(8,128)(2,1)}, bf16[256,2048]{1,0:T(8,128)(2,1)}, u32[]{:S(2)}, u32[]{:S(2)}) collective-permute-start(bf16[256,2048]{1,0:T(8,128)(2,1)} %collective-permute-done.4.refs_1_), channel_id=1, source_target_pairs={{0,1},{1,2},{2,3},{3,0},{4,5},{5,6},{6,7},{7,4},{8,9},{9,10},{10,1... | collective-permute-start | bytes 3145736 | tf_op jit(solution)/shard_map/ppermute | solution.py:378
  260.5 69.2 %collective-permute-start.31 = (bf16[256,2048]{1,0:T(8,128)(2,1)}, bf16[256,2048]{1,0:T(8,128)(2,1)}, u32[]{:S(2)}, u32[]{:S(2)}) collective-permute-start(bf16[256,2048]{1,0:T(8,128)(2,1)} %collective-permute-done.4.refs_1_), channel_id=1, source_target_pairs={{0,4},{4,0},{1,5},{5,1},{2,6},{6,2},{3,7},{7,3},{8,12},{12,8},{9,1... | collective-permute-start | bytes 3145736 | tf_op jit(solution)/shard_map/ppermute | solution.py:198
  302.6 27.1 %collective-permute-start.32 = (bf16[256,2048]{1,0:T(8,128)(2,1)}, bf16[256,2048]{1,0:T(8,128)(2,1)}, u32[]{:S(2)}, u32[]{:S(2)}) collective-permute-start(bf16[256,2048]{1,0:T(8,128)(2,1)} %collective-permute-done.28.refs_2_), channel_id=1, source_target_pairs={{0,4},{4,0},{1,5},{5,1},{2,6},{6,2},{3,7},{7,3},{8,12},{12,8},{9,1... | collective-permute-start | bytes 3145736 | tf_op jit(solution)/shard_map/ppermute | solution.py:198
  338.4 25.6 %collective-permute-start.34 = (bf16[512,1024]{1,0:T(8,128)(2,1)S(1)}, bf16[512,1024]{1,0:T(8,128)(2,1)S(1)}, u32[]{:S(2)}, u32[]{:S(2)}) collective-permute-start(bf16[512,1024]{1,0:T(8,128)(2,1)S(1)} %fusion.54), channel_id=1, source_target_pairs={{0,16},{16,0},{1,17},{17,1},{2,18},{18,2},{3,19},{19,3},{4,20},{20... | collective-permute-start | bytes 3145736 | tf_op jit(solution)/shard_map/ppermute | solution.py:198
  340.1 25.3 %collective-permute-start.35 = (bf16[512,1024]{1,0:T(8,128)(2,1)S(1)}, bf16[512,1024]{1,0:T(8,128)(2,1)S(1)}, u32[]{:S(2)}, u32[]{:S(2)}) collective-permute-start(bf16[512,1024]{1,0:T(8,128)(2,1)S(1)} %fusion.59), channel_id=1, source_target_pairs={{0,8},{8,0},{1,9},{9,1},{2,10},{10,2},{3,11},{11,3},{4,12},{12,4},... | collective-permute-start | bytes 3145736 | tf_op jit(solution)/shard_map/ppermute | solution.py:198
  444.7 153.3 %reduce-scatter.6.cloned.1.call-start = ((), (), s32[]{:S(2)}) async-start(), calls=%async_computation.13 | async-start | bytes 5242880 | tf_op jit(solution)/shard_map/reduce_scatter | solution.py:870
  471.5 41.7 %collective-permute-start.46 = (bf16[1024,2048]{1,0:T(8,128)(2,1)}, bf16[1024,2048]{1,0:T(8,128)(2,1)}, u32[]{:S(2)}, u32[]{:S(2)}) collective-permute-start(bf16[1024,2048]{1,0:T(8,128)(2,1)} %convolution_convert_fusion.5), channel_id=1, source_target_pairs={{0,4},{4,0},{1,5},{5,1},{2,6},{6,2},{3,7},{7,3},{8,12},{12,8},{9,1... | collective-permute-start | bytes 12582920 | tf_op jit(solution)/shard_map/ppermute | solution.py:198
  494.0 27.0 %collective-permute-start.47 = (bf16[512,1024]{1,0:T(8,128)(2,1)}, bf16[512,1024]{1,0:T(8,128)(2,1)}, u32[]{:S(2)}, u32[]{:S(2)}) collective-permute-start(bf16[512,1024]{1,0:T(8,128)(2,1)} %get-tuple-element.303), channel_id=1, source_target_pairs={{0,16},{16,0},{1,17},{17,1},{2,18},{18,2},{3,19},{19,3},{4,20},{20... | collective-permute-start | bytes 3145736 | tf_op jit(solution)/shard_map/ppermute | solution.py:198
  494.6 26.4 %collective-permute-start.48 = (bf16[512,1024]{1,0:T(8,128)(2,1)S(1)}, bf16[512,1024]{1,0:T(8,128)(2,1)}, u32[]{:S(2)}, u32[]{:S(2)}) collective-permute-start(bf16[512,1024]{1,0:T(8,128)(2,1)S(1)} %get-tuple-element.304), channel_id=1, source_target_pairs={{0,8},{8,0},{1,9},{9,1},{2,10},{10,2},{3,11},{11,3},{4,12},{12,4},... | collective-permute-start | bytes 3145736 | tf_op jit(solution)/shard_map/ppermute | solution.py:198
  521.0 37.1 %collective-permute-start.51 = (bf16[1024,2048]{1,0:T(8,128)(2,1)}, bf16[1024,2048]{1,0:T(8,128)(2,1)}, u32[]{:S(2)}, u32[]{:S(2)}) collective-permute-start(bf16[1024,2048]{1,0:T(8,128)(2,1)} %convolution_convert_fusion.4), channel_id=1, source_target_pairs={{0,4},{4,0},{1,5},{5,1},{2,6},{6,2},{3,7},{7,3},{8,12},{12,8},{9,1... | collective-permute-start | bytes 12582920 | tf_op jit(solution)/shard_map/ppermute | solution.py:198
  598.0 27.3 %all-to-all-start.3 = ((bf16[4,64,2048]{2,1,0:T(8,128)(2,1)}), bf16[4,64,2048]{2,1,0:T(8,128)(2,1)S(1)}, u32[]{:S(2)}, u32[]{:S(2)}) async-start(bf16[4,64,2048]{2,1,0:T(8,128)(2,1)} %bitcast.216), calls=%async_computation.5 | async-start | bytes 2097152 | tf_op jit(solution)/shard_map/all_to_all | solution.py:450
  601.7 112.0 %reduce-scatter.8.cloned.1.call-start = ((), (), s32[]{:S(2)}) async-start(), calls=%async_computation.14 | async-start | bytes 5242880 | tf_op jit(solution)/shard_map/reduce_scatter | solution.py:883
  677.1 32.3 %collective-permute-start.68 = (bf16[512,1024]{1,0:T(8,128)(2,1)}, bf16[512,1024]{1,0:T(8,128)(2,1)}, u32[]{:S(2)}, u32[]{:S(2)}) collective-permute-start(bf16[512,1024]{1,0:T(8,128)(2,1)} %fusion.38), channel_id=1, source_target_pairs={{0,16},{16,0},{1,17},{17,1},{2,18},{18,2},{3,19},{19,3},{4,20},{20... | collective-permute-start | bytes 3145736 | tf_op jit(solution)/shard_map/ppermute | solution.py:198
  678.6 30.8 %collective-permute-start.69 = (bf16[512,1024]{1,0:T(8,128)(2,1)}, bf16[512,1024]{1,0:T(8,128)(2,1)}, u32[]{:S(2)}, u32[]{:S(2)}) collective-permute-start(bf16[512,1024]{1,0:T(8,128)(2,1)} %fusion.43), channel_id=1, source_target_pairs={{0,8},{8,0},{1,9},{9,1},{2,10},{10,2},{3,11},{11,3},{4,12},{12,4},... | collective-permute-start | bytes 3145736 | tf_op jit(solution)/shard_map/ppermute | solution.py:198
  682.2 27.1 %collective-permute-start.65 = (bf16[256,1536]{1,0:T(8,128)(2,1)}, bf16[256,1536]{1,0:T(8,128)(2,1)}, u32[]{:S(2)}, u32[]{:S(2)}) collective-permute-start(bf16[256,1536]{1,0:T(8,128)(2,1)} %add_convert_fusion.6), channel_id=1, source_target_pairs={{0,1},{1,2},{2,3},{3,0},{4,5},{5,6},{6,7},{7,4},{8,9},{9,10},{10,1... | collective-permute-start | bytes 2359304 | tf_op jit(solution)/shard_map/ppermute | solution.py:378
  713.7 25.7 %collective-permute-start.70 = (bf16[256,1536]{1,0:T(8,128)(2,1)}, bf16[256,1536]{1,0:T(8,128)(2,1)}, u32[]{:S(2)}, u32[]{:S(2)}) collective-permute-start(bf16[256,1536]{1,0:T(8,128)(2,1)} %add_convert_fusion.5), channel_id=1, source_target_pairs={{0,1},{1,2},{2,3},{3,0},{4,5},{5,6},{6,7},{7,4},{8,9},{9,10},{10,1... | collective-permute-start | bytes 2359304 | tf_op jit(solution)/shard_map/ppermute | solution.py:378
  713.7 25.7 %all-to-all-start.4 = ((bf16[4,64,2048]{2,1,0:T(8,128)(2,1)}), bf16[4,64,2048]{2,1,0:T(8,128)(2,1)S(1)}, u32[]{:S(2)}, u32[]{:S(2)}) async-start(bf16[4,64,2048]{2,1,0:T(8,128)(2,1)} %bitcast.215), calls=%async_computation.7 | async-start | bytes 2097152 | tf_op jit(solution)/shard_map/all_to_all | solution.py:450
  (138 other events, 1478.9 us)
Sparse Core Ops, SparseCore 0:
  11.5 55.5 all-gather.3
  110.0 90.5 all-gather.5
  202.2 93.6 all-gather.7
  444.8 73.5 reduce-scatter.3
  521.2 76.8 reduce-scatter.5
  604.5 77.7 reduce-scatter.7
